TPU v7x, 32 devices: a whole 2x2x4 slice. The times are simulated.
32 devices in a mesh: pipe: 4 (over y, core), dp: 4 (over z), tensor: 2 (over x).
Axes of the slice: x: 2, y: 2, z: 4, core: 2. Of those that a mesh axis runs over, the one named last changes fastest.
Arguments:
- output_gradient: bfloat16 [16, 128, 8192], P('dp', None, 'tensor'), may hold values from -6 to 6
- acts: bfloat16 [16, 4, 128, 8192], P('dp', 'pipe', None, 'tensor'), may hold values from -6 to 6
- weights: bfloat16 [4, 8192, 8192], P('pipe', 'tensor'), may hold values from -0.0625 to 0.0625
- adapter_down_factors: bfloat16 [4, 8192, 128], P('pipe', 'tensor'), may hold values from -0.0625 to 0.0625
- adapter_up_factors: bfloat16 [4, 128, 8192], P('pipe'), may hold values from -0.0625 to 0.0625
- feature_sign_bits: int32 [8192, 64], replicated, may hold values from 0 to 1
- rank_sign_bits: int32 [128, 128], replicated, may hold values from 0 to 1
- lengths: int32 [16], P('dp'), may hold values from 32 to 128, as said below
Outputs:
- features: float32 [16, 4, 8192], P('dp', 'pipe', 'tensor')
Inputs may be any that keep to these rules, and one draw needn't show every extreme that they name: `lengths`: the first example has exactly 128 real tokens.
All inputs are finite; a program needn't handle non-finite values.
Results may differ from a plain program's by a relative error of at most 0.0065.
Values may be sent and summed in bfloat16 or wider, within the bound.
No kernel may reach another device: no remote copies, remote signals or barrier semaphores. Data moves between devices by JAX's collectives and lax.ppermute only.
A program may use at most 192 MiB of HBM per device.

v0:
```python
import math

import jax
import jax.numpy as jnp
from jax import lax
from jax.sharding import PartitionSpec as P

ADAPTER_SCALE = 2.0


def from_behind(value, axis, steps):
    count = lax.axis_size(axis)
    leading, last = (max(0, -steps), min(count, count - steps))
    return lax.ppermute(value, axis, [(source, source + steps) for source in range(leading, last)])


def times_t(left, right):
    return lax.dot_general(
        left, right, (((1,), (1,)), ((), ())), preferred_element_type=jnp.float32
    )


def features_of(xp, xb, uq, yp, keep, seq):
    xp = xp * keep[:, None]
    xb = xb * keep[:, None]
    left = jnp.dot(xp.T, uq, precision=lax.Precision.HIGHEST, preferred_element_type=jnp.float32)
    right = jnp.dot(
        xb.T,
        yp.astype(jnp.float32),
        precision=lax.Precision.HIGHEST,
        preferred_element_type=jnp.float32,
    )
    return jnp.concatenate([left.reshape(-1), right.reshape(-1)]) * (ADAPTER_SCALE / math.sqrt(seq))


def per_device(
    output_gradient,
    acts,
    weights,
    adapter_down_factors,
    adapter_up_factors,
    feature_sign_bits,
    rank_sign_bits,
    lengths,
):
    sections = lax.axis_size("pipe")
    section_index = lax.axis_index("pipe")
    parts = lax.axis_size("tensor")
    part = lax.axis_index("tensor")
    count, seq, local_in = output_gradient.shape
    width = local_in * parts
    rank_position = adapter_up_factors.shape[1]
    proj = feature_sign_bits.shape[1]
    feat_local = 2 * proj * proj // parts
    w_local = weights[0]
    down_factor_local = adapter_down_factors[0]
    up_factor_whole = adapter_up_factors[0]
    wide = (2 * feature_sign_bits - 1).astype(jnp.bfloat16)
    wide_rows = lax.dynamic_slice_in_dim(wide, part * local_in, local_in, 0)
    low = (2 * rank_sign_bits - 1).astype(jnp.float32)
    low_left = low[:, :proj].astype(jnp.bfloat16)
    low_right = low[:, proj:]
    inv_d = 1.0 / math.sqrt(width)
    inv_r = 1.0 / math.sqrt(rank_position)
    positions = jnp.arange(seq)
    is_last = section_index == sections - 1
    saved = acts[:, 0]
    feats = jnp.zeros((count, 1, feat_local), jnp.float32)
    total_steps = count + sections - 1
    b_cols = lax.dynamic_slice_in_dim(up_factor_whole, part * local_in, local_in, 1)
    incoming = jnp.zeros((seq, local_in), jnp.bfloat16)
    for step in range(total_steps):
        micro = step - (sections - 1 - section_index)
        active = (micro >= 0) & (micro < count)
        slot = jnp.clip(micro, 0, count - 1)
        given = lax.dynamic_index_in_dim(output_gradient, slot, 0, False)
        dy_cols = jnp.where(is_last, given, incoming)
        current_input = lax.dynamic_index_in_dim(saved, slot, 0, False)
        keep = (positions < lengths[slot]).astype(jnp.float32)
        u_part = times_t(dy_cols, b_cols)
        yp_part = jnp.dot(dy_cols, wide_rows, preferred_element_type=jnp.float32) * inv_d
        xp_part = jnp.dot(current_input, wide_rows, preferred_element_type=jnp.float32) * inv_d
        xa_part = jnp.dot(current_input, down_factor_local, preferred_element_type=jnp.float32)
        u_sum, yp_sum, xp_all, xa_all = lax.psum((u_part, yp_part, xp_part, xa_part), "tensor")
        u_all = u_sum.astype(jnp.bfloat16)
        yp_all = yp_sum.astype(jnp.bfloat16)
        empty = jnp.zeros((seq, local_in), jnp.float32)
        total = empty
        piece = lax.all_gather(dy_cols, "tensor", axis=1, tiled=True)
        frozen_weight = lax.cond(active, lambda: times_t(piece, w_local), lambda: total)
        u_proj = jnp.dot(u_all, low_left, preferred_element_type=jnp.float32) * inv_r
        x_low = (
            jnp.dot(
                xa_all,
                low_right,
                precision=lax.Precision.HIGHEST,
                preferred_element_type=jnp.float32,
            )
            * inv_r
        )
        full = features_of(xp_all, x_low, u_proj, yp_all, keep, seq)
        mine = lax.dynamic_slice_in_dim(full, part * feat_local, feat_local, 0)
        updated = lax.dynamic_update_index_in_dim(feats, mine[None, :], slot, 0)
        feats = jnp.where(active, updated, feats)
        if step + 1 < total_steps:
            dx_cols = (frozen_weight + ADAPTER_SCALE * times_t(u_all, down_factor_local)).astype(
                jnp.bfloat16
            )
            incoming = from_behind(dx_cols, "pipe", -1)
    return feats


def solution(mesh):
    placed = (
        P("dp", None, "tensor"),
        P("dp", "pipe", None, "tensor"),
        P("pipe", "tensor", None),
        P("pipe", "tensor", None),
        P("pipe", None, None),
        P(),
        P(),
        P("dp"),
    )
    return jax.shard_map(
        per_device, mesh=mesh, in_specs=placed, out_specs=P("dp", "pipe", "tensor"), check_vma=False
    )
```

profile of v0, /device:TPU:12, one launch (start us, length us, event | category | flops | bytes accessed | tf_op | source)
XLA Modules:
  0.0 541.1 jit_solution(8179145949261616446)
XLA Ops:
  6.5 2.4 dynamic-slice_select_fusion
  9.0 1.7 fusion.48
  10.7 8.9 %psum.197 = bf16[128,128]{1,0:T(8,128)(2,1)S(1)} all-reduce(f32[128,128]{1,0:T(8,128)S(1)} %fusion.48), channel_id=1, replica_groups=mesh['pipe'=4,'dp'=4,'tensor'=2] {'tensor'}, use_global_device_ids=true, to_apply=%region_1.2 | all-reduce | flops 16384 | bytes 98304 | tf_op jit(solution)/shard_map/psum | solution.py:84
  19.6 23.8 %all-gather.18.cloned.1.call-done = bf16[1,128,8192]{2,1,0:T(8,128)(2,1)} async-done(((bf16[1,128,4096]{2,1,0:T(8,128)(2,1)}), bf16[1,128,8192]{2,1,0:T(8,128)(2,1)}) %all-gather.18.cloned.1.call-update) | async-done | bytes 2097168 | tf_op jit(solution)/shard_map/all_gather | solution.py:89
  43.4 1.6 conditional.6
  44.9 3.0 fusion.1
  48.0 1.9 collective-permute-start
  49.9 29.7 %collective-permute-done = bf16[128,4096]{1,0:T(8,128)(2,1)} collective-permute-done((bf16[128,4096]{1,0:T(8,128)(2,1)}, bf16[128,4096]{1,0:T(8,128)(2,1)}, u32[]{:S(2)}, u32[]{:S(2)}) %collective-permute-start) | collective-permute-done | bytes 1048608 | tf_op jit(solution)/shard_map/ppermute | solution.py:14
  79.6 2.6 bitcast_select_fusion.5
  82.3 1.7 fusion.46
  83.9 8.0 %psum.201 = bf16[128,128]{1,0:T(8,128)(2,1)S(1)} all-reduce(f32[128,128]{1,0:T(8,128)S(1)} %fusion.46), channel_id=1, replica_groups=mesh['pipe'=4,'dp'=4,'tensor'=2] {'tensor'}, use_global_device_ids=true, to_apply=%region_7.8 | all-reduce | flops 16384 | bytes 98304 | tf_op jit(solution)/shard_map/psum | solution.py:84
  91.9 1.8 convolution_multiply_fusion.4
  93.7 21.8 %all-gather.8.cloned.1.call-done = bf16[128,8192]{1,0:T(8,128)(2,1)} async-done(((bf16[128,4096]{1,0:T(8,128)(2,1)}), bf16[128,8192]{1,0:T(8,128)(2,1)}) %all-gather.8.cloned.1.call-update) | async-done | bytes 2097168 | tf_op jit(solution)/shard_map/all_gather | solution.py:89
  115.5 29.5 %conditional.7 = (f32[128,4096]{1,0:T(8,128)}) conditional(s32[]{:T(128)} %convert_element_type.152, () %tuple.43, (bf16[128,8192]{1,0:T(8,128)(2,1)}, bf16[4096,8192]{1,0:T(8,128)(2,1)}) %tuple.44), branch_computations={%region_11.12_spmd, %region_12.13_spmd} | conditional | flops 8589934592 | bytes 71303176 | solution.py:90
  115.5 29.5 %fusion.182 = f32[128,4096]{1,0:T(8,128)} fusion(bf16[128,8192]{1,0:T(8,128)(2,1)} %get-tuple-element.44, bf16[4096,8192]{1,0:T(8,128)(2,1)} %get-tuple-element.48), kind=kOutput, calls=%fused_computation.266 | convolution fusion | flops 8589934592 | bytes 71303168 | tf_op jit(solution)/shard_map/cond/branch_1_fun/dot_general | solution.py:18
  145.0 3.4 add_convert_fusion.4
  148.4 1.9 collective-permute-start.1
  150.4 12.6 %collective-permute-done.1 = bf16[128,4096]{1,0:T(8,128)(2,1)} collective-permute-done((bf16[128,4096]{1,0:T(8,128)(2,1)}, bf16[128,4096]{1,0:T(8,128)(2,1)}, u32[]{:S(2)}, u32[]{:S(2)}) %collective-permute-start.1) | collective-permute-done | bytes 1048608 | tf_op jit(solution)/shard_map/ppermute | solution.py:14
  163.0 2.7 bitcast_select_fusion.4
  165.7 1.7 fusion.44
  167.4 7.9 %psum.205 = bf16[128,128]{1,0:T(8,128)(2,1)S(1)} all-reduce(f32[128,128]{1,0:T(8,128)S(1)} %fusion.44), channel_id=1, replica_groups=mesh['pipe'=4,'dp'=4,'tensor'=2] {'tensor'}, use_global_device_ids=true, to_apply=%region_13.14 | all-reduce | flops 16384 | bytes 98304 | tf_op jit(solution)/shard_map/psum | solution.py:84
  175.3 1.8 convolution_multiply_fusion.3
  177.1 22.3 %all-gather.10.cloned.1.call-done = bf16[128,8192]{1,0:T(8,128)(2,1)} async-done(((bf16[128,4096]{1,0:T(8,128)(2,1)}), bf16[128,8192]{1,0:T(8,128)(2,1)}) %all-gather.10.cloned.1.call-update) | async-done | bytes 2097168 | tf_op jit(solution)/shard_map/all_gather | solution.py:89
  199.4 29.5 %conditional.8 = (f32[128,4096]{1,0:T(8,128)}) conditional(s32[]{:T(128)} %convert_element_type.157, () %tuple.45, (bf16[128,8192]{1,0:T(8,128)(2,1)}, bf16[4096,8192]{1,0:T(8,128)(2,1)}) %tuple.46), branch_computations={%region_17.18_spmd, %region_18.19_spmd} | conditional | flops 8589934592 | bytes 71303176 | solution.py:90
  199.4 29.5 %fusion.183 = f32[128,4096]{1,0:T(8,128)} fusion(bf16[128,8192]{1,0:T(8,128)(2,1)} %get-tuple-element.50, bf16[4096,8192]{1,0:T(8,128)(2,1)} %get-tuple-element.52), kind=kOutput, calls=%fused_computation.267 | convolution fusion | flops 8589934592 | bytes 71303168 | tf_op jit(solution)/shard_map/cond/branch_1_fun/dot_general | solution.py:18
  228.9 3.4 add_convert_fusion.3
  232.3 1.9 collective-permute-start.2
  234.3 12.6 %collective-permute-done.2 = bf16[128,4096]{1,0:T(8,128)(2,1)} collective-permute-done((bf16[128,4096]{1,0:T(8,128)(2,1)}, bf16[128,4096]{1,0:T(8,128)(2,1)}, u32[]{:S(2)}, u32[]{:S(2)}) %collective-permute-start.2) | collective-permute-done | bytes 1048608 | tf_op jit(solution)/shard_map/ppermute | solution.py:14
  246.9 2.6 bitcast_select_fusion.3
  249.8 2.4 fusion.34
  252.2 2.3 fusion.19
  268.9 2.2 fusion.3
  271.0 1.7 fusion.42
  272.7 9.3 %psum.209 = bf16[128,128]{1,0:T(8,128)(2,1)S(1)} all-reduce(f32[128,128]{1,0:T(8,128)S(1)} %fusion.42), channel_id=1, replica_groups=mesh['pipe'=4,'dp'=4,'tensor'=2] {'tensor'}, use_global_device_ids=true, to_apply=%region_19.20 | all-reduce | flops 16384 | bytes 98304 | tf_op jit(solution)/shard_map/psum | solution.py:84
  282.0 1.8 convolution_multiply_fusion.2
  284.7 29.6 %conditional.9 = (f32[128,4096]{1,0:T(8,128)}) conditional(s32[]{:T(128)} %convert_element_type.162, () %tuple.47, (bf16[128,8192]{1,0:T(8,128)(2,1)}, bf16[4096,8192]{1,0:T(8,128)(2,1)}) %tuple.48), branch_computations={%region_23.24_spmd, %region_24.25_spmd} | conditional | flops 8589934592 | bytes 71303176 | solution.py:90
  284.7 29.6 %fusion.184 = f32[128,4096]{1,0:T(8,128)} fusion(bf16[128,8192]{1,0:T(8,128)(2,1)} %get-tuple-element.53, bf16[4096,8192]{1,0:T(8,128)(2,1)} %get-tuple-element.54), kind=kOutput, calls=%fused_computation.268 | convolution fusion | flops 8589934592 | bytes 71303168 | tf_op jit(solution)/shard_map/cond/branch_1_fun/dot_general | solution.py:18
  314.3 2.6 add_convert_fusion.2
  316.9 2.1 collective-permute-start.3
  324.1 7.2 %collective-permute-done.3 = bf16[128,4096]{1,0:T(8,128)(2,1)S(1)} collective-permute-done((bf16[128,4096]{1,0:T(8,128)(2,1)S(1)}, bf16[128,4096]{1,0:T(8,128)(2,1)S(1)}, u32[]{:S(2)}, u32[]{:S(2)}) %collective-permute-start.3) | collective-permute-done | bytes 1048608 | tf_op jit(solution)/shard_map/ppermute | solution.py:14
  331.3 2.3 bitcast_select_fusion.2
  334.9 2.6 convolution_multiply_fusion.25
  337.5 2.4 convolution_multiply_fusion.21
  339.9 2.3 convolution_multiply_fusion.17
  345.4 1.7 fusion.40
  347.1 9.9 %psum.213 = bf16[128,128]{1,0:T(8,128)(2,1)S(1)} all-reduce(f32[128,128]{1,0:T(8,128)S(1)} %fusion.40), channel_id=1, replica_groups=mesh['pipe'=4,'dp'=4,'tensor'=2] {'tensor'}, use_global_device_ids=true, to_apply=%region_25.26 | all-reduce | flops 16384 | bytes 98304 | tf_op jit(solution)/shard_map/psum | solution.py:84
  357.0 1.8 convolution_multiply_fusion.1
  358.8 10.3 %all-gather.14.cloned.1.call-done = bf16[128,8192]{1,0:T(8,128)(2,1)} async-done(((bf16[128,4096]{1,0:T(8,128)(2,1)}), bf16[128,8192]{1,0:T(8,128)(2,1)}) %all-gather.14.cloned.1.call-update) | async-done | bytes 2097168 | tf_op jit(solution)/shard_map/all_gather | solution.py:89
  369.1 29.5 %conditional.10 = (f32[128,4096]{1,0:T(8,128)}) conditional(s32[]{:T(128)} %convert_element_type.167, () %tuple.49, (bf16[128,8192]{1,0:T(8,128)(2,1)}, bf16[4096,8192]{1,0:T(8,128)(2,1)}) %tuple.50), branch_computations={%region_29.30_spmd, %region_30.31_spmd} | conditional | flops 8589934592 | bytes 71303176 | solution.py:90
  369.1 29.5 %fusion.185 = f32[128,4096]{1,0:T(8,128)} fusion(bf16[128,8192]{1,0:T(8,128)(2,1)} %get-tuple-element.55, bf16[4096,8192]{1,0:T(8,128)(2,1)} %get-tuple-element.56), kind=kOutput, calls=%fused_computation.269 | convolution fusion | flops 8589934592 | bytes 71303168 | tf_op jit(solution)/shard_map/cond/branch_1_fun/dot_general | solution.py:18
  398.6 2.5 add_convert_fusion.1
  401.1 2.0 collective-permute-start.4
  407.0 8.4 %collective-permute-done.4 = bf16[128,4096]{1,0:T(8,128)(2,1)S(1)} collective-permute-done((bf16[128,4096]{1,0:T(8,128)(2,1)S(1)}, bf16[128,4096]{1,0:T(8,128)(2,1)S(1)}, u32[]{:S(2)}, u32[]{:S(2)}) %collective-permute-start.4) | collective-permute-done | bytes 1048608 | tf_op jit(solution)/shard_map/ppermute | solution.py:14
  415.4 2.3 bitcast_select_fusion.1
  419.1 2.4 convolution_multiply_fusion.26
  426.2 9.8 %psum.217 = bf16[128,128]{1,0:T(8,128)(2,1)S(1)} all-reduce(f32[128,128]{1,0:T(8,128)} %fusion.38), channel_id=1, replica_groups=mesh['pipe'=4,'dp'=4,'tensor'=2] {'tensor'}, use_global_device_ids=true, to_apply=%region_31.32 | all-reduce | flops 16384 | bytes 98304 | tf_op jit(solution)/shard_map/psum | solution.py:84
  436.1 1.8 convolution_multiply_fusion
  437.8 14.3 %all-gather.16.cloned.1.call-done = bf16[128,8192]{1,0:T(8,128)(2,1)} async-done(((bf16[128,4096]{1,0:T(8,128)(2,1)}), bf16[128,8192]{1,0:T(8,128)(2,1)}) %all-gather.16.cloned.1.call-update) | async-done | bytes 2097168 | tf_op jit(solution)/shard_map/all_gather | solution.py:89
  452.1 1.6 conditional.11
  452.1 1.6 broadcast.103
  453.7 2.6 add_convert_fusion
  456.3 30.0 %collective-permute-start.5 = (bf16[128,4096]{1,0:T(8,128)(2,1)S(1)}, bf16[128,4096]{1,0:T(8,128)(2,1)S(1)}, u32[]{:S(2)}, u32[]{:S(2)}) collective-permute-start(bf16[128,4096]{1,0:T(8,128)(2,1)S(1)} %add_convert_fusion), channel_id=1, source_target_pairs={{8,0},{16,8},{24,16},{9,1},{17,9},{25,17},{10,2},{18,10},{26,18},{... | collective-permute-start | bytes 3145736 | tf_op jit(solution)/shard_map/ppermute | solution.py:14
  488.9 9.7 %collective-permute-done.5 = bf16[128,4096]{1,0:T(8,128)(2,1)S(1)} collective-permute-done((bf16[128,4096]{1,0:T(8,128)(2,1)S(1)}, bf16[128,4096]{1,0:T(8,128)(2,1)S(1)}, u32[]{:S(2)}, u32[]{:S(2)}) %collective-permute-start.5) | collective-permute-done | bytes 1048608 | tf_op jit(solution)/shard_map/ppermute | solution.py:14
  500.8 20.3 %all-reduce.6 = (f32[128,64]{1,0:T(8,128)S(1)}, bf16[128,64]{1,0:T(8,128)(2,1)}, f32[128,64]{1,0:T(8,128)S(1)}, bf16[128,64]{1,0:T(8,128)(2,1)}, f32[128,64]{1,0...) all-reduce(f32[128,64]{1,0:T(8,128)} %convolution_multiply_fusion.3, ...), channel_id=1, replica_groups=mesh['pipe'=4,'dp'=4,'tensor'=2] {'tensor'}, use_global_device_ids=true, to_apply=%region_0.1 | all-reduce | flops 131072 | bytes 901120 | tf_op jit(solution)/shard_map/psum | solution.py:84
  (170 shorter events, 54.5 us)
Async XLA Ops:
  6.5 2.5 copy-start
  6.5 36.8 %all-gather.18.cloned.1.call-start = ((), (), s32[]{:S(2)}) async-start(), calls=%async_computation.5 | async-start | bytes 3145728 | tf_op jit(solution)/shard_map/all_gather | solution.py:89
  9.0 106.5 %all-gather.8.cloned.1.call-start = ((), (), s32[]{:S(2)}) async-start(), calls=%async_computation | async-start | bytes 3145728 | tf_op jit(solution)/shard_map/all_gather | solution.py:89
  43.4 1.6 copy-start.1
  48.0 31.6 %collective-permute-start = (bf16[128,4096]{1,0:T(8,128)(2,1)}, bf16[128,4096]{1,0:T(8,128)(2,1)}, u32[]{:S(2)}, u32[]{:S(2)}) collective-permute-start(bf16[128,4096]{1,0:T(8,128)(2,1)} %fusion.1), channel_id=1, source_target_pairs={{8,0},{16,8},{24,16},{9,1},{17,9},{25,17},{10,2},{18,10},{26,18},{... | collective-permute-start | bytes 3145736 | tf_op jit(solution)/shard_map/ppermute | solution.py:14
  82.2 117.2 %all-gather.10.cloned.1.call-start = ((), (), s32[]{:S(2)}) async-start(), calls=%async_computation.1 | async-start | bytes 3145728 | tf_op jit(solution)/shard_map/all_gather | solution.py:89
  148.4 14.5 %collective-permute-start.1 = (bf16[128,4096]{1,0:T(8,128)(2,1)}, bf16[128,4096]{1,0:T(8,128)(2,1)}, u32[]{:S(2)}, u32[]{:S(2)}) collective-permute-start(bf16[128,4096]{1,0:T(8,128)(2,1)} %add_convert_fusion.4), channel_id=1, source_target_pairs={{8,0},{16,8},{24,16},{9,1},{17,9},{25,17},{10,2},{18,10},{26,18},{... | collective-permute-start | bytes 3145736 | tf_op jit(solution)/shard_map/ppermute | solution.py:14
  165.7 119.0 %all-gather.12.cloned.1.call-start = ((), (), s32[]{:S(2)}) async-start(), calls=%async_computation.2 | async-start | bytes 3145728 | tf_op jit(solution)/shard_map/all_gather | solution.py:89
  232.3 14.6 %collective-permute-start.2 = (bf16[128,4096]{1,0:T(8,128)(2,1)}, bf16[128,4096]{1,0:T(8,128)(2,1)}, u32[]{:S(2)}, u32[]{:S(2)}) collective-permute-start(bf16[128,4096]{1,0:T(8,128)(2,1)} %add_convert_fusion.3), channel_id=1, source_target_pairs={{8,0},{16,8},{24,16},{9,1},{17,9},{25,17},{10,2},{18,10},{26,18},{... | collective-permute-start | bytes 3145736 | tf_op jit(solution)/shard_map/ppermute | solution.py:14
  249.5 94.8 %all-reduce.5.cloned.1.call-start = ((), (), s32[]{:S(2)}) async-start(), calls=%async_computation.6 | async-start | bytes 917504 | tf_op jit(solution)/shard_map/psum | solution.py:84
  249.7 4.7 copy-start.6
  257.6 2.2 copy-start.32
  257.6 11.3 %copy-start.29 = (s32[128,128]{1,0:T(8,128)S(1)}, s32[128,128]{1,0:T(8,128)}, u32[]{:S(2)}) copy-start(s32[128,128]{1,0:T(8,128)} %param.26) | copy-start | bytes 196612
  259.7 109.4 %all-gather.14.cloned.1.call-start = ((), (), s32[]{:S(2)}) async-start(), calls=%async_computation.3 | async-start | bytes 3145728 | tf_op jit(solution)/shard_map/all_gather | solution.py:89
  314.3 6.6 %copy-start.2 = (bf16[4096,64]{0,1:T(8,128)(2,1)S(1)}, bf16[4096,64]{0,1:T(8,128)(2,1)}, u32[]{:S(2)}) copy-start(bf16[4096,64]{0,1:T(8,128)(2,1)} %fusion.3) | copy-start | bytes 1572868
  314.3 6.6 %copy-start.7 = (bf16[4,1,128,4096]{3,2,1,0:T(8,128)(2,1)S(1)}, bf16[4,1,128,4096]{3,2,1,0:T(8,128)(2,1)}, u32[]{:S(2)}) copy-start(bf16[4,1,128,4096]{3,2,1,0:T(8,128)(2,1)} %param.21) | copy-start | bytes 12582916
  316.9 6.1 %copy-start.14 = (bf16[1,128,4096]{2,1,0:T(8,128)(2,1)S(1)}, bf16[1,128,4096]{2,1,0:T(8,128)(2,1)}, u32[]{:S(2)}) copy-start(bf16[1,128,4096]{2,1,0:T(8,128)(2,1)} %dynamic-slice_select_fusion) | copy-start | bytes 3145732
  316.9 14.4 %collective-permute-start.3 = (bf16[128,4096]{1,0:T(8,128)(2,1)S(1)}, bf16[128,4096]{1,0:T(8,128)(2,1)S(1)}, u32[]{:S(2)}, u32[]{:S(2)}) collective-permute-start(bf16[128,4096]{1,0:T(8,128)(2,1)S(1)} %add_convert_fusion.2), channel_id=1, source_target_pairs={{8,0},{16,8},{24,16},{9,1},{17,9},{25,17},{10,2},{18,10},{26,18},{... | collective-permute-start | bytes 3145736 | tf_op jit(solution)/shard_map/ppermute | solution.py:14
  333.6 118.5 %all-gather.16.cloned.1.call-start = ((), (), s32[]{:S(2)}) async-start(), calls=%async_computation.4 | async-start | bytes 3145728 | tf_op jit(solution)/shard_map/all_gather | solution.py:89
  334.9 5.0 copy-start.3
  334.9 7.3 %copy-start.8 = (bf16[4,1,128,4096]{3,2,1,0:T(8,128)(2,1)S(1)}, bf16[4,1,128,4096]{3,2,1,0:T(8,128)(2,1)}, u32[]{:S(2)}) copy-start(bf16[4,1,128,4096]{3,2,1,0:T(8,128)(2,1)} %param.21) | copy-start | bytes 12582916
  398.6 4.5 copy-start.28
  398.6 5.4 %copy-start.27 = (f32[128,128]{1,0:T(8,128)S(1)}, f32[128,128]{1,0:T(8,128)}, u32[]{:S(2)}) copy-start(f32[128,128]{1,0:T(8,128)} %get-tuple-element.75) | copy-start | bytes 196612
  398.6 6.3 %copy-start.26 = (f32[128,128]{1,0:T(8,128)S(1)}, f32[128,128]{1,0:T(8,128)}, u32[]{:S(2)}) copy-start(f32[128,128]{1,0:T(8,128)} %get-tuple-element.78) | copy-start | bytes 196612
  398.6 7.3 %copy-start.25 = (f32[128,128]{1,0:T(8,128)S(1)}, f32[128,128]{1,0:T(8,128)}, u32[]{:S(2)}) copy-start(f32[128,128]{1,0:T(8,128)} %get-tuple-element.77) | copy-start | bytes 196612
  398.6 8.1 %copy-start.24 = (f32[128,128]{1,0:T(8,128)S(1)}, f32[128,128]{1,0:T(8,128)}, u32[]{:S(2)}) copy-start(f32[128,128]{1,0:T(8,128)} %get-tuple-element.80) | copy-start | bytes 196612
  401.1 14.3 %collective-permute-start.4 = (bf16[128,4096]{1,0:T(8,128)(2,1)S(1)}, bf16[128,4096]{1,0:T(8,128)(2,1)S(1)}, u32[]{:S(2)}, u32[]{:S(2)}) collective-permute-start(bf16[128,4096]{1,0:T(8,128)(2,1)S(1)} %add_convert_fusion.1), channel_id=1, source_target_pairs={{8,0},{16,8},{24,16},{9,1},{17,9},{25,17},{10,2},{18,10},{26,18},{... | collective-permute-start | bytes 3145736 | tf_op jit(solution)/shard_map/ppermute | solution.py:14
  417.8 4.5 copy-start.4
  417.8 4.5 copy-start.9
  417.8 6.3 %copy-start.10 = (bf16[128,4096]{1,0:T(8,128)(2,1)S(1)}, bf16[128,4096]{1,0:T(8,128)(2,1)}, u32[]{:S(2)}) copy-start(bf16[128,4096]{1,0:T(8,128)(2,1)} %bitcast_select_fusion.3) | copy-start | bytes 3145732
  421.5 3.6 copy-start.12
  453.7 32.7 %copy-start.5 = (bf16[4096,64]{0,1:T(8,128)(2,1)S(1)}, bf16[4096,64]{0,1:T(8,128)(2,1)}, u32[]{:S(2)}) copy-start(bf16[4096,64]{0,1:T(8,128)(2,1)} %fusion.3) | copy-start | bytes 1572868
  453.7 32.7 %copy-start.11 = (bf16[128,4096]{1,0:T(8,128)(2,1)S(1)}, bf16[128,4096]{1,0:T(8,128)(2,1)}, u32[]{:S(2)}) copy-start(bf16[128,4096]{1,0:T(8,128)(2,1)} %bitcast_select_fusion.2) | copy-start | bytes 3145732
  453.7 44.9 %copy-start.15 = (bf16[4,128,4096]{2,1,0:T(8,128)(2,1)S(1)}, bf16[4,128,4096]{2,1,0:T(8,128)(2,1)}, u32[]{:S(2)}) copy-start(bf16[4,128,4096]{2,1,0:T(8,128)(2,1)} %param.20) | copy-start | bytes 12582916
  456.3 31.3 %copy-start.13 = (bf16[128,4096]{1,0:T(8,128)(2,1)S(1)}, bf16[128,4096]{1,0:T(8,128)(2,1)}, u32[]{:S(2)}) copy-start(bf16[128,4096]{1,0:T(8,128)(2,1)} %bitcast_select_fusion.1) | copy-start | bytes 3145732
  456.3 42.3 %collective-permute-start.5 = (bf16[128,4096]{1,0:T(8,128)(2,1)S(1)}, bf16[128,4096]{1,0:T(8,128)(2,1)S(1)}, u32[]{:S(2)}, u32[]{:S(2)}) collective-permute-start(bf16[128,4096]{1,0:T(8,128)(2,1)S(1)} %add_convert_fusion), channel_id=1, source_target_pairs={{8,0},{16,8},{24,16},{9,1},{17,9},{25,17},{10,2},{18,10},{26,18},{... | collective-permute-start | bytes 3145736 | tf_op jit(solution)/shard_map/ppermute | solution.py:14
  499.7 21.4 %copy-start.21 = (f32[128,64]{1,0:T(8,128)S(1)}, f32[128,64]{1,0:T(8,128)}, u32[]{:S(2)}) copy-start(f32[128,64]{1,0:T(8,128)} %convolution_multiply_fusion.32) | copy-start | bytes 98308
  499.7 23.4 %copy-start.23 = (f32[128,64]{1,0:T(8,128)S(1)}, f32[128,64]{1,0:T(8,128)}, u32[]{:S(2)}) copy-start(f32[128,64]{1,0:T(8,128)} %convolution_multiply_fusion.24) | copy-start | bytes 98308
  499.7 24.5 %copy-start.20 = (f32[128,64]{1,0:T(8,128)S(1)}, f32[128,64]{1,0:T(8,128)}, u32[]{:S(2)}) copy-start(f32[128,64]{1,0:T(8,128)} %convolution_multiply_fusion.23) | copy-start | bytes 98308
  499.7 25.5 %copy-start.19 = (f32[128,64]{1,0:T(8,128)S(1)}, f32[128,64]{1,0:T(8,128)}, u32[]{:S(2)}) copy-start(f32[128,64]{1,0:T(8,128)} %convolution_multiply_fusion.27) | copy-start | bytes 98308
  499.7 26.6 %copy-start.22 = (f32[128,64]{1,0:T(8,128)S(1)}, f32[128,64]{1,0:T(8,128)}, u32[]{:S(2)}) copy-start(f32[128,64]{1,0:T(8,128)} %convolution_multiply_fusion.28) | copy-start | bytes 98308
  499.7 27.4 %copy-start.18 = (f32[128,64]{1,0:T(8,128)S(1)}, f32[128,64]{1,0:T(8,128)}, u32[]{:S(2)}) copy-start(f32[128,64]{1,0:T(8,128)} %convolution_multiply_fusion.15) | copy-start | bytes 98308
  499.7 28.5 %copy-start.17 = (f32[128,64]{1,0:T(8,128)S(1)}, f32[128,64]{1,0:T(8,128)}, u32[]{:S(2)}) copy-start(f32[128,64]{1,0:T(8,128)} %convolution_multiply_fusion.19) | copy-start | bytes 98308
  521.9 8.3 %copy-start.31 = (bf16[128,64]{1,0:T(8,128)(2,1)S(1)}, bf16[128,64]{1,0:T(8,128)(2,1)}, u32[]{:S(2)}) copy-start(bf16[128,64]{1,0:T(8,128)(2,1)} %get-tuple-element.73) | copy-start | bytes 49156
  521.9 8.6 %copy-start.30 = (bf16[128,64]{1,0:T(8,128)(2,1)S(1)}, bf16[128,64]{1,0:T(8,128)(2,1)}, u32[]{:S(2)}) copy-start(bf16[128,64]{1,0:T(8,128)(2,1)} %get-tuple-element.70) | copy-start | bytes 49156
  532.2 0.6 copy-start.16
Sparse Core Ops, SparseCore 0:
  9.1 34.2 all-gather.17
  82.3 33.1 all-gather.7
  165.8 33.5 all-gather.9
  249.6 35.0 all-gather.11
  287.2 28.1 all-reduce.4
  333.7 35.3 all-gather.13
  417.9 34.2 all-gather.15
where the time goes:
time: 547 us; the launch traced here: 541 us
  matrix products  189 us (35%)
  waiting for transfers between devices  174 us (32%)
  blocking collectives  74 us (14%)
  other arithmetic  43.9 us (8%)
  starting transfers between devices  40.2 us (7%)
  between operations  14.2 us (3%)
  local copies, waits for them, and re-layouts  5.69 us (1%)
    dot_general x17, matrix products, times_t(): lax.dot_general(left, right, (((1,), (1,)), ((), ())), preferred_element_...  141 us
    all_gather x6, waiting for transfers between devices, per_device(): piece = lax.all_gather(dy_cols, 'tensor', axis=1, tiled=True)  93.4 us
    ppermute x6, waiting for transfers between devices, from_behind(): lax.ppermute(value, axis, [(source, source + steps) for source in range(l...  80.2 us
    psum x7, blocking collectives, per_device(): lax.psum((u_part, yp_part, xp_part, xa_part), 'tensor')  74 us
    ppermute x6, starting transfers between devices, from_behind(): lax.ppermute(value, axis, [(source, source + steps) for source in range(l...  39.8 us
    select_n x6, other arithmetic, per_device(): dy_cols = jnp.where(is_last, given, incoming)  14.9 us
    convert_element_type x5, other arithmetic, per_device(): (frozen_weight + ADAPTER_SCALE * times_t(u_all, down_factor_local)).astyp...  14.4 us
    dot_general x7, matrix products, per_device(): jnp.dot(current_input, wide_rows, preferred_element_type=jnp.float32)  11.4 us
  transfers between devices with their start and end apart: 13, of which 12 were waited for; matrix products, arithmetic and copies ran while one was open for 19% of the time, Pallas kernels for 0%

commit v1 on v0

v1 whole, which is shorter than its diff:
```python
import functools
import math

import jax
import jax.numpy as jnp
from jax import lax
from jax.experimental import pallas as pl
from jax.experimental.pallas import tpu as pltpu
from jax.sharding import PartitionSpec as P

ADAPTER_SCALE = 2.0
AXES = ("pipe", "dp", "tensor")
F32 = jnp.float32
BF16 = jnp.bfloat16


def nt(left, right, precision=None):
    return lax.dot_general(
        left, right, (((1,), (1,)), ((), ())), precision=precision, preferred_element_type=F32
    )


def shift(value, source_stage, target_stage, by_dp, by_tensor):
    groups, parts = lax.axis_size("dp"), lax.axis_size("tensor")

    def place(stage, group, part):
        return (stage * groups + group % groups) * parts + part % parts

    pairs = [
        (place(source_stage, g, k), place(target_stage, g + by_dp, k + by_tensor))
        for g in range(groups)
        for k in range(parts)
    ]
    return lax.ppermute(value, AXES, pairs)


def pull_kernel(group, x_ref, w_ref, a_ref, b_ref, out_ref, low_ref):
    @pl.when(pl.program_id(0) == 0)
    def _():
        low = jnp.dot(x_ref[...], a_ref[...], preferred_element_type=F32)
        low_ref[...] = (ADAPTER_SCALE * low).astype(BF16)

    total = jnp.dot(x_ref[...], w_ref[...], preferred_element_type=F32)
    total += jnp.dot(low_ref[...], b_ref[...], preferred_element_type=F32)
    out_ref[...] = total.astype(BF16)


def pull(x, weight, down, up, group, groups, parts):
    rows, depth = x.shape
    rank, width = up.shape
    run = width // parts // groups
    block = min(512, run)
    per_run = run // block

    def column(j, group_ref):
        return (j // per_run) * (groups * per_run) + group_ref[0] * per_run + j % per_run

    return pl.pallas_call(
        pull_kernel,
        grid_spec=pltpu.PrefetchScalarGridSpec(
            num_scalar_prefetch=1,
            grid=(parts * per_run,),
            in_specs=[
                pl.BlockSpec((rows, depth), lambda j, g: (0, 0)),
                pl.BlockSpec((depth, block), lambda j, g: (0, column(j, g))),
                pl.BlockSpec((depth, rank), lambda j, g: (0, 0)),
                pl.BlockSpec((rank, block), lambda j, g: (0, column(j, g))),
            ],
            out_specs=pl.BlockSpec((rows, block), lambda j, g: (0, j)),
            scratch_shapes=[pltpu.VMEM((rows, rank), BF16)],
        ),
        out_shape=jax.ShapeDtypeStruct((rows, parts * run), BF16),
        compiler_params=pltpu.CompilerParams(vmem_limit_bytes=40 * 2**20),
    )(group.reshape(1), x, weight, down, up)


def first_push_kernel(part, g_ref, w_ref, out_ref):
    out_ref[...] = nt(g_ref[...], w_ref[...])


def first_push(grad, weight, part):
    tokens, depth = grad.shape
    rows = weight.shape[0]
    block = min(512, rows)
    return pl.pallas_call(
        first_push_kernel,
        grid_spec=pltpu.PrefetchScalarGridSpec(
            num_scalar_prefetch=1,
            grid=(rows // block,),
            in_specs=[
                pl.BlockSpec((tokens, depth), lambda i, p: (0, 0)),
                pl.BlockSpec((block, depth), lambda i, p: (i, p[0])),
            ],
            out_specs=pl.BlockSpec((tokens, block), lambda i, p: (0, i)),
        ),
        out_shape=jax.ShapeDtypeStruct((tokens, rows), F32),
        compiler_params=pltpu.CompilerParams(vmem_limit_bytes=40 * 2**20),
    )(part.reshape(1), grad, weight)


def last_push_kernel(others, part, near_ref, far_ref, w_ref, acc_ref, u_ref, a_ref, out_ref, total_ref):
    k = pl.program_id(1)

    @pl.when(k == 0)
    def _():
        total_ref[...] = acc_ref[...] + ADAPTER_SCALE * nt(u_ref[...], a_ref[...])

    half = near_ref.shape[1]
    total_ref[:half] += nt(near_ref[0], w_ref[...])
    total_ref[half:] += nt(far_ref[0], w_ref[...])

    @pl.when(k == others - 1)
    def _():
        out_ref[...] = total_ref[...].astype(BF16)


def last_push(near, far, weight, total, u_all, down, part, parts):
    others, half, depth = near.shape
    tokens = total.shape[0]
    rows = weight.shape[0]
    rank = down.shape[1]
    block = min(512, rows)
    return pl.pallas_call(
        functools.partial(last_push_kernel, others),
        grid_spec=pltpu.PrefetchScalarGridSpec(
            num_scalar_prefetch=1,
            grid=(rows // block, others),
            in_specs=[
                pl.BlockSpec((1, half, depth), lambda i, k, p: (k, 0, 0)),
                pl.BlockSpec((1, half, depth), lambda i, k, p: (k, 0, 0)),
                pl.BlockSpec((block, depth), lambda i, k, p: (i, lax.rem(p[0] + k + 1, parts))),
                pl.BlockSpec((tokens, block), lambda i, k, p: (0, i)),
                pl.BlockSpec((tokens, rank), lambda i, k, p: (0, 0)),
                pl.BlockSpec((block, rank), lambda i, k, p: (i, 0)),
            ],
            out_specs=pl.BlockSpec((tokens, block), lambda i, k, p: (0, i)),
            scratch_shapes=[pltpu.VMEM((tokens, block), F32)],
        ),
        out_shape=jax.ShapeDtypeStruct((tokens, rows), BF16),
        compiler_params=pltpu.CompilerParams(vmem_limit_bytes=40 * 2**20),
    )(part.reshape(1), near, far, weight, total, u_all, down)


def per_device(
    output_gradient,
    acts,
    weights,
    adapter_down_factors,
    adapter_up_factors,
    feature_sign_bits,
    rank_sign_bits,
    lengths,
):
    stages, groups, parts = (lax.axis_size(name) for name in AXES)
    stage, group, part = (lax.axis_index(name) for name in AXES)
    last = stages - 1
    count, seq, local = output_gradient.shape
    tokens = count * seq
    width = local * parts
    rank = adapter_up_factors.shape[1]
    proj = feature_sign_bits.shape[1]
    run = local // groups
    grad = output_gradient.reshape(tokens, local)
    saved = acts[:, 0].reshape(tokens, local)
    weight, down, up = weights[0], adapter_down_factors[0], adapter_up_factors[0]

    def local_columns(whole, which):
        return lax.dynamic_slice_in_dim(whole, which * local, local, 1)

    near = [shift(grad[: tokens // 2], last, last, 0, -k) for k in range(1, parts)]
    far = [shift(grad[tokens // 2 :], 0, last, 0, -k) for k in range(1, parts)]

    bits = lax.dynamic_slice_in_dim(feature_sign_bits, part * local, local, 0)
    signs = (2 * bits - 1).astype(BF16).T
    low = 2 * rank_sign_bits - 1
    low_left, low_right = low[:, :proj].astype(BF16), low[:, proj:].astype(F32)

    up_low = lax.dot_general(
        low_left, local_columns(up, part), (((0,), (0,)), ((), ())), preferred_element_type=F32
    ).astype(BF16)
    below = [shift(up_low, s, s + 1, 0, 0) for s in range(last)]

    def on(wanted, step, shape, dtype):
        return lax.cond(stage == wanted, step, lambda: jnp.zeros(shape, dtype))

    reach = {last - 1: []}
    moving = None
    finished = []
    for s in range(1, last):
        own = jnp.concatenate([below[s - 1], signs])
        if s > 1:
            whole = on(
                s, lambda: pull(own, weight, down, up, 0 * group, 1, parts), (2 * proj, width), BF16
            )
            total = 0
            for k in range(parts):
                target = lax.rem(part + k, parts)
                total += shift(local_columns(whole, target), s, s + 1, 0, k).astype(F32)
            finished.append(total.astype(BF16))
        source = own if s == 1 else moving
        pulled = on(
            s,
            lambda: pull(source, weight, down, up, group, groups, parts),
            (2 * proj, parts * run),
            BF16,
        )
        total = 0
        for k in range(parts):
            target = lax.rem(part + k, parts)
            total += shift(lax.dynamic_slice_in_dim(pulled, target * run, run, 1), s, s + 1, 0, k).astype(F32)
        slice_ = total.astype(BF16)
        moving = jnp.zeros((2 * proj, local), BF16)
        moving = lax.dynamic_update_slice_in_dim(moving, slice_, group * run, 1)
        for k in range(1, groups):
            origin = lax.rem(group + groups - k, groups)
            arrived = shift(slice_, s + 1, s + 1, k, 0)
            moving = lax.dynamic_update_slice_in_dim(moving, arrived, origin * run, 1)

    begun = on(last, lambda: first_push(grad, weight, part), (tokens, local), F32)
    near, far = jnp.stack(near), jnp.stack(far)

    def finish():
        def sums(right):
            total = nt(grad, right[0])
            for k in range(1, parts):
                other = jnp.concatenate([near[k - 1], far[k - 1]])
                total += nt(other, right[k])
            return total

        order = [lax.rem(part + k, parts) for k in range(parts)]
        u_all = sums([local_columns(up, q) for q in order]).astype(BF16)
        every = (2 * feature_sign_bits - 1).astype(BF16).T
        yp = sums([local_columns(every, q) for q in order])
        uq = jnp.dot(u_all, low_left, preferred_element_type=F32)
        return last_push(near, far, weight, begun, u_all, down, part, parts), jnp.concatenate([uq, yp], 1)

    grad_below, mine_last = lax.cond(
        stage == last,
        finish,
        lambda: (jnp.zeros((tokens, local), BF16), jnp.zeros((tokens, 2 * proj), F32)),
    )

    x_signs = nt(saved, signs)
    x_down = jnp.dot(saved, down, preferred_element_type=F32)
    x_low = jnp.dot(x_down, low_right, precision=lax.Precision.HIGHEST, preferred_element_type=F32)
    x_part = jnp.concatenate([x_signs, x_low], 1)
    share = 2 * proj // parts
    x_side = 0
    for k in range(parts):
        target = lax.rem(part + k, parts)
        piece = lax.dynamic_slice_in_dim(x_part, target * share, share, 1)
        if k:
            piece = lax.ppermute(piece, "tensor", [(q, (q + k) % parts) for q in range(parts)])
        x_side += piece

    def side_of(which):
        return which * 2 // parts * proj

    y_side = lax.dynamic_slice_in_dim(mine_last, side_of(part), proj, 1)
    rights = [jnp.concatenate([below[last - 1], signs])] + finished + [moving]
    for s, right in zip(range(last - 1, -1, -1), rights):
        y_part = nt(grad_below, right)
        total = 0
        for k in range(parts):
            target = lax.rem(part + k, parts)
            piece = lax.dynamic_slice_in_dim(y_part, side_of(target), proj, 1)
            total += shift(piece, last, s, 0, k)
        y_side = jnp.where(stage == s, total, y_side)

    keep = jnp.arange(seq)[None, :] < lengths[:, None]
    scale = ADAPTER_SCALE / math.sqrt(seq) / math.sqrt(width) / math.sqrt(rank)
    left = jnp.where(keep[:, :, None], x_side.reshape(count, seq, share), 0.0) * scale
    right = y_side.reshape(count, seq, proj)
    feats = lax.dot_general(
        left,
        right,
        (((1,), (1,)), ((0,), (0,))),
        precision=lax.Precision.HIGHEST,
        preferred_element_type=F32,
    )
    return feats.reshape(count, 1, share * proj)


def solution(mesh):
    placed = (
        P("dp", None, "tensor"),
        P("dp", "pipe", None, "tensor"),
        P("pipe", "tensor", None),
        P("pipe", "tensor", None),
        P("pipe", None, None),
        P(),
        P(),
        P("dp"),
    )
    return jax.shard_map(
        per_device, mesh=mesh, in_specs=placed, out_specs=P("dp", "pipe", "tensor"), check_vma=False
    )
```

time: 547 us -> 239 us (0.44)
  matrix products: 189 us -> 22.2 us
  waiting for transfers between devices: 174 us -> 87.9 us
  blocking collectives: 74 us -> 0 us
  Pallas kernels: 0 us -> 36.9 us
  other arithmetic: 43.9 us -> 7.96 us
  local copies, waits for them, and re-layouts: 5.69 us -> 40.4 us
  between operations: 14.2 us -> 0.37 us
    dot_general x66 -> x8, matrix products: 189 us -> 22.2 us  [the longest x4 16.1 us: nt(): lax.dot_general(left, right, (((1,), (1,)), ((), ())), precision=precisio...]
    all_gather x6 -> x0, waiting for transfers between devices: 93.4 us -> none  [per_device(): piece = lax.all_gather(dy_cols, 'tensor', axis=1, tiled=True)]
    psum x7 -> x0, blocking collectives: 74 us -> none  [per_device(): lax.psum((u_part, yp_part, xp_part, xa_part), 'tensor')]
    pallas_call x0 -> x2, Pallas kernels: none -> 36.9 us  [pull(): pl.pallas_call(pull_kernel, grid_spec=pltpu.PrefetchScalarGridSpec(num_sc...]
    convert_element_type x14 -> x1, other arithmetic: 22.5 us -> 0.07 us  [per_device(): slice_ = total.astype(BF16)]
    dynamic_update_slice x0 -> x7, local copies, waits for them, and re-layouts: none -> 17.4 us  [the longest x6 14.9 us: per_device(): moving = lax.dynamic_update_slice_in_dim(moving, arrived, origin * run, 1)]
    select_n x13 -> x0, other arithmetic: 16.4 us -> none  [the longest x6 14.9 us: per_device(): dy_cols = jnp.where(is_last, given, incoming)]
    ppermute x6 -> x24, waiting for transfers between devices: 80.2 us -> 87.9 us  [the longest x23 87.9 us: shift(): return lax.ppermute(value, AXES, pairs)]
  transfers between devices with their start and end apart: 13 -> 24, of which waited for: 12 -> 6; matrix products, arithmetic and copies ran while one was open for 19% -> 24% of each run, Pallas kernels for 0% -> 16%
where the time goes in v1:
time: 239 us; the launch traced here: 237 us
  waiting for transfers between devices  87.9 us (37%)
  starting transfers between devices  41.3 us (17%)
  local copies, waits for them, and re-layouts  40.4 us (17%)
  Pallas kernels  36.9 us (15%)
  matrix products  22.2 us (9%)
  other arithmetic  7.96 us (3%)
    ppermute x23, waiting for transfers between devices, shift(): return lax.ppermute(value, AXES, pairs)  87.9 us
    ppermute x23, starting transfers between devices, shift(): return lax.ppermute(value, AXES, pairs)  39.8 us
    pallas_call x2, Pallas kernels, pull(): pl.pallas_call(pull_kernel, grid_spec=pltpu.PrefetchScalarGridSpec(num_sc...  36.9 us
    dot_general x4, matrix products, nt(): lax.dot_general(left, right, (((1,), (1,)), ((), ())), precision=precisio...  16.1 us
    dynamic_update_slice x6, local copies, waits for them, and re-layouts, per_device(): moving = lax.dynamic_update_slice_in_dim(moving, arrived, origin * run, 1)  14.9 us
    another operation x6, local copies, waits for them, and re-layouts  8.94 us
    slice x1, local copies, waits for them, and re-layouts, per_device(): far = [shift(grad[tokens // 2:], 0, last, 0, -k) for k in range(1, parts)]  4.78 us
  transfers between devices with their start and end apart: 24, of which 6 were waited for; matrix products, arithmetic and copies ran while one was open for 24% of the time, Pallas kernels for 16%

profile of v1, /device:TPU:12, one launch (start us, length us, event | category | flops | bytes accessed | tf_op | source)
XLA Modules:
  0.0 237.2 jit_solution(12816679859766145843)
XLA Ops:
  0.0 1.0 multiply_add_fusion
  1.0 2.4 %convolution_convert_fusion = bf16[64,4096]{1,0:T(8,128)(2,1)} fusion(bf16[128,64]{1,0:T(8,128)(2,1)S(1)} %slice_convert_fusion, bf16[1,128,8192]{2,1,0:T(8,128)(2,1)} %param.22, s32[]{:T(128)S(6)} %select_n.100), kind=kOutput, calls=%fused_computation.19 | convolution fusion | flops 67371008 | bytes 1589252 | tf_op jit(solution)/shard_map/dot_general | solution.py:178
  3.4 1.3 collective-permute-start.16
  4.7 1.5 collective-permute-start.3
  6.2 1.3 fusion.28
  7.5 6.7 %collective-permute-done.16 = bf16[64,4096]{1,0:T(8,128)(2,1)} collective-permute-done((bf16[64,4096]{1,0:T(8,128)(2,1)}, bf16[64,4096]{1,0:T(8,128)(2,1)}, u32[]{:S(2)}, u32[]{:S(2)}) %collective-permute-start.16) | collective-permute-done | bytes 524320 | tf_op jit(solution)/shard_map/ppermute | solution.py:34
  14.2 2.8 %pad_maximum_fusion.3 = (bf16[128,4096]{1,0:T(8,128)(2,1)}, bf16[128,4096]{1,0:T(8,128)(2,1)}) fusion(bf16[64,4096]{1,0:T(8,128)(2,1)S(1)} %fusion.28, bf16[64,4096]{1,0:T(8,128)(2,1)} %collective-permute-done.3, bf16[64,4096]{1,0:T(8,128)(2,1)} %collective-permute-done.16), kind=kLoop, calls=%fused_computation.23 | loop fusion | flops 3670016 | bytes 3670016 | tf_op jit(solution)/shard_map/concatenate | solution.py:190
  17.1 0.9 conditional.7
  17.1 0.9 broadcast.56
  18.0 1.1 constant_dynamic-slice_fusion.11
  19.0 1.3 collective-permute-start.4
  20.3 1.6 collective-permute-start.5
  21.9 4.8 %fusion.42 = (bf16[2,128,4096]{2,1,0:T(8,128)(2,1)}, bf16[2,128,4096]{2,1,0:T(8,128)(2,1)}) fusion(bf16[4,128,4096]{2,1,0:T(8,128)(2,1)} %param.18), kind=kLoop, calls=%fused_computation.82 | loop fusion | bytes 8388608 | tf_op jit(solution)/shard_map/slice | solution.py:171
  26.7 2.0 collective-permute-start.1
  28.7 2.0 collective-permute-start.2
  30.7 26.2 %collective-permute-done.4 = bf16[128,1024]{1,0:T(8,128)(2,1)S(1)} collective-permute-done((bf16[128,1024]{1,0:T(8,128)(2,1)S(1)}, bf16[128,1024]{1,0:T(8,128)(2,1)S(1)}, u32[]{:S(2)}, u32[]{:S(2)}) %collective-permute-start.4) | collective-permute-done | bytes 262176 | tf_op jit(solution)/shard_map/ppermute | solution.py:34
  57.0 3.5 %collective-permute-start.6 = (bf16[128,1024]{1,0:T(8,128)(2,1)S(1)}, bf16[128,1024]{1,0:T(8,128)(2,1)}, u32[]{:S(2)}, u32[]{:S(2)}) collective-permute-start(bf16[128,1024]{1,0:T(8,128)(2,1)S(1)} %add_convert_fusion.5), channel_id=1, source_target_pairs={{16,18},{17,19},{18,20},{19,21},{20,22},{21,23},{22,16},{23,17}} | collective-permute-start | bytes 786440 | tf_op jit(solution)/shard_map/ppermute | solution.py:34
  60.5 3.1 %collective-permute-start.7 = (bf16[128,1024]{1,0:T(8,128)(2,1)S(1)}, bf16[128,1024]{1,0:T(8,128)(2,1)}, u32[]{:S(2)}, u32[]{:S(2)}) collective-permute-start(bf16[128,1024]{1,0:T(8,128)(2,1)S(1)} %add_convert_fusion.5), channel_id=1, source_target_pairs={{16,20},{17,21},{18,22},{19,23},{20,16},{21,17},{22,18},{23,19}} | collective-permute-start | bytes 786440 | tf_op jit(solution)/shard_map/ppermute | solution.py:34
  63.6 3.7 %collective-permute-start.8 = (bf16[128,1024]{1,0:T(8,128)(2,1)S(1)}, bf16[128,1024]{1,0:T(8,128)(2,1)}, u32[]{:S(2)}, u32[]{:S(2)}) collective-permute-start(bf16[128,1024]{1,0:T(8,128)(2,1)S(1)} %add_convert_fusion.5), channel_id=1, source_target_pairs={{16,22},{17,23},{18,16},{19,17},{20,18},{21,19},{22,20},{23,21}} | collective-permute-start | bytes 786440 | tf_op jit(solution)/shard_map/ppermute | solution.py:34
  67.3 2.0 fusion.36
  69.3 3.8 %collective-permute-done.7 = bf16[128,1024]{1,0:T(8,128)(2,1)} collective-permute-done((bf16[128,1024]{1,0:T(8,128)(2,1)S(1)}, bf16[128,1024]{1,0:T(8,128)(2,1)}, u32[]{:S(2)}, u32[]{:S(2)}) %collective-permute-start.7) | collective-permute-done | bytes 262176 | tf_op jit(solution)/shard_map/ppermute | solution.py:34
  73.1 1.5 collective-permute-done.8
  74.6 22.2 %conditional.8 = (bf16[128,2048]{1,0:T(8,128)(2,1)}) conditional(s32[]{:T(128)} %convert_element_type.57, () %tuple.45, (s32[]{:T(128)}, bf16[128,1024]{1,0:T(8,128)(2,1)S(1)}, s32[]{:T(128)}, bf16[128,1024]{1,0:T(8,128)(2,1)}, s32[]{:T(128)}, /*index=5*/bf16[128,1024]{1,0:T(8,128)(2,1)}, s32[]{:T(128)}, bf16[128,1024]{1,0:T(8,128)(2,1)}, s32[]{:T(128)}, ...), branch_computations={%region_6.0_spmd, %region_7.0_spmd} | conditional | bytes 7340086 | solution.py:184
  74.6 1.0 copy-done.4
  75.7 2.5 %dynamic_update_slice.36 = bf16[128,4096]{1,0:T(8,128)(2,1)S(1)} dynamic-update-slice(bf16[128,4096]{1,0:T(8,128)(2,1)S(1)} %broadcast.58, bf16[128,1024]{1,0:T(8,128)(2,1)S(1)} %get-tuple-element.169, s32[]{:T(128)} %constant.121.clone, s32[]{:T(128)} %get-tuple-element.170) | dynamic-update-slice | bytes 524292 | tf_op jit(solution)/shard_map/dynamic_update_slice | solution.py:213
  78.1 3.4 %dynamic_update_slice.37 = bf16[128,4096]{1,0:T(8,128)(2,1)S(1)} dynamic-update-slice(bf16[128,4096]{1,0:T(8,128)(2,1)S(1)} %dynamic_update_slice.36, bf16[128,1024]{1,0:T(8,128)(2,1)} %get-tuple-element.171, s32[]{:T(128)} %constant.121.clone, s32[]{:T(128)} %get-tuple-element.172) | dynamic-update-slice | bytes 524292 | tf_op jit(solution)/shard_map/dynamic_update_slice | solution.py:217
  81.5 3.1 %dynamic_update_slice.38 = bf16[128,4096]{1,0:T(8,128)(2,1)S(1)} dynamic-update-slice(bf16[128,4096]{1,0:T(8,128)(2,1)S(1)} %dynamic_update_slice.37, bf16[128,1024]{1,0:T(8,128)(2,1)} %get-tuple-element.173, s32[]{:T(128)} %constant.121.clone, s32[]{:T(128)} %get-tuple-element.174) | dynamic-update-slice | bytes 524292 | tf_op jit(solution)/shard_map/dynamic_update_slice | solution.py:217
  84.6 3.4 %dynamic_update_slice.39.x_ref = bf16[128,4096]{1,0:T(8,128)(2,1)S(1)} dynamic-update-slice(bf16[128,4096]{1,0:T(8,128)(2,1)S(1)} %dynamic_update_slice.38, bf16[128,1024]{1,0:T(8,128)(2,1)} %get-tuple-element.175, s32[]{:T(128)} %constant.121.clone, s32[]{:T(128)} %get-tuple-element.176) | dynamic-update-slice | bytes 524292 | tf_op jit(solution)/shard_map/dynamic_update_slice | solution.py:217
  88.0 8.8 %branch_1_fun.10 = bf16[128,2048]{1,0:T(8,128)(2,1)} custom-call(s32[1]{0:T(128)} %bitcast.7.group, bf16[128,4096]{1,0:T(8,128)(2,1)S(1)} %dynamic_update_slice.39.x_ref, bf16[4096,8192]{1,0:T(8,128)(2,1)} %get-tuple-element.177.w_ref, bf16[4096,128]{1,0:T(8,128)(2,1)} %copy-done.4, bf16[128,8192]{1,0:T(8,128)(2,1)S(1)} %get-tuple-element.179.b_ref), custom_call_target="tpu_custom_call" | custom-call | tf_op jit(solution)/shard_map/cond/branch_1_fun/pallas_call | solution.py:58
  96.8 1.9 constant_dynamic-slice_fusion.9
  98.8 2.0 collective-permute-start.10
  100.8 2.0 collective-permute-start.9
  102.8 3.9 %convolution_bitcast_fusion.2 = f32[512,64]{0,1:T(8,128)S(1)} fusion(bf16[512,4096]{1,0:T(8,128)(2,1)} %bitcast.72, s32[8192,64]{0,1:T(8,128)} %param.23, s32[]{:T(128)S(6)} %select_n.100), kind=kOutput, calls=%fused_computation.24 | convolution fusion | flops 269221888 | bytes 5373956 | tf_op jit(solution)/shard_map/dot_general | solution.py:18
  106.7 28.1 %conditional.9 = (bf16[128,8192]{1,0:T(8,128)(2,1)}) conditional(s32[]{:T(128)} %convert_element_type.57, () %tuple.49, (bf16[128,4096]{1,0:T(8,128)(2,1)}, bf16[4096,8192]{1,0:T(8,128)(2,1)}, bf16[4096,128]{1,0:T(8,128)(2,1)S(1)}, bf16[128,8192]{1,0:T(8,128)(2,1)S(1)}) %tuple.79), branch_computations={%region_8.0_spmd, %region_9.0_spmd} | conditional | bytes 2097162 | solution.py:184
  106.7 28.1 %branch_1_fun.11 = bf16[128,8192]{1,0:T(8,128)(2,1)} custom-call(s32[1]{0:T(128)} %constant.123.clone.group, bf16[128,4096]{1,0:T(8,128)(2,1)} %get-tuple-element.180.x_ref, bf16[4096,8192]{1,0:T(8,128)(2,1)} %get-tuple-element.181.w_ref, bf16[4096,128]{1,0:T(8,128)(2,1)S(1)} %get-tuple-element.182.a_ref, bf16[128,8192]{1,0:T(8,128)(2,1)S(1)} %get-tuple-element.183.b_ref), custom_call_target="tpu_custom_call" | custom-call | tf_op jit(solution)/shard_map/cond/branch_1_fun/pallas_call | solution.py:58
  134.8 1.1 broadcast.65
  135.9 2.0 constant_dynamic-update-slice_fusion.5
  138.5 1.4 collective-permute-start.12
  139.9 3.1 %constant_dynamic-slice_fusion.5 = (bf16[128,4096]{1,0:T(8,128)(2,1)}, bf16[128,4096]{1,0:T(8,128)(2,1)}) fusion(bf16[128,8192]{1,0:T(8,128)(2,1)} %get-tuple-element.223, s32[]{:T(128)S(6)} %select_n.116, s32[]{:T(128)S(6)} %select_n.117), kind=kLoop, calls=%fused_computation.61 | loop fusion | bytes 4194312 | tf_op jit(solution)/shard_map/dynamic_slice | solution.py:168
  143.0 2.3 collective-permute-start.17
  145.3 0.7 copy-done.14
  146.0 2.3 collective-permute-start.18
  148.8 1.4 collective-permute-start.13
  150.9 4.3 %conditional.5 = (f32[512,4096]{1,0:T(8,128)}) conditional(s32[]{:T(128)} %convert_element_type.56, () %tuple.42, (s32[]{:T(128)}, bf16[512,4096]{1,0:T(8,128)(2,1)}, bf16[4096,8192]{1,0:T(8,128)(2,1)}) %tuple.71), branch_computations={%region_0.0_spmd, %region_1.0_spmd} | conditional | bytes 8388620 | solution.py:184
  150.9 4.3 %broadcast.51 = f32[512,4096]{1,0:T(8,128)} broadcast(f32[]{:T(128)} %constant.109.clone), dimensions={} | broadcast | bytes 8388612 | tf_op jit(solution)/shard_map/broadcast.8
  155.2 1.7 constant_dynamic-update-slice_fusion.4
  156.9 1.7 constant_dynamic-update-slice_fusion.3
  158.6 2.1 collective-permute-start.21
  160.7 1.7 constant_dynamic-update-slice_fusion.2
  162.4 1.5 collective-permute-start
  163.9 2.6 %conditional.6 = (bf16[512,4096]{1,0:T(8,128)(2,1)}, f32[512,128]{0,1:T(8,128)S(1)}) conditional(s32[]{:T(128)} %convert_element_type.56, () %tuple.41, (s32[]{:T(128)}, bf16[256,4096]{1,0:T(8,128)(2,1)}, bf16[256,4096]{1,0:T(8,128)(2,1)}, bf16[128,8192]{1,0:T(8,128)(2,1)S(1)}, bf16[512,4096]{1,0:T(8,128)(2,1)}, ...), branch_computations={%region_2.0_spmd, %region_3.0_spmd} | conditional | flops 1620803584 | bytes 59588948 | solution.py:237
  163.9 2.6 %broadcast.52 = bf16[512,4096]{1,0:T(8,128)(2,1)} broadcast(bf16[]{:T(256)} %constant.110.clone), dimensions={} | broadcast | bytes 4194306 | tf_op jit(solution)/shard_map/broadcast.12
  167.2 4.0 %fusion.44 = f32[512,128]{0,1:T(8,128)S(1)} fusion(bf16[512,4096]{1,0:T(8,128)(2,1)} %get-tuple-element.186, bf16[128,4096]{1,0:T(8,128)(2,1)} %constant_dynamic-update-slice_fusion.2), kind=kOutput, calls=%fused_computation.84 | convolution fusion | flops 536870912 | bytes 5505024 | tf_op jit(solution)/shard_map/dot_general | solution.py:18
  171.2 0.8 collective-permute-start.14
  172.0 0.9 collective-permute-start.15
  173.0 4.3 %fusion.14 = f32[512,128]{0,1:T(8,128)S(1)} fusion(bf16[512,4096]{1,0:T(8,128)(2,1)} %get-tuple-element.186, bf16[128,4096]{1,0:T(8,128)(2,1)} %collective-permute-done.18, bf16[128,4096]{1,0:T(8,128)(2,1)} %collective-permute-done.17), kind=kOutput, calls=%fused_computation.26 | convolution fusion | flops 538968064 | bytes 6553600 | tf_op jit(solution)/shard_map/dot_general | solution.py:18
  177.3 0.8 collective-permute-start.19
  178.8 3.8 %fusion.13 = f32[512,128]{0,1:T(8,128)S(1)} fusion(bf16[512,4096]{1,0:T(8,128)(2,1)} %get-tuple-element.186, bf16[64,4096]{1,0:T(8,128)(2,1)S(1)} %copy-done.8, bf16[64,4096]{1,0:T(8,128)(2,1)} %collective-permute-done.21), kind=kOutput, calls=%fused_computation.25 | convolution fusion | flops 538968064 | bytes 5505024 | tf_op jit(solution)/shard_map/dot_general | solution.py:18
  182.7 1.3 collective-permute-start.22
  184.0 1.3 collective-permute-start.23
  185.4 45.5 %collective-permute-done.22 = f32[512,64]{0,1:T(8,128)S(1)} collective-permute-done((f32[512,64]{0,1:T(8,128)S(1)}, f32[512,64]{0,1:T(8,128)S(1)}, u32[]{:S(2)}, u32[]{:S(2)}) %collective-permute-start.22) | collective-permute-done | bytes 131104 | tf_op jit(solution)/shard_map/ppermute | solution.py:34
  230.9 4.2 %collective-permute-done.23 = f32[512,64]{0,1:T(8,128)S(1)} collective-permute-done((f32[512,64]{0,1:T(8,128)S(1)}, f32[512,64]{0,1:T(8,128)S(1)}, u32[]{:S(2)}, u32[]{:S(2)}) %collective-permute-start.23) | collective-permute-done | bytes 131104 | tf_op jit(solution)/shard_map/ppermute | solution.py:34
  235.1 1.3 fusion.22
  236.4 0.8 reshape.52
  (54 shorter events, 3.6 us)
Async XLA Ops:
  0.0 17.1 %copy-start.1 = (bf16[1,128,8192]{2,1,0:T(8,128)(2,1)S(1)}, bf16[1,128,8192]{2,1,0:T(8,128)(2,1)}, u32[]{:S(2)}) copy-start(bf16[1,128,8192]{2,1,0:T(8,128)(2,1)} %param.22) | copy-start | bytes 6291460
  0.0 17.1 %copy-start.2 = (bf16[1,4096,128]{2,1,0:T(8,128)(2,1)S(1)}, bf16[1,4096,128]{2,1,0:T(8,128)(2,1)}, u32[]{:S(2)}) copy-start(bf16[1,4096,128]{2,1,0:T(8,128)(2,1)} %param.21) | copy-start | bytes 3145732
  1.0 16.1 %copy-start.12 = (bf16[128,64]{1,0:T(8,128)(2,1)}, bf16[128,64]{1,0:T(8,128)(2,1)S(1)}, u32[]{:S(2)}) copy-start(bf16[128,64]{1,0:T(8,128)(2,1)S(1)} %slice_convert_fusion) | copy-start | bytes 49156
  3.4 10.8 %collective-permute-start.16 = (bf16[64,4096]{1,0:T(8,128)(2,1)}, bf16[64,4096]{1,0:T(8,128)(2,1)}, u32[]{:S(2)}, u32[]{:S(2)}) collective-permute-start(bf16[64,4096]{1,0:T(8,128)(2,1)} %convolution_convert_fusion), channel_id=1, source_target_pairs={{8,16},{9,17},{10,18},{11,19},{12,20},{13,21},{14,22},{15,23}} | collective-permute-start | bytes 1572872 | tf_op jit(solution)/shard_map/ppermute | solution.py:34
  4.7 9.5 %collective-permute-start.3 = (bf16[64,4096]{1,0:T(8,128)(2,1)}, bf16[64,4096]{1,0:T(8,128)(2,1)}, u32[]{:S(2)}, u32[]{:S(2)}) collective-permute-start(bf16[64,4096]{1,0:T(8,128)(2,1)} %convolution_convert_fusion), channel_id=1, source_target_pairs={{0,8},{1,9},{2,10},{3,11},{4,12},{5,13},{6,14},{7,15}} | collective-permute-start | bytes 1572872 | tf_op jit(solution)/shard_map/ppermute | solution.py:34
  7.5 6.7 %copy-start.7 = (bf16[64,4096]{1,0:T(8,128)(2,1)}, bf16[64,4096]{1,0:T(8,128)(2,1)S(1)}, u32[]{:S(2)}) copy-start(bf16[64,4096]{1,0:T(8,128)(2,1)S(1)} %fusion.28) | copy-start | bytes 1572868
  19.0 37.9 %collective-permute-start.4 = (bf16[128,1024]{1,0:T(8,128)(2,1)S(1)}, bf16[128,1024]{1,0:T(8,128)(2,1)S(1)}, u32[]{:S(2)}, u32[]{:S(2)}) collective-permute-start(bf16[128,1024]{1,0:T(8,128)(2,1)S(1)} %get-tuple-element.206), channel_id=1, source_target_pairs={{8,16},{9,17},{10,18},{11,19},{12,20},{13,21},{14,22},{15,23}} | collective-permute-start | bytes 786440 | tf_op jit(solution)/shard_map/ppermute | solution.py:34
  20.3 47.0 %copy-start.5 = (bf16[4,1,128,4096]{3,2,1,0:T(8,128)(2,1)S(1)}, bf16[4,1,128,4096]{3,2,1,0:T(8,128)(2,1)}, u32[]{:S(2)}) copy-start(bf16[4,1,128,4096]{3,2,1,0:T(8,128)(2,1)} %param.19) | copy-start | bytes 12582916
  20.3 36.5 %collective-permute-start.5 = (bf16[128,1024]{1,0:T(8,128)(2,1)S(1)}, bf16[128,1024]{1,0:T(8,128)(2,1)S(1)}, u32[]{:S(2)}, u32[]{:S(2)}) collective-permute-start(bf16[128,1024]{1,0:T(8,128)(2,1)S(1)} %get-tuple-element.207), channel_id=1, source_target_pairs={{8,17},{9,16},{10,19},{11,18},{12,21},{13,20},{14,23},{15,22}} | collective-permute-start | bytes 786440 | tf_op jit(solution)/shard_map/ppermute | solution.py:34
  26.7 135.7 %collective-permute-start.1 = (bf16[256,4096]{1,0:T(8,128)(2,1)}, bf16[256,4096]{1,0:T(8,128)(2,1)}, u32[]{:S(2)}, u32[]{:S(2)}) collective-permute-start(bf16[256,4096]{1,0:T(8,128)(2,1)} %bitcast.11), channel_id=1, source_target_pairs={{24,25},{25,24},{26,27},{27,26},{28,29},{29,28},{30,31},{31,30}} | collective-permute-start | bytes 6291464 | tf_op jit(solution)/shard_map/ppermute | solution.py:34
  28.7 135.2 %collective-permute-start.2 = (bf16[256,4096]{1,0:T(8,128)(2,1)}, bf16[256,4096]{1,0:T(8,128)(2,1)}, u32[]{:S(2)}, u32[]{:S(2)}) collective-permute-start(bf16[256,4096]{1,0:T(8,128)(2,1)} %bitcast.12), channel_id=1, source_target_pairs={{0,25},{1,24},{2,27},{3,26},{4,29},{5,28},{6,31},{7,30}} | collective-permute-start | bytes 6291464 | tf_op jit(solution)/shard_map/ppermute | solution.py:34
  57.0 12.3 %collective-permute-start.6 = (bf16[128,1024]{1,0:T(8,128)(2,1)S(1)}, bf16[128,1024]{1,0:T(8,128)(2,1)}, u32[]{:S(2)}, u32[]{:S(2)}) collective-permute-start(bf16[128,1024]{1,0:T(8,128)(2,1)S(1)} %add_convert_fusion.5), channel_id=1, source_target_pairs={{16,18},{17,19},{18,20},{19,21},{20,22},{21,23},{22,16},{23,17}} | collective-permute-start | bytes 786440 | tf_op jit(solution)/shard_map/ppermute | solution.py:34
  60.5 12.6 %collective-permute-start.7 = (bf16[128,1024]{1,0:T(8,128)(2,1)S(1)}, bf16[128,1024]{1,0:T(8,128)(2,1)}, u32[]{:S(2)}, u32[]{:S(2)}) collective-permute-start(bf16[128,1024]{1,0:T(8,128)(2,1)S(1)} %add_convert_fusion.5), channel_id=1, source_target_pairs={{16,20},{17,21},{18,22},{19,23},{20,16},{21,17},{22,18},{23,19}} | collective-permute-start | bytes 786440 | tf_op jit(solution)/shard_map/ppermute | solution.py:34
  63.6 11.0 %collective-permute-start.8 = (bf16[128,1024]{1,0:T(8,128)(2,1)S(1)}, bf16[128,1024]{1,0:T(8,128)(2,1)}, u32[]{:S(2)}, u32[]{:S(2)}) collective-permute-start(bf16[128,1024]{1,0:T(8,128)(2,1)S(1)} %add_convert_fusion.5), channel_id=1, source_target_pairs={{16,22},{17,23},{18,16},{19,17},{20,18},{21,19},{22,20},{23,21}} | collective-permute-start | bytes 786440 | tf_op jit(solution)/shard_map/ppermute | solution.py:34
  74.6 1.0 copy-start.4
  96.8 9.8 %copy-start.3 = (bf16[1,4096,128]{2,1,0:T(8,128)(2,1)S(1)}, bf16[1,4096,128]{2,1,0:T(8,128)(2,1)}, u32[]{:S(2)}) copy-start(bf16[1,4096,128]{2,1,0:T(8,128)(2,1)} %param.21) | copy-start | bytes 3145732
  98.8 36.0 %collective-permute-start.10 = (bf16[128,1024]{1,0:T(8,128)(2,1)}, bf16[128,1024]{1,0:T(8,128)(2,1)}, u32[]{:S(2)}, u32[]{:S(2)}) collective-permute-start(bf16[128,1024]{1,0:T(8,128)(2,1)} %get-tuple-element.205), channel_id=1, source_target_pairs={{16,25},{17,24},{18,27},{19,26},{20,29},{21,28},{22,31},{23,30}} | collective-permute-start | bytes 786440 | tf_op jit(solution)/shard_map/ppermute | solution.py:34
  100.8 34.0 %collective-permute-start.9 = (bf16[128,1024]{1,0:T(8,128)(2,1)}, bf16[128,1024]{1,0:T(8,128)(2,1)}, u32[]{:S(2)}, u32[]{:S(2)}) collective-permute-start(bf16[128,1024]{1,0:T(8,128)(2,1)} %get-tuple-element.204), channel_id=1, source_target_pairs={{16,24},{17,25},{18,26},{19,27},{20,28},{21,29},{22,30},{23,31}} | collective-permute-start | bytes 786440 | tf_op jit(solution)/shard_map/ppermute | solution.py:34
  134.8 13.5 %copy-start.9 = (f32[512,128]{1,0:T(8,128)S(1)}, f32[512,128]{1,0:T(8,128)}, u32[]{:S(2)}) copy-start(f32[512,128]{1,0:T(8,128)} %fusion.36) | copy-start | bytes 786436
  137.8 7.5 %collective-permute-start.11 = (bf16[128,1024]{1,0:T(8,128)(2,1)}, bf16[128,1024]{1,0:T(8,128)(2,1)S(1)}, u32[]{:S(2)}, u32[]{:S(2)}) collective-permute-start(bf16[128,1024]{1,0:T(8,128)(2,1)} %get-tuple-element.199), channel_id=1, source_target_pairs={{24,26},{25,27},{26,28},{27,29},{28,30},{29,31},{30,24},{31,25}} | collective-permute-start | bytes 786440 | tf_op jit(solution)/shard_map/ppermute | solution.py:34
  138.5 10.3 %collective-permute-start.12 = (bf16[128,1024]{1,0:T(8,128)(2,1)}, bf16[128,1024]{1,0:T(8,128)(2,1)}, u32[]{:S(2)}, u32[]{:S(2)}) collective-permute-start(bf16[128,1024]{1,0:T(8,128)(2,1)} %get-tuple-element.199), channel_id=1, source_target_pairs={{24,28},{25,29},{26,30},{27,31},{28,24},{29,25},{30,26},{31,27}} | collective-permute-start | bytes 786440 | tf_op jit(solution)/shard_map/ppermute | solution.py:34
  143.0 29.0 %collective-permute-start.17 = (bf16[128,4096]{1,0:T(8,128)(2,1)}, bf16[128,4096]{1,0:T(8,128)(2,1)}, u32[]{:S(2)}, u32[]{:S(2)}) collective-permute-start(bf16[128,4096]{1,0:T(8,128)(2,1)} %get-tuple-element.202), channel_id=1, source_target_pairs={{16,24},{17,25},{18,26},{19,27},{20,28},{21,29},{22,30},{23,31}} | collective-permute-start | bytes 3145736 | tf_op jit(solution)/shard_map/ppermute | solution.py:34
  145.3 0.7 copy-start.14
  146.0 26.9 %collective-permute-start.18 = (bf16[128,4096]{1,0:T(8,128)(2,1)}, bf16[128,4096]{1,0:T(8,128)(2,1)}, u32[]{:S(2)}, u32[]{:S(2)}) collective-permute-start(bf16[128,4096]{1,0:T(8,128)(2,1)} %get-tuple-element.203), channel_id=1, source_target_pairs={{16,25},{17,24},{18,27},{19,26},{20,29},{21,28},{22,31},{23,30}} | collective-permute-start | bytes 3145736 | tf_op jit(solution)/shard_map/ppermute | solution.py:34
  148.8 9.8 %collective-permute-start.13 = (bf16[128,1024]{1,0:T(8,128)(2,1)}, bf16[128,1024]{1,0:T(8,128)(2,1)}, u32[]{:S(2)}, u32[]{:S(2)}) collective-permute-start(bf16[128,1024]{1,0:T(8,128)(2,1)} %get-tuple-element.199), channel_id=1, source_target_pairs={{24,30},{25,31},{26,24},{27,25},{28,26},{29,27},{30,28},{31,29}} | collective-permute-start | bytes 786440 | tf_op jit(solution)/shard_map/ppermute | solution.py:34
  158.6 19.5 %collective-permute-start.21 = (bf16[64,4096]{1,0:T(8,128)(2,1)}, bf16[64,4096]{1,0:T(8,128)(2,1)}, u32[]{:S(2)}, u32[]{:S(2)}) collective-permute-start(bf16[64,4096]{1,0:T(8,128)(2,1)} %convolution_convert_fusion), channel_id=1, source_target_pairs={{16,24},{17,25},{18,26},{19,27},{20,28},{21,29},{22,30},{23,31}} | collective-permute-start | bytes 1572872 | tf_op jit(solution)/shard_map/ppermute | solution.py:34
  162.4 20.3 %collective-permute-start = (f32[512,64]{0,1:T(8,128)}, f32[512,64]{0,1:T(8,128)}, u32[]{:S(2)}, u32[]{:S(2)}) collective-permute-start(f32[512,64]{0,1:T(8,128)} %fusion.18), channel_id=1, source_target_pairs={{0,1},{1,0},{2,3},{3,2},{4,5},{5,4},{6,7},{7,6},{8,9},{9,8},{10,11... | collective-permute-start | bytes 393224 | tf_op jit(solution)/shard_map/ppermute | solution.py:253
  166.5 0.7 copy-start.10
  171.2 7.7 %copy-start.8 = (bf16[64,4096]{1,0:T(8,128)(2,1)S(1)}, bf16[64,4096]{1,0:T(8,128)(2,1)}, u32[]{:S(2)}) copy-start(bf16[64,4096]{1,0:T(8,128)(2,1)} %copy-done.7) | copy-start | bytes 1572868
  171.2 12.8 %collective-permute-start.14 = (f32[512,64]{0,1:T(8,128)S(1)}, f32[512,64]{0,1:T(8,128)S(1)}, u32[]{:S(2)}, u32[]{:S(2)}) collective-permute-start(f32[512,64]{0,1:T(8,128)S(1)} %get-tuple-element.211), channel_id=1, source_target_pairs={{24,0},{25,1},{26,2},{27,3},{28,4},{29,5},{30,6},{31,7}} | collective-permute-start | bytes 393224 | tf_op jit(solution)/shard_map/ppermute | solution.py:34
  172.0 13.4 %collective-permute-start.15 = (f32[512,64]{0,1:T(8,128)S(1)}, f32[512,64]{0,1:T(8,128)S(1)}, u32[]{:S(2)}, u32[]{:S(2)}) collective-permute-start(f32[512,64]{0,1:T(8,128)S(1)} %get-tuple-element.210), channel_id=1, source_target_pairs={{24,1},{25,0},{26,3},{27,2},{28,5},{29,4},{30,7},{31,6}} | collective-permute-start | bytes 393224 | tf_op jit(solution)/shard_map/ppermute | solution.py:34
  177.3 8.1 %copy-start.15 = (s32[4]{0:T(128)S(1)}, s32[4]{0:T(128)}, u32[]{:S(2)}) copy-start(s32[4]{0:T(128)} %param.25) | copy-start | bytes 52
  177.3 57.8 %copy-start.11 = (f32[512,128]{0,1:T(8,128)S(1)}, f32[512,128]{0,1:T(8,128)}, u32[]{:S(2)}) copy-start(f32[512,128]{0,1:T(8,128)} %copy-done.10) | copy-start | bytes 786436
  177.3 8.1 %collective-permute-start.19 = (f32[512,64]{0,1:T(8,128)S(1)}, f32[512,64]{0,1:T(8,128)S(1)}, u32[]{:S(2)}, u32[]{:S(2)}) collective-permute-start(f32[512,64]{0,1:T(8,128)S(1)} %get-tuple-element.213), channel_id=1, source_target_pairs={{24,8},{25,9},{26,10},{27,11},{28,12},{29,13},{30,14},{31,15}} | collective-permute-start | bytes 393224 | tf_op jit(solution)/shard_map/ppermute | solution.py:34
  178.2 7.3 %collective-permute-start.20 = (f32[512,64]{0,1:T(8,128)S(1)}, f32[512,64]{0,1:T(8,128)S(1)}, u32[]{:S(2)}, u32[]{:S(2)}) collective-permute-start(f32[512,64]{0,1:T(8,128)S(1)} %get-tuple-element.212), channel_id=1, source_target_pairs={{24,9},{25,8},{26,11},{27,10},{28,13},{29,12},{30,15},{31,14}} | collective-permute-start | bytes 393224 | tf_op jit(solution)/shard_map/ppermute | solution.py:34
  182.7 48.2 %collective-permute-start.22 = (f32[512,64]{0,1:T(8,128)S(1)}, f32[512,64]{0,1:T(8,128)S(1)}, u32[]{:S(2)}, u32[]{:S(2)}) collective-permute-start(f32[512,64]{0,1:T(8,128)S(1)} %get-tuple-element.215), channel_id=1, source_target_pairs={{24,16},{25,17},{26,18},{27,19},{28,20},{29,21},{30,22},{31,23}} | collective-permute-start | bytes 393224 | tf_op jit(solution)/shard_map/ppermute | solution.py:34
  184.0 51.1 %collective-permute-start.23 = (f32[512,64]{0,1:T(8,128)S(1)}, f32[512,64]{0,1:T(8,128)S(1)}, u32[]{:S(2)}, u32[]{:S(2)}) collective-permute-start(f32[512,64]{0,1:T(8,128)S(1)} %get-tuple-element.214), channel_id=1, source_target_pairs={{24,17},{25,16},{26,19},{27,18},{28,21},{29,20},{30,23},{31,22}} | collective-permute-start | bytes 393224 | tf_op jit(solution)/shard_map/ppermute | solution.py:34

commit v2 on v0

v2 whole, which is shorter than its diff:
```python
import math

import jax
import jax.numpy as jnp
from jax import lax
from jax.experimental import pallas as pl
from jax.experimental.pallas import tpu as pltpu
from jax.sharding import PartitionSpec as P

ADAPTER_SCALE = 2.0
AXES = ("pipe", "dp", "tensor")
F32 = jnp.float32
BF16 = jnp.bfloat16
SMEM, VMEM, HBM, ANY = pltpu.SMEM, pltpu.VMEM, pltpu.HBM, pl.ANY
ROWS = 16
BEST = lax.Precision.HIGHEST


def nt(left, right, precision=None):
    return lax.dot_general(
        left, right, (((1,), (1,)), ((), ())), precision=precision, preferred_element_type=F32
    )


def nn(left, right, precision=None):
    return jnp.dot(left, right, precision=precision, preferred_element_type=F32)


def placed(array, space):
    return pltpu.with_memory_space_constraint(array, HBM) if space is HBM else array


def launch(body, ins, outs, scratch=(), after=(), room=22):
    count, extra = len(ins), len(after)

    def kernel(*refs):
        body(*refs[:count], *refs[count + extra :])

    return pl.pallas_call(
        kernel,
        in_specs=[pl.BlockSpec(memory_space=space) for _, space in ins]
        + [pl.BlockSpec(memory_space=ANY)] * extra,
        out_specs=[pl.BlockSpec(memory_space=space) for _, _, space in outs],
        out_shape=[
            pltpu.HBM(shape, dtype) if space is HBM else jax.ShapeDtypeStruct(shape, dtype)
            for shape, dtype, space in outs
        ],
        scratch_shapes=list(scratch),
        compiler_params=pltpu.CompilerParams(vmem_limit_bytes=room * 2**20),
        cost_estimate=pl.CostEstimate(flops=0, bytes_accessed=0, transcendentals=0),
    )(*[placed(array, space) for array, space in ins], *after)


def shift(value, routes, to_group, by_tensor):
    groups, parts = lax.axis_size("dp"), lax.axis_size("tensor")

    def place(stage, group, part):
        return (stage * groups + group) * parts + part % parts

    pairs = [
        (place(source, g, k), place(target, to_group(g), k + by_tensor))
        for source, target in routes
        for g in range(groups)
        for k in range(parts)
    ]
    return lax.ppermute(value, AXES, pairs)


def copies(sems, *pairs):
    made = [pltpu.make_async_copy(source, target, sems.at[i]) for i, (source, target) in enumerate(pairs)]
    for copy in made:
        copy.start()
    return made


def finish(made):
    for copy in made:
        copy.wait()


def packed_at(lengths, count):
    starts = [jnp.int32(0)]
    for e in range(count):
        starts.append(starts[-1] + (lengths[e] + ROWS - 1) // ROWS * ROWS)
    return starts


def by_rows(rows, sizes, step):
    least = 0
    for size in sizes:
        pl.when((rows > least) & (rows <= size))(lambda size=size: step(size))
        least = size


def per_device(
    output_gradient,
    acts,
    weights,
    adapter_down_factors,
    adapter_up_factors,
    feature_sign_bits,
    rank_sign_bits,
    lengths,
):
    stages, groups, parts = (lax.axis_size(name) for name in AXES)
    last = stages - 1
    count, seq, local = output_gradient.shape
    tokens = count * seq
    half = tokens // 2
    width = local * parts
    rank = adapter_up_factors.shape[1]
    proj = feature_sign_bits.shape[1]
    share = 2 * proj // parts
    block = min(512, local)
    spans = groups // 2
    span = local // spans
    piece = min(512, span)
    per_span = span // piece
    weight, down, up = weights[0], adapter_down_factors[0], adapter_up_factors[0]
    bits = feature_sign_bits.T
    info = jnp.stack([lax.axis_index(name) for name in AXES]).astype(jnp.int32)

    def target_of(part, k):
        return lax.rem(part + k, parts)

    def origin_of(group, k):
        return lax.rem(lax.rem(group, spans) + spans - k, spans)

    def neighbour(k):
        return lambda g: g // spans * spans + (g + k) % spans

    def further(k):
        return lambda g: (g + k) % groups

    def same(g):
        return g

    def columns(which):
        return pl.ds(pl.multiple_of(which * local, 128), local)

    def side_of(part):
        return part // (parts // 2)

    def signs_of(values):
        return (2 * values - 1).astype(F32)

    def prepare(info, lengths, bits, low_bits, up, grad, signs, up_low, top, bottom, bits_buf, up_buf, raw, sems):
        mine = columns(info[2])
        is_last = info[0] == last
        made = copies(sems, (up.at[:, mine], up_buf), (bits.at[:, mine], bits_buf))
        loads = [pltpu.make_async_copy(grad.at[e], raw.at[e], sems.at[2 + e]) for e in range(count)]

        @pl.when(is_last)
        def _():
            for load in loads:
                load.start()

        low_left = signs_of(low_bits[...]).T[:proj, :].astype(BF16)
        made[0].wait()
        up_low[...] = nn(low_left, up_buf[...]).astype(BF16)
        made[1].wait()
        signs[...] = signs_of(bits_buf[...]).astype(BF16)

        @pl.when(is_last)
        def _():
            starts = packed_at(lengths, count)
            for e in range(count):
                loads[e].wait()
                for j in range(seq // ROWS):
                    row = starts[e] + ROWS * j
                    real = ROWS * j < lengths[e]

                    @pl.when(real & (row < half))
                    def _(e=e, j=j, row=row):
                        top[pl.ds(pl.multiple_of(row, ROWS), ROWS), :] = raw[e, ROWS * j : ROWS * (j + 1), :]

                    @pl.when(real & (row >= half))
                    def _(e=e, j=j, row=row):
                        there = pl.ds(pl.multiple_of(row - half, ROWS), ROWS)
                        bottom[there, :] = raw[e, ROWS * j : ROWS * (j + 1), :]

    near_targets, far_targets = list(range(max(1, parts // 2))), list(range(max(1, parts // 2), parts))
    ahead = 3
    far_count, near_count = len(far_targets) * per_span, len(near_targets) * per_span

    order = far_targets + near_targets

    def fetches(info, weight, buffer, sems, first, end):
        made = []
        for i in range(first, end):
            column = (
                target_of(info[2], order[i // per_span]) * local
                + lax.rem(info[1], spans) * span
                + i % per_span * piece
            )
            where = pl.ds(pl.multiple_of(column, 128), piece)
            slot = (i - first) % buffer.shape[0]
            made.append(pltpu.make_async_copy(weight.at[:, where], buffer.at[slot], sems.at[slot]))
        return made

    def lookups(info, up, up_buf, sems, targets):
        pairs = []
        for i, k in enumerate(targets):
            column = target_of(info[2], k) * local + lax.rem(info[1], spans) * span
            pairs.append((up.at[:, pl.ds(pl.multiple_of(column, 128), span)], up_buf.at[i]))
        return copies(sems, *pairs)

    def in_turn(made, use):
        for copy in made[:ahead]:
            copy.start()
        for i, copy in enumerate(made):
            copy.wait()
            if i + ahead < len(made):
                made[i + ahead].start()
            use(i)

    def first_step(info, weight, down, up, even, signs, *rest):
        outs, (held, x, low, up_buf, sems, up_sems) = rest[:parts], rest[parts:]
        stage, group = info[0], info[1]

        @pl.when(stage == 1)
        def _():
            made = fetches(info, weight, held, sems, 0, far_count + near_count)
            ready = lookups(info, up, up_buf, up_sems, order)
            x[...] = jnp.where(group < spans, even[...], signs[...])
            low[...] = (ADAPTER_SCALE * nn(x[...], down[...])).astype(BF16)

            def use(i):
                if i == 0:
                    finish(ready)
                at = pl.ds(i % per_span * piece, piece)
                total = nn(x[...], held[i % far_count]) + nn(low[...], up_buf[i // per_span, :, at])
                outs[order[i // per_span]][:, at] = total.astype(BF16)

            in_turn(made, use)

        @pl.when(stage == 2)
        def _():
            in_turn(fetches(info, weight, held, sems, 0, far_count), lambda i: None)

    wide = 3 * proj

    def step_out(i, at, total, outs):
        outs[2 * (i // per_span)][:, at] = total[:proj].astype(BF16)
        outs[2 * (i // per_span) + 1][:, at] = total[proj:].astype(BF16)

    def second_far(info, held, down, up, *rest):
        given, rest = rest[: spans * parts + 2], rest[spans * parts + 2 :]
        outs, (x, low, up_buf, up_sems) = rest[: 2 * len(far_targets)], rest[2 * len(far_targets) :]
        group = info[1]

        @pl.when(info[0] == 2)
        def _():
            ready = lookups(info, up, up_buf, up_sems, far_targets)
            for k in range(spans):
                total = given[k * parts][...].astype(F32)
                for value in given[k * parts + 1 : (k + 1) * parts]:
                    total += value[...].astype(F32)
                first = pl.multiple_of(origin_of(group, k) * span, 128)
                x[:proj, pl.ds(first, span)] = total.astype(BF16)
            x[proj : 2 * proj, :] = given[-2][...]
            x[2 * proj :, :] = given[-1][...]
            low[...] = (ADAPTER_SCALE * nn(x[...], down[...])).astype(BF16)
            finish(ready)
            for i in range(len(far_targets) * per_span):
                at = pl.ds(i % per_span * piece, piece)
                step_out(i, at, nn(x[...], held[i]) + nn(low[...], up_buf[i // per_span, :, at]), outs)

    def second_near(info, weight, up, x, low, *rest):
        outs, (w, up_buf, sems, up_sems) = rest[: 2 * len(near_targets)], rest[2 * len(near_targets) :]

        @pl.when(info[0] == 2)
        def _():
            made = fetches(info, weight, w, sems, far_count, far_count + near_count)
            ready = lookups(info, up, up_buf, up_sems, near_targets)

            def use(i):
                if i == 0:
                    finish(ready)
                at = pl.ds(i % per_span * piece, piece)
                step_out(i, at, nn(x[...], w[i]) + nn(low[...], up_buf[i // per_span, :, at]), outs)

            in_turn(made, use)

    def added(values):
        total = values[0].astype(F32)
        for value in values[1:]:
            total += value.astype(F32)
        return total.astype(BF16)

    blocks, ring = local // block, 4

    def stream(weight, ring_buf, sems, count_of, part_of, use):
        def fetch(n):
            i, k = n // count_of, n % count_of
            first = pl.multiple_of(i * block, block)
            slot = lax.rem(n, ring)
            return pltpu.make_async_copy(
                weight.at[pl.ds(first, block), columns(part_of(k))], ring_buf.at[slot], sems.at[slot]
            )

        total_steps = blocks * count_of
        for n in range(min(ring - 1, total_steps)):
            fetch(jnp.int32(n)).start()

        def step(n, _):
            fetch(n).wait()

            @pl.when(n + ring - 1 < total_steps)
            def _():
                fetch(n + ring - 1).start()

            use(n // count_of, n % count_of, lax.rem(n, ring))
            return 0

        return lambda: lax.fori_loop(0, total_steps, step, 0)

    def push_own(info, lengths, top, bottom, weight, up, signs, total, u_part, y_part, both, ring_buf, sems, ring_sems):
        part = info[2]

        @pl.when(info[0] == last)
        def _():
            rows = packed_at(lengths, count)[count]

            def use(i, k, slot):
                at = pl.ds(pl.multiple_of(i * block, block), block)
                total[:half, at] = nt(top[...], ring_buf[slot])

                def sized(size):
                    total[half : half + size, at] = nt(bottom[:size], ring_buf[slot])

                by_rows(rows - half, range(half // 4, half + 1, half // 4), sized)

            made = copies(sems, (up.at[:, columns(part)], both.at[:rank]))
            go = stream(weight, ring_buf, ring_sems, 1, lambda k: part, use)
            both[rank:, :] = signs[...]
            finish(made)
            for i, grad in enumerate((top, bottom)):
                low = nt(grad[...], both[...])
                u_part[i * half : (i + 1) * half], y_part[i * half : (i + 1) * half] = low[:, :rank], low[:, rank:]
            go()

    def push_rest(which):
        def body(info, lengths, bits, low_bits, weight, up, down, total, u_part, y_part, *rest):
            given, rest = rest[: parts - 1], rest[parts - 1 :]
            below, own, bits_buf, both, u_all, so_far, ring_buf, sems, ring_sems = rest
            part = info[2]
            mine = slice(which * half, (which + 1) * half)

            @pl.when(info[0] == last)
            def _():
                rows = packed_at(lengths, count)[count] - which * half

                def use(i, k, slot):
                    at = pl.ds(pl.multiple_of(i * block, block), block)

                    def sized(size):
                        for j in range(parts - 1):

                            @pl.when(k == j)
                            def _(j=j):
                                value = nt(given[j][:size], ring_buf[slot])
                                if j == 0:
                                    value += total[mine.start : mine.start + size, at]
                                    value += ADAPTER_SCALE * nt(u_all[:size], down[at, :])
                                else:
                                    value += so_far[:size]
                                if j == parts - 2:
                                    below[:size, at] = value.astype(BF16)
                                else:
                                    so_far[:size] = value

                    if which:
                        by_rows(rows, range(half // 4, half + 1, half // 4), sized)
                    else:
                        sized(half)

                pairs = []
                for k in range(parts - 1):
                    there = columns(target_of(part, k + 1))
                    pairs += [(up.at[:, there], both.at[k, :rank]), (bits.at[:, there], bits_buf.at[k])]
                made = copies(sems, *pairs)
                go = stream(weight, ring_buf, ring_sems, parts - 1, lambda k: lax.rem(part + k + 1, parts), use)
                finish(made)
                u_sum, y_sum = u_part[mine, :], y_part[mine, :]
                for k in range(parts - 1):
                    both[k, rank:, :] = signs_of(bits_buf[k]).astype(BF16)
                    low = nt(given[k][...], both[k])
                    u_sum += low[:, :rank]
                    y_sum += low[:, rank:]
                u_all[...] = u_sum.astype(BF16)
                low_left = signs_of(low_bits[...]).T[:proj, :].astype(BF16)
                own[:, :proj] = nt(u_all[...], low_left)
                own[:, proj:] = y_sum
                go()

        return body

    def meet(kind, sources, after=()):
        def body(info, top, bottom, *rest):
            given, rest = rest[: len(sources)], rest[len(sources) :]
            outs, (x,) = rest[:parts], rest[parts:]
            group, part = info[1], info[2]

            @pl.when(info[0] == last)
            def _():
                if kind == "here":
                    x[:proj, :], x[proj:, :] = given[0][...], given[1][...]
                elif kind == "spans":
                    for k in range(spans):
                        x[:, pl.ds(pl.multiple_of(origin_of(group, k) * span, 128), span)] = given[k][...]
                else:
                    for k in range(groups):
                        origin = lax.rem(group + groups - k, groups)
                        first = pl.multiple_of(lax.rem(origin, spans) * span, 128)
                        row = pl.multiple_of(origin // spans * proj, proj)
                        x[pl.ds(row, proj), pl.ds(first, span)] = given[k][...]
                for i, grad in enumerate((top, bottom)):
                    y = nt(grad[...], x[...])
                    for k in range(parts):
                        left = side_of(target_of(part, k)) == 0
                        outs[k][:, i * proj : (i + 1) * proj] = jnp.where(left, y[:, :proj], y[:, proj:]).astype(BF16)

        return launch(
            body,
            [(info, SMEM)] + [(v, VMEM) for v in below_grad] + [(s, VMEM) for s in sources],
            [((half, 2 * proj), BF16, VMEM)] * parts,
            [pltpu.VMEM((2 * proj, local), BF16)],
            after,
            8,
        )

    def inputs_side(info, saved, signs, down, low_bits, *rest):
        outs, (saved_buf, both, sems) = rest[:parts], rest[parts:]
        part = info[2]
        finish(copies(sems, (saved, saved_buf)))
        both[:proj, :] = nt(signs[...], saved_buf[...])
        reduced = nn(saved_buf[...], down[...])
        both[proj:, :] = nt(signs_of(low_bits[...]).T[proj:, :], reduced, BEST)
        for k in range(parts):
            first = pl.multiple_of(target_of(part, k) * share, share)
            outs[k][...] = both[pl.ds(first, share), :]

    scale = ADAPTER_SCALE / math.sqrt(seq) / math.sqrt(width) / math.sqrt(rank)

    def features(info, lengths, own_top, own_bottom, *rest):
        xs, ys, (out, y) = rest[:parts], rest[parts : (last + 1) * parts], rest[(last + 1) * parts :]
        total = ys[0][...].astype(F32)
        for value in ys[1:]:
            total += value[...].astype(F32)
        y[:half, :] = total[:, :proj]
        y[half:, :] = total[:, proj:]

        @pl.when(info[0] == last)
        def _():
            left = side_of(info[2]) == 0
            y[:half, :] = jnp.where(left, own_top[:, :proj], own_top[:, proj:])
            y[half:, :] = jnp.where(left, own_bottom[:, :proj], own_bottom[:, proj:])

        x = xs[0][...]
        for value in xs[1:]:
            x += value[...]
        starts = packed_at(lengths, count)
        for e in range(count):
            real = lengths[e]
            left = x[:, e * seq : (e + 1) * seq] * scale
            left = jnp.where(lax.broadcasted_iota(jnp.int32, left.shape, 1) < real, left, 0.0)
            right = y[pl.ds(pl.multiple_of(starts[e], ROWS), seq), :]
            right = jnp.where(lax.broadcasted_iota(jnp.int32, right.shape, 0) < real, right, 0.0)
            out[e] = nn(left, right, BEST)

    signs, up_low, *packed = launch(
        prepare,
        [(info, SMEM), (lengths, SMEM), (bits, HBM), (rank_sign_bits, VMEM), (up, HBM), (output_gradient, HBM)],
        [((proj, local), BF16, VMEM)] * 2 + [((half, local), BF16, VMEM)] * 2,
        [
            pltpu.VMEM((proj, local), jnp.int32),
            pltpu.VMEM((rank, local), BF16),
            pltpu.VMEM((count, seq, local), BF16),
            pltpu.SemaphoreType.DMA((2 + count,)),
        ],
    )
    below = [None] * stages
    for s in range(last - 2, -1, -1):
        below[s + 1] = shift(up_low, [(s, s + 1)], same, 0)
    others = [[shift(packed[i], [(last, last)], same, -k) for k in range(1, parts)] for i in (1, 0)][::-1]
    total, u_part, y_part = launch(
        push_own,
        [(info, SMEM), (lengths, SMEM)] + [(v, VMEM) for v in packed] + [(weight, HBM), (up, HBM), (signs, VMEM)],
        [((tokens, local), F32, VMEM), ((tokens, rank), F32, VMEM), ((tokens, proj), F32, VMEM)],
        [
            pltpu.VMEM((rank + proj, local), BF16),
            pltpu.VMEM((ring, block, local), BF16),
            pltpu.SemaphoreType.DMA((1,)),
            pltpu.SemaphoreType.DMA((ring,)),
        ],
    )

    def rest_of(which, after):
        return launch(
            push_rest(which),
            [(info, SMEM), (lengths, SMEM), (bits, HBM), (rank_sign_bits, VMEM)]
            + [(weight, HBM), (up, HBM), (down, VMEM), (total, VMEM), (u_part, VMEM), (y_part, VMEM)]
            + [(value, VMEM) for value in others[which]],
            [((half, local), BF16, VMEM), ((half, 2 * proj), F32, VMEM)],
            [
                pltpu.VMEM((parts - 1, proj, local), jnp.int32),
                pltpu.VMEM((parts - 1, rank + proj, local), BF16),
                pltpu.VMEM((half, rank), BF16),
                pltpu.VMEM((half, block), F32),
                pltpu.VMEM((ring, block, local), BF16),
                pltpu.SemaphoreType.DMA((2 * (parts - 1),)),
                pltpu.SemaphoreType.DMA((ring,)),
            ],
            after,
        )

    below_top, own_top = rest_of(0, [])
    *outs, held = launch(
        first_step,
        [(info, SMEM), (weight, HBM), (down, VMEM), (up, HBM), (below[1], VMEM), (signs, VMEM)],
        [((proj, span), BF16, VMEM)] * parts + [((far_count, local, piece), BF16, VMEM)],
        [
            pltpu.VMEM((proj, local), BF16),
            pltpu.VMEM((proj, rank), BF16),
            pltpu.VMEM((parts, rank, span), BF16),
            pltpu.SemaphoreType.DMA((far_count,)),
            pltpu.SemaphoreType.DMA((parts,)),
        ],
        [own_top],
        6,
    )
    arrived = [shift(v, [(1, 2)], neighbour(z), k) for z in range(spans) for k, v in enumerate(outs)]
    *far_outs, x, low = launch(
        second_far,
        [(info, SMEM), (held, VMEM), (down, VMEM), (up, HBM)]
        + [(v, VMEM) for v in arrived + [below[2], signs]],
        [((proj, span), BF16, VMEM), ((2 * proj, span), BF16, VMEM)] * len(far_targets)
        + [((wide, local), BF16, VMEM), ((wide, rank), BF16, VMEM)],
        [
            pltpu.VMEM((len(far_targets), rank, span), BF16),
            pltpu.SemaphoreType.DMA((len(far_targets),)),
        ],
        room=12,
    )
    near_outs = launch(
        second_near,
        [(info, SMEM), (weight, HBM), (up, HBM), (x, VMEM), (low, VMEM)],
        [((proj, span), BF16, VMEM), ((2 * proj, span), BF16, VMEM)] * len(near_targets),
        [
            pltpu.VMEM((near_count, local, piece), BF16),
            pltpu.VMEM((len(near_targets), rank, span), BF16),
            pltpu.SemaphoreType.DMA((near_count,)),
            pltpu.SemaphoreType.DMA((len(near_targets),)),
        ],
        [far_outs[0]],
        20,
    )
    outs = list(near_outs) + list(far_outs)
    second = [shift(v, [(2, 2)], same, k) if k else v for k, v in enumerate(outs[::2])]
    direct, _ = lax.optimization_barrier((outs[1::2], near_outs[0]))
    direct = [shift(v, [(2, 2)], same, k) if k else v for k, v in enumerate(direct)]
    reach_zero = added(second)
    direct, _ = lax.optimization_barrier((direct, reach_zero))
    reach_one = added(direct)
    reach_one = [shift(reach_one, [(2, last)], neighbour(z), 0) for z in range(spans)]
    reach_zero = [shift(reach_zero, [(2, last)], further(k), 0) for k in range(groups)]
    below_bottom, own_bottom = rest_of(1, [near_outs[0]])
    below_grad = [below_top, below_bottom]
    up_low, _ = lax.optimization_barrier((up_low, near_outs[0]))
    below[last] = shift(up_low, [(last - 1, last)], same, 0)

    y_all = []
    to_two = meet("here", [below[last], signs])
    y_all += [shift(v, [(last, 2)], same, k) for k, v in enumerate(to_two)]
    to_one = meet("spans", reach_one, [to_two[0]])
    y_all += [shift(v, [(last, 1)], same, k) for k, v in enumerate(to_one)]
    to_zero = meet("all", reach_zero, [to_one[0]])
    y_all += [shift(v, [(last, 0)], same, k) for k, v in enumerate(to_zero)]
    x_all = launch(
        inputs_side,
        [
            (info, SMEM),
            (acts[:, 0].reshape(tokens, local), HBM),
            (signs, VMEM),
            (down, VMEM),
            (rank_sign_bits, VMEM),
        ],
        [((share, tokens), F32, VMEM)] * parts,
        [
            pltpu.VMEM((tokens, local), BF16),
            pltpu.VMEM((2 * proj, tokens), F32),
            pltpu.SemaphoreType.DMA((1,)),
        ],
        [to_zero[0]],
    )
    x_all = [
        lax.ppermute(v, "tensor", [(q, (q + k) % parts) for q in range(parts)]) if k else v
        for k, v in enumerate(x_all)
    ]
    (feats,) = launch(
        features,
        [(info, SMEM), (lengths, SMEM), (own_top, VMEM), (own_bottom, VMEM)] + [(x, VMEM) for x in x_all] + [(y, VMEM) for y in y_all],
        [((count, share, proj), F32, VMEM)],
        [pltpu.VMEM((tokens, proj), F32)],
    )
    return feats.reshape(count, 1, share * proj)


def solution(mesh):
    placed = (
        P("dp", None, "tensor"),
        P("dp", "pipe", None, "tensor"),
        P("pipe", "tensor", None),
        P("pipe", "tensor", None),
        P("pipe", None, None),
        P(),
        P(),
        P("dp"),
    )
    return jax.shard_map(
        per_device, mesh=mesh, in_specs=placed, out_specs=P("dp", "pipe", "tensor"), check_vma=False
    )
```

time: 547 us -> 129 us (0.24)
  the two profiles are of different devices: /device:TPU:12 before, /device:TPU:25 now
where the time goes in v2:
time: 129 us; the launch traced here: 128 us
  waiting for transfers between devices  73.1 us (57%)
  Pallas kernels  27.2 us (21%)
  starting transfers between devices  24.1 us (19%)
  local copies, waits for them, and re-layouts  2.87 us (2%)
    ppermute x23, waiting for transfers between devices, shift(): return lax.ppermute(value, AXES, pairs)  73.1 us
    pallas_call x12, Pallas kernels, launch(): pl.pallas_call(kernel, in_specs=[pl.BlockSpec(memory_space=space) for _,...  27.2 us
    ppermute x23, starting transfers between devices, shift(): return lax.ppermute(value, AXES, pairs)  22.8 us
  transfers between devices with their start and end apart: 24, of which 3 were waited for; matrix products, arithmetic and copies ran while one was open for 0% of the time, Pallas kernels for 19%

profile of v2, /device:TPU:25, one launch (start us, length us, event | category | flops | bytes accessed | tf_op | source)
XLA Modules:
  0.0 128.0 jit_solution(657292433388314004)
XLA Ops:
  0.0 0.1 pad_add_fusion.refs_0_
  0.1 0.8 copy-done.1
  0.9 0.7 copy-done.3
  1.6 2.3 %shard_map.82 = (bf16[64,4096]{1,0:T(8,128)(2,1)S(1)}, bf16[64,4096]{1,0:T(8,128)(2,1)S(1)}, bf16[256,4096]{1,0:T(8,128)(2,1)S(1)}, bf16[256,4096]{1,0:T(8,128)(2,1)S(1)}) custom-call(s32[3]{0:T(128)S(1)} %pad_add_fusion.refs_0_, s32[4]{0:T(128)S(1)} %copy-done.3, s32[64,8192]{1,0:T(8,128)} %bitcast.20, s32[128,128]{1,0:T(8,128)S(1)} %copy-done.1, ...), custom_call_target="tpu_custom_call" | custom-call | tf_op jit(solution)/shard_map/pallas_call | solution.py:39
  3.8 0.8 collective-permute-start
  4.6 1.3 %collective-permute-start.2 = (bf16[64,4096]{1,0:T(8,128)(2,1)S(1)}, bf16[64,4096]{1,0:T(8,128)(2,1)S(1)}, u32[]{:S(2)}, u32[]{:S(2)}) collective-permute-start(bf16[64,4096]{1,0:T(8,128)(2,1)S(1)} %get-tuple-element.62), channel_id=1, source_target_pairs={{0,8},{1,9},{2,10},{3,11},{4,12},{5,13},{6,14},{7,15}} | collective-permute-start | bytes 1572872 | tf_op jit(solution)/shard_map/ppermute | solution.py:66
  5.9 3.1 %collective-permute-start.7 = (bf16[64,4096]{1,0:T(8,128)(2,1)S(1)}, bf16[64,4096]{1,0:T(8,128)(2,1)S(1)}, u32[]{:S(2)}, u32[]{:S(2)}) collective-permute-start(bf16[64,4096]{1,0:T(8,128)(2,1)S(1)} %get-tuple-element.62), channel_id=1, source_target_pairs={{8,16},{9,17},{10,18},{11,19},{12,20},{13,21},{14,22},{15,23}} | collective-permute-start | bytes 1572872 | tf_op jit(solution)/shard_map/ppermute | solution.py:66
  9.1 0.8 collective-permute-start.1
  9.9 0.0 copy-start
  9.9 0.6 shard_map.83
  10.5 0.6 copy-done
  11.1 0.6 shard_map.84
  11.7 0.0 collective-permute-done.2.refs_4_
  11.7 13.1 %shard_map.85 = (bf16[64,2048]{1,0:T(8,128)(2,1)S(1)}, bf16[64,2048]{1,0:T(8,128)(2,1)S(1)}, bf16[4,4096,512]{2,1,0:T(8,128)(2,1)S(1)}) custom-call(s32[3]{0:T(128)S(1)} %pad_add_fusion.refs_0_, bf16[4096,8192]{1,0:T(8,128)(2,1)} %bitcast.4.refs_4_.refs_1_, bf16[4096,128]{1,0:T(8,128)(2,1)S(1)} %bitcast.9, bf16[128,8192]{1,0:T(8,128)(2,1)} %bitcast.16, ...), custom_call_target="tpu_custom_call" | custom-call | tf_op jit(solution)/shard_map/pallas_call | solution.py:39
  24.9 1.3 %collective-permute-start.5 = (bf16[64,2048]{1,0:T(8,128)(2,1)S(1)}, bf16[64,2048]{1,0:T(8,128)(2,1)S(1)}, u32[]{:S(2)}, u32[]{:S(2)}) collective-permute-start(bf16[64,2048]{1,0:T(8,128)(2,1)S(1)} %get-tuple-element.47), channel_id=1, source_target_pairs={{8,18},{9,19},{10,16},{11,17},{12,22},{13,23},{14,20},{15,21}} | collective-permute-start | bytes 786440 | tf_op jit(solution)/shard_map/ppermute | solution.py:66
  26.2 1.3 %collective-permute-start.3 = (bf16[64,2048]{1,0:T(8,128)(2,1)S(1)}, bf16[64,2048]{1,0:T(8,128)(2,1)S(1)}, u32[]{:S(2)}, u32[]{:S(2)}) collective-permute-start(bf16[64,2048]{1,0:T(8,128)(2,1)S(1)} %get-tuple-element.47), channel_id=1, source_target_pairs={{8,16},{9,17},{10,18},{11,19},{12,20},{13,21},{14,22},{15,23}} | collective-permute-start | bytes 786440 | tf_op jit(solution)/shard_map/ppermute | solution.py:66
  27.5 1.3 %collective-permute-start.6 = (bf16[64,2048]{1,0:T(8,128)(2,1)S(1)}, bf16[64,2048]{1,0:T(8,128)(2,1)S(1)}, u32[]{:S(2)}, u32[]{:S(2)}) collective-permute-start(bf16[64,2048]{1,0:T(8,128)(2,1)S(1)} %get-tuple-element.48), channel_id=1, source_target_pairs={{8,19},{9,18},{10,17},{11,16},{12,23},{13,22},{14,21},{15,20}} | collective-permute-start | bytes 786440 | tf_op jit(solution)/shard_map/ppermute | solution.py:66
  28.8 0.0 collective-permute-done.7.refs_8_
  28.8 1.3 %collective-permute-start.4 = (bf16[64,2048]{1,0:T(8,128)(2,1)S(1)}, bf16[64,2048]{1,0:T(8,128)(2,1)S(1)}, u32[]{:S(2)}, u32[]{:S(2)}) collective-permute-start(bf16[64,2048]{1,0:T(8,128)(2,1)S(1)} %get-tuple-element.48), channel_id=1, source_target_pairs={{8,17},{9,16},{10,19},{11,18},{12,21},{13,20},{14,23},{15,22}} | collective-permute-start | bytes 786440 | tf_op jit(solution)/shard_map/ppermute | solution.py:66
  30.2 7.6 %collective-permute-done.3.refs_4_ = bf16[64,2048]{1,0:T(8,128)(2,1)S(1)} collective-permute-done((bf16[64,2048]{1,0:T(8,128)(2,1)S(1)}, bf16[64,2048]{1,0:T(8,128)(2,1)S(1)}, u32[]{:S(2)}, u32[]{:S(2)}) %collective-permute-start.3) | collective-permute-done | bytes 262176 | tf_op jit(solution)/shard_map/ppermute | solution.py:66
  37.8 0.0 collective-permute-done.6.refs_7_
  37.8 0.0 collective-permute-done.4.refs_5_
  37.8 0.6 shard_map.86
  38.4 0.7 collective-permute-start.8
  39.1 0.6 shard_map.87
  39.7 0.0 copy-start.2
  39.7 0.0 copy-start.4
  39.7 0.8 collective-permute-start.13
  40.5 0.7 collective-permute-start.16
  41.2 0.0 collective-permute-done.8
  41.2 0.1 add_convert_fusion.1
  41.3 0.1 add_convert_fusion
  41.5 0.7 collective-permute-start.15
  42.2 0.7 collective-permute-start.14
  42.9 0.7 collective-permute-start.12
  43.5 0.0 collective-permute-done.1.refs_10_
  43.6 0.7 collective-permute-start.11
  44.2 0.7 collective-permute-start.10
  44.9 0.0 collective-permute-done.15.refs_4_
  44.9 0.7 collective-permute-start.9
  45.6 0.8 shard_map.88
  46.5 0.6 shard_map.89
  47.0 0.0 collective-permute-done.14.refs_3_
  47.1 0.7 collective-permute-start.18
  47.7 0.6 shard_map.90
  48.3 0.0 collective-permute-done.12.refs_6_
  48.3 0.7 collective-permute-start.19
  49.0 0.0 collective-permute-done.11.refs_5_
  49.0 0.0 collective-permute-done.10.refs_4_
  49.0 0.6 shard_map.91
  49.6 5.9 %shard_map.92 = (f32[64,512]{1,0:T(8,128)S(1)}, f32[64,512]{1,0:T(8,128)S(1)}) custom-call(s32[3]{0:T(128)S(1)} %pad_add_fusion.refs_0_, bf16[512,4096]{1,0:T(8,128)(2,1)} %bitcast.23, bf16[64,4096]{1,0:T(8,128)(2,1)S(1)} %get-tuple-element.40.refs_6_.refs_5_.refs_9_.refs_4_.refs_2_, bf16[4096,128]{1,0:T(8,128)(2,1)S(1)} %bitcast.12, ...), custom_call_target="tpu_custom_call" | custom-call | tf_op jit(solution)/shard_map/pallas_call | solution.py:39
  55.5 1.3 %collective-permute-start.17 = (f32[64,512]{1,0:T(8,128)S(1)}, f32[64,512]{1,0:T(8,128)S(1)}, u32[]{:S(2)}, u32[]{:S(2)}) collective-permute-start(f32[64,512]{1,0:T(8,128)S(1)} %get-tuple-element.67), channel_id=1, source_target_pairs={{0,1},{1,0},{2,3},{3,2},{4,5},{5,4},{6,7},{7,6},{8,9},{9,8},{10,11... | collective-permute-start | bytes 393224 | tf_op jit(solution)/shard_map/ppermute | solution.py:598
  56.8 0.7 collective-permute-start.22
  57.4 0.7 collective-permute-start.23
  58.1 0.0 collective-permute-done.19.refs_7_
  58.1 1.3 %collective-permute-start.21 = (bf16[256,128]{1,0:T(8,128)(2,1)S(1)}, bf16[256,128]{1,0:T(8,128)(2,1)S(1)}, u32[]{:S(2)}, u32[]{:S(2)}) collective-permute-start(bf16[256,128]{1,0:T(8,128)(2,1)S(1)} %get-tuple-element.69), channel_id=1, source_target_pairs={{24,9},{25,8},{26,11},{27,10},{28,13},{29,12},{30,15},{31,14}} | collective-permute-start | bytes 196616 | tf_op jit(solution)/shard_map/ppermute | solution.py:66
  59.4 0.0 collective-permute-done.18.refs_6_
  59.4 1.3 %collective-permute-start.20 = (bf16[256,128]{1,0:T(8,128)(2,1)S(1)}, bf16[256,128]{1,0:T(8,128)(2,1)S(1)}, u32[]{:S(2)}, u32[]{:S(2)}) collective-permute-start(bf16[256,128]{1,0:T(8,128)(2,1)S(1)} %get-tuple-element.64.refs_7_), channel_id=1, source_target_pairs={{24,8},{25,9},{26,10},{27,11},{28,12},{29,13},{30,14},{31,15}} | collective-permute-start | bytes 196616 | tf_op jit(solution)/shard_map/ppermute | solution.py:66
  60.7 0.0 collective-permute-done.22.refs_10_
  60.7 64.8 %collective-permute-done.21.refs_9_ = bf16[256,128]{1,0:T(8,128)(2,1)S(1)} collective-permute-done((bf16[256,128]{1,0:T(8,128)(2,1)S(1)}, bf16[256,128]{1,0:T(8,128)(2,1)S(1)}, u32[]{:S(2)}, u32[]{:S(2)}) %collective-permute-start.21) | collective-permute-done | bytes 65568 | tf_op jit(solution)/shard_map/ppermute | solution.py:66
  125.5 0.7 collective-permute-done.20.refs_8_
  126.2 0.0 collective-permute-done.17.refs_5_
  126.2 1.0 shard_map.93
  127.2 0.8 reshape.4
  (10 shorter events, 0.0 us)
Async XLA Ops:
  0.1 0.8 copy-start.1
  0.9 0.7 copy-start.3
  3.8 6.7 %collective-permute-start = (bf16[256,4096]{1,0:T(8,128)(2,1)S(1)}, bf16[256,4096]{1,0:T(8,128)(2,1)S(1)}, u32[]{:S(2)}, u32[]{:S(2)}) collective-permute-start(bf16[256,4096]{1,0:T(8,128)(2,1)S(1)} %get-tuple-element.38.refs_2_), channel_id=1, source_target_pairs={{24,25},{25,24},{26,27},{27,26},{28,29},{29,28},{30,31},{31,30}} | collective-permute-start | bytes 6291464 | tf_op jit(solution)/shard_map/ppermute | solution.py:66
  4.6 7.1 %collective-permute-start.2 = (bf16[64,4096]{1,0:T(8,128)(2,1)S(1)}, bf16[64,4096]{1,0:T(8,128)(2,1)S(1)}, u32[]{:S(2)}, u32[]{:S(2)}) collective-permute-start(bf16[64,4096]{1,0:T(8,128)(2,1)S(1)} %get-tuple-element.62), channel_id=1, source_target_pairs={{0,8},{1,9},{2,10},{3,11},{4,12},{5,13},{6,14},{7,15}} | collective-permute-start | bytes 1572872 | tf_op jit(solution)/shard_map/ppermute | solution.py:66
  5.9 22.9 %collective-permute-start.7 = (bf16[64,4096]{1,0:T(8,128)(2,1)S(1)}, bf16[64,4096]{1,0:T(8,128)(2,1)S(1)}, u32[]{:S(2)}, u32[]{:S(2)}) collective-permute-start(bf16[64,4096]{1,0:T(8,128)(2,1)S(1)} %get-tuple-element.62), channel_id=1, source_target_pairs={{8,16},{9,17},{10,18},{11,19},{12,20},{13,21},{14,22},{15,23}} | collective-permute-start | bytes 1572872 | tf_op jit(solution)/shard_map/ppermute | solution.py:66
  9.1 34.5 %collective-permute-start.1 = (bf16[256,4096]{1,0:T(8,128)(2,1)S(1)}, bf16[256,4096]{1,0:T(8,128)(2,1)S(1)}, u32[]{:S(2)}, u32[]{:S(2)}) collective-permute-start(bf16[256,4096]{1,0:T(8,128)(2,1)S(1)} %get-tuple-element.39.refs_3_), channel_id=1, source_target_pairs={{24,25},{25,24},{26,27},{27,26},{28,29},{29,28},{30,31},{31,30}} | collective-permute-start | bytes 6291464 | tf_op jit(solution)/shard_map/ppermute | solution.py:66
  9.9 1.2 copy-start
  24.9 5.3 %collective-permute-start.5 = (bf16[64,2048]{1,0:T(8,128)(2,1)S(1)}, bf16[64,2048]{1,0:T(8,128)(2,1)S(1)}, u32[]{:S(2)}, u32[]{:S(2)}) collective-permute-start(bf16[64,2048]{1,0:T(8,128)(2,1)S(1)} %get-tuple-element.47), channel_id=1, source_target_pairs={{8,18},{9,19},{10,16},{11,17},{12,22},{13,23},{14,20},{15,21}} | collective-permute-start | bytes 786440 | tf_op jit(solution)/shard_map/ppermute | solution.py:66
  26.2 11.6 %collective-permute-start.3 = (bf16[64,2048]{1,0:T(8,128)(2,1)S(1)}, bf16[64,2048]{1,0:T(8,128)(2,1)S(1)}, u32[]{:S(2)}, u32[]{:S(2)}) collective-permute-start(bf16[64,2048]{1,0:T(8,128)(2,1)S(1)} %get-tuple-element.47), channel_id=1, source_target_pairs={{8,16},{9,17},{10,18},{11,19},{12,20},{13,21},{14,22},{15,23}} | collective-permute-start | bytes 786440 | tf_op jit(solution)/shard_map/ppermute | solution.py:66
  27.5 10.3 %collective-permute-start.6 = (bf16[64,2048]{1,0:T(8,128)(2,1)S(1)}, bf16[64,2048]{1,0:T(8,128)(2,1)S(1)}, u32[]{:S(2)}, u32[]{:S(2)}) collective-permute-start(bf16[64,2048]{1,0:T(8,128)(2,1)S(1)} %get-tuple-element.48), channel_id=1, source_target_pairs={{8,19},{9,18},{10,17},{11,16},{12,23},{13,22},{14,21},{15,20}} | collective-permute-start | bytes 786440 | tf_op jit(solution)/shard_map/ppermute | solution.py:66
  28.8 9.0 %collective-permute-start.4 = (bf16[64,2048]{1,0:T(8,128)(2,1)S(1)}, bf16[64,2048]{1,0:T(8,128)(2,1)S(1)}, u32[]{:S(2)}, u32[]{:S(2)}) collective-permute-start(bf16[64,2048]{1,0:T(8,128)(2,1)S(1)} %get-tuple-element.48), channel_id=1, source_target_pairs={{8,17},{9,16},{10,19},{11,18},{12,21},{13,20},{14,23},{15,22}} | collective-permute-start | bytes 786440 | tf_op jit(solution)/shard_map/ppermute | solution.py:66
  38.4 2.9 %collective-permute-start.8 = (bf16[64,2048]{1,0:T(8,128)(2,1)S(1)}, bf16[64,2048]{1,0:T(8,128)(2,1)S(1)}, u32[]{:S(2)}, u32[]{:S(2)}) collective-permute-start(bf16[64,2048]{1,0:T(8,128)(2,1)S(1)} %get-tuple-element.51.refs_5_), channel_id=1, source_target_pairs={{16,17},{17,16},{18,19},{19,18},{20,21},{21,20},{22,23},{23,22}} | collective-permute-start | bytes 786440 | tf_op jit(solution)/shard_map/ppermute | solution.py:66
  39.7 6.0 %copy-start.2 = (s32[128,128]{1,0:T(8,128)S(1)}, s32[128,128]{1,0:T(8,128)}, u32[]{:S(2)}) copy-start(s32[128,128]{1,0:T(8,128)} %refs_4_.1) | copy-start | bytes 196612
  39.7 6.0 %copy-start.4 = (s32[4]{0:T(128)S(1)}, s32[4]{0:T(128)}, u32[]{:S(2)}) copy-start(s32[4]{0:T(128)} %refs_1_.9) | copy-start | bytes 52
  39.7 1.6 %collective-permute-start.13 = (bf16[128,2048]{1,0:T(8,128)(2,1)S(1)}, bf16[128,2048]{1,0:T(8,128)(2,1)S(1)}, u32[]{:S(2)}, u32[]{:S(2)}) collective-permute-start(bf16[128,2048]{1,0:T(8,128)(2,1)S(1)} %get-tuple-element.59), channel_id=1, source_target_pairs={{16,17},{17,16},{18,19},{19,18},{20,21},{21,20},{22,23},{23,22}} | collective-permute-start | bytes 1572872 | tf_op jit(solution)/shard_map/ppermute | solution.py:66
  40.5 3.7 %collective-permute-start.16 = (bf16[64,4096]{1,0:T(8,128)(2,1)S(1)}, bf16[64,4096]{1,0:T(8,128)(2,1)S(1)}, u32[]{:S(2)}, u32[]{:S(2)}) collective-permute-start(bf16[64,4096]{1,0:T(8,128)(2,1)S(1)} %get-tuple-element.62), channel_id=1, source_target_pairs={{16,24},{17,25},{18,26},{19,27},{20,28},{21,29},{22,30},{23,31}} | collective-permute-start | bytes 1572872 | tf_op jit(solution)/shard_map/ppermute | solution.py:66
  41.5 3.5 %collective-permute-start.15 = (bf16[128,2048]{1,0:T(8,128)(2,1)S(1)}, bf16[128,2048]{1,0:T(8,128)(2,1)S(1)}, u32[]{:S(2)}, u32[]{:S(2)}) collective-permute-start(bf16[128,2048]{1,0:T(8,128)(2,1)S(1)} %add_convert_fusion), channel_id=1, source_target_pairs={{16,26},{17,27},{18,24},{19,25},{20,30},{21,31},{22,28},{23,29}} | collective-permute-start | bytes 1572872 | tf_op jit(solution)/shard_map/ppermute | solution.py:66
  42.2 4.9 %collective-permute-start.14 = (bf16[128,2048]{1,0:T(8,128)(2,1)S(1)}, bf16[128,2048]{1,0:T(8,128)(2,1)S(1)}, u32[]{:S(2)}, u32[]{:S(2)}) collective-permute-start(bf16[128,2048]{1,0:T(8,128)(2,1)S(1)} %add_convert_fusion), channel_id=1, source_target_pairs={{16,24},{17,25},{18,26},{19,27},{20,28},{21,29},{22,30},{23,31}} | collective-permute-start | bytes 1572872 | tf_op jit(solution)/shard_map/ppermute | solution.py:66
  42.9 5.4 %collective-permute-start.12 = (bf16[64,2048]{1,0:T(8,128)(2,1)S(1)}, bf16[64,2048]{1,0:T(8,128)(2,1)S(1)}, u32[]{:S(2)}, u32[]{:S(2)}) collective-permute-start(bf16[64,2048]{1,0:T(8,128)(2,1)S(1)} %add_convert_fusion.1), channel_id=1, source_target_pairs={{16,30},{17,31},{18,24},{19,25},{20,26},{21,27},{22,28},{23,29}} | collective-permute-start | bytes 786440 | tf_op jit(solution)/shard_map/ppermute | solution.py:66
  43.6 5.4 %collective-permute-start.11 = (bf16[64,2048]{1,0:T(8,128)(2,1)S(1)}, bf16[64,2048]{1,0:T(8,128)(2,1)S(1)}, u32[]{:S(2)}, u32[]{:S(2)}) collective-permute-start(bf16[64,2048]{1,0:T(8,128)(2,1)S(1)} %add_convert_fusion.1), channel_id=1, source_target_pairs={{16,28},{17,29},{18,30},{19,31},{20,24},{21,25},{22,26},{23,27}} | collective-permute-start | bytes 786440 | tf_op jit(solution)/shard_map/ppermute | solution.py:66
  44.2 4.7 %collective-permute-start.10 = (bf16[64,2048]{1,0:T(8,128)(2,1)S(1)}, bf16[64,2048]{1,0:T(8,128)(2,1)S(1)}, u32[]{:S(2)}, u32[]{:S(2)}) collective-permute-start(bf16[64,2048]{1,0:T(8,128)(2,1)S(1)} %add_convert_fusion.1), channel_id=1, source_target_pairs={{16,26},{17,27},{18,28},{19,29},{20,30},{21,31},{22,24},{23,25}} | collective-permute-start | bytes 786440 | tf_op jit(solution)/shard_map/ppermute | solution.py:66
  44.9 4.1 %collective-permute-start.9 = (bf16[64,2048]{1,0:T(8,128)(2,1)S(1)}, bf16[64,2048]{1,0:T(8,128)(2,1)S(1)}, u32[]{:S(2)}, u32[]{:S(2)}) collective-permute-start(bf16[64,2048]{1,0:T(8,128)(2,1)S(1)} %add_convert_fusion.1), channel_id=1, source_target_pairs={{16,24},{17,25},{18,26},{19,27},{20,28},{21,29},{22,30},{23,31}} | collective-permute-start | bytes 786440 | tf_op jit(solution)/shard_map/ppermute | solution.py:66
  47.1 12.4 %collective-permute-start.18 = (bf16[256,128]{1,0:T(8,128)(2,1)S(1)}, bf16[256,128]{1,0:T(8,128)(2,1)S(1)}, u32[]{:S(2)}, u32[]{:S(2)}) collective-permute-start(bf16[256,128]{1,0:T(8,128)(2,1)S(1)} %get-tuple-element.63.refs_5_), channel_id=1, source_target_pairs={{24,16},{25,17},{26,18},{27,19},{28,20},{29,21},{30,22},{31,23}} | collective-permute-start | bytes 196616 | tf_op jit(solution)/shard_map/ppermute | solution.py:66
  48.3 9.8 %collective-permute-start.19 = (bf16[256,128]{1,0:T(8,128)(2,1)S(1)}, bf16[256,128]{1,0:T(8,128)(2,1)S(1)}, u32[]{:S(2)}, u32[]{:S(2)}) collective-permute-start(bf16[256,128]{1,0:T(8,128)(2,1)S(1)} %get-tuple-element.68), channel_id=1, source_target_pairs={{24,17},{25,16},{26,19},{27,18},{28,21},{29,20},{30,23},{31,22}} | collective-permute-start | bytes 196616 | tf_op jit(solution)/shard_map/ppermute | solution.py:66
  55.5 70.7 %collective-permute-start.17 = (f32[64,512]{1,0:T(8,128)S(1)}, f32[64,512]{1,0:T(8,128)S(1)}, u32[]{:S(2)}, u32[]{:S(2)}) collective-permute-start(f32[64,512]{1,0:T(8,128)S(1)} %get-tuple-element.67), channel_id=1, source_target_pairs={{0,1},{1,0},{2,3},{3,2},{4,5},{5,4},{6,7},{7,6},{8,9},{9,8},{10,11... | collective-permute-start | bytes 393224 | tf_op jit(solution)/shard_map/ppermute | solution.py:598
  56.8 4.0 %collective-permute-start.22 = (bf16[256,128]{1,0:T(8,128)(2,1)S(1)}, bf16[256,128]{1,0:T(8,128)(2,1)S(1)}, u32[]{:S(2)}, u32[]{:S(2)}) collective-permute-start(bf16[256,128]{1,0:T(8,128)(2,1)S(1)} %get-tuple-element.65.refs_5_), channel_id=1, source_target_pairs={{24,0},{25,1},{26,2},{27,3},{28,4},{29,5},{30,6},{31,7}} | collective-permute-start | bytes 196616 | tf_op jit(solution)/shard_map/ppermute | solution.py:66
  57.4 3.3 %collective-permute-start.23 = (bf16[256,128]{1,0:T(8,128)(2,1)S(1)}, bf16[256,128]{1,0:T(8,128)(2,1)S(1)}, u32[]{:S(2)}, u32[]{:S(2)}) collective-permute-start(bf16[256,128]{1,0:T(8,128)(2,1)S(1)} %get-tuple-element.70), channel_id=1, source_target_pairs={{24,1},{25,0},{26,3},{27,2},{28,5},{29,4},{30,7},{31,6}} | collective-permute-start | bytes 196616 | tf_op jit(solution)/shard_map/ppermute | solution.py:66
  58.1 67.4 %collective-permute-start.21 = (bf16[256,128]{1,0:T(8,128)(2,1)S(1)}, bf16[256,128]{1,0:T(8,128)(2,1)S(1)}, u32[]{:S(2)}, u32[]{:S(2)}) collective-permute-start(bf16[256,128]{1,0:T(8,128)(2,1)S(1)} %get-tuple-element.69), channel_id=1, source_target_pairs={{24,9},{25,8},{26,11},{27,10},{28,13},{29,12},{30,15},{31,14}} | collective-permute-start | bytes 196616 | tf_op jit(solution)/shard_map/ppermute | solution.py:66
  59.4 66.8 %collective-permute-start.20 = (bf16[256,128]{1,0:T(8,128)(2,1)S(1)}, bf16[256,128]{1,0:T(8,128)(2,1)S(1)}, u32[]{:S(2)}, u32[]{:S(2)}) collective-permute-start(bf16[256,128]{1,0:T(8,128)(2,1)S(1)} %get-tuple-element.64.refs_7_), channel_id=1, source_target_pairs={{24,8},{25,9},{26,10},{27,11},{28,12},{29,13},{30,14},{31,15}} | collective-permute-start | bytes 196616 | tf_op jit(solution)/shard_map/ppermute | solution.py:66

commit v3 on v2

v3 whole, which is shorter than its diff:
```python
import math

import jax
import jax.numpy as jnp
from jax import lax
from jax.experimental import pallas as pl
from jax.experimental.pallas import tpu as pltpu
from jax.sharding import PartitionSpec as P

ADAPTER_SCALE = 2.0
AXES = ("pipe", "dp", "tensor")
F32 = jnp.float32
BF16 = jnp.bfloat16
SMEM, VMEM, HBM, ANY = pltpu.SMEM, pltpu.VMEM, pltpu.HBM, pl.ANY
ROWS = 16
BEST = lax.Precision.HIGHEST


def nt(left, right, precision=None):
    return lax.dot_general(
        left, right, (((1,), (1,)), ((), ())), precision=precision, preferred_element_type=F32
    )


def nn(left, right, precision=None):
    return jnp.dot(left, right, precision=precision, preferred_element_type=F32)


def placed(array, space):
    return pltpu.with_memory_space_constraint(array, HBM) if space is HBM else array


def launch(body, ins, outs, scratch=(), after=(), room=8):
    count, extra = len(ins), len(after)

    def kernel(*refs):
        body(*refs[:count], *refs[count + extra :])

    return pl.pallas_call(
        kernel,
        in_specs=[pl.BlockSpec(memory_space=space) for _, space in ins]
        + [pl.BlockSpec(memory_space=ANY)] * extra,
        out_specs=[pl.BlockSpec(memory_space=space) for _, _, space in outs],
        out_shape=[
            pltpu.HBM(shape, dtype) if space is HBM else jax.ShapeDtypeStruct(shape, dtype)
            for shape, dtype, space in outs
        ],
        scratch_shapes=list(scratch),
        compiler_params=pltpu.CompilerParams(vmem_limit_bytes=room * 2**20),
        cost_estimate=pl.CostEstimate(flops=0, bytes_accessed=0, transcendentals=0),
    )(*[placed(array, space) for array, space in ins], *after)


def shift(value, routes, to_group, by_tensor):
    groups, parts = lax.axis_size("dp"), lax.axis_size("tensor")

    def place(stage, group, part):
        return (stage * groups + group) * parts + part % parts

    pairs = [
        (place(source, g, k), place(target, to_group(g), k + by_tensor))
        for source, target in routes
        for g in range(groups)
        for k in range(parts)
    ]
    return lax.ppermute(value, AXES, pairs)


def copies(sems, *pairs):
    made = [pltpu.make_async_copy(source, target, sems.at[i]) for i, (source, target) in enumerate(pairs)]
    for copy in made:
        copy.start()
    return made


def finish(made):
    for copy in made:
        copy.wait()


def packed_at(lengths, count):
    starts = [jnp.int32(0)]
    for e in range(count):
        starts.append(starts[-1] + (lengths[e] + ROWS - 1) // ROWS * ROWS)
    return starts


def by_rows(rows, sizes, step):
    least = 0
    for size in sizes:
        pl.when((rows > least) & (rows <= size))(lambda size=size: step(size))
        least = size


def per_device(
    output_gradient,
    acts,
    weights,
    adapter_down_factors,
    adapter_up_factors,
    feature_sign_bits,
    rank_sign_bits,
    lengths,
):
    stages, groups, parts = (lax.axis_size(name) for name in AXES)
    last = stages - 1
    count, seq, local = output_gradient.shape
    tokens = count * seq
    half = tokens // 2
    width = local * parts
    rank = adapter_up_factors.shape[1]
    proj = feature_sign_bits.shape[1]
    share = 2 * proj // parts
    block = min(256, local)
    assert local % block == 0 and seq % ROWS == 0
    spans = groups // 2
    span = local // spans
    piece = min(512, span)
    per_span = span // piece
    weight, down, up = weights[0], adapter_down_factors[0], adapter_up_factors[0]
    bits = feature_sign_bits.T
    info = jnp.stack([lax.axis_index(name) for name in AXES]).astype(jnp.int32)

    def target_of(part, k):
        return lax.rem(part + k, parts)

    def origin_of(group, k):
        return lax.rem(lax.rem(group, spans) + spans - k, spans)

    def neighbour(k):
        return lambda g: g // spans * spans + (g + k) % spans

    def further(k):
        return lambda g: (g + k) % groups

    def same(g):
        return g

    def columns(which):
        return pl.ds(pl.multiple_of(which * local, 128), local)

    def side_of(part):
        return part // (parts // 2)

    def signs_of(values):
        return (2 * values - 1).astype(F32)

    def prepare(info, bits, low_bits, up, signs, up_low, low_buf, bits_buf, up_buf, sems):
        mine = columns(info[2])
        made = copies(sems, (low_bits, low_buf), (up.at[:, mine], up_buf), (bits.at[:, mine], bits_buf))
        made[0].wait()
        low_left = signs_of(low_buf[...]).T[:proj, :].astype(BF16)
        made[1].wait()
        up_low[...] = nn(low_left, up_buf[...]).astype(BF16)
        made[2].wait()
        signs[...] = signs_of(bits_buf[...]).astype(BF16)

    def pack(lengths, source, target):
        starts = packed_at(lengths, count)
        for e in range(count):
            target[pl.ds(pl.multiple_of(starts[e], ROWS), seq), :] = source[e * seq : (e + 1) * seq, :]

    near_targets, far_targets = list(range(max(1, parts // 2))), list(range(max(1, parts // 2), parts))
    slots = 3
    far_count, near_count = len(far_targets) * per_span, len(near_targets) * per_span

    order = far_targets + near_targets

    def fetches(info, weight, buffer, sems, first, end):
        made = []
        for i in range(first, end):
            column = (
                target_of(info[2], order[i // per_span]) * local
                + lax.rem(info[1], spans) * span
                + i % per_span * piece
            )
            where = pl.ds(pl.multiple_of(column, 128), piece)
            slot = (i - first) % buffer.shape[0]
            made.append(pltpu.make_async_copy(weight.at[:, where], buffer.at[slot], sems.at[slot]))
        return made

    def lookups(info, up, up_buf, sems, targets):
        pairs = []
        for i, k in enumerate(targets):
            column = target_of(info[2], k) * local + lax.rem(info[1], spans) * span
            pairs.append((up.at[:, pl.ds(pl.multiple_of(column, 128), span)], up_buf.at[i]))
        return copies(sems, *pairs)

    def in_turn(made, ahead, use):
        for copy in made[:ahead]:
            copy.start()
        for i, copy in enumerate(made):
            copy.wait()
            if i + ahead < len(made):
                made[i + ahead].start()
            use(i)

    def first_step(info, weight, down, up, even, signs, *rest):
        outs, (held, x, low, down_buf, up_buf, sems, up_sems) = rest[:parts], rest[parts:]
        stage, group = info[0], info[1]

        @pl.when(stage == 1)
        def _():
            made = fetches(info, weight, held, sems, 0, far_count + near_count)
            ready = lookups(info, up, up_buf, up_sems, order)
            down_copy = pltpu.make_async_copy(down, down_buf, up_sems.at[parts])
            down_copy.start()
            x[...] = jnp.where(group < spans, even[...], signs[...])

            def use(i):
                if i == 0:
                    down_copy.wait()
                    low[...] = (ADAPTER_SCALE * nn(x[...], down_buf[...])).astype(BF16)
                    finish(ready)
                at = pl.ds(i % per_span * piece, piece)
                total = nn(x[...], held[i % far_count]) + nn(low[...], up_buf[i // per_span, :, at])
                outs[order[i // per_span]][:, at] = total.astype(BF16)

            in_turn(made, min(slots, far_count - 1), use)

        @pl.when(stage == 2)
        def _():
            in_turn(fetches(info, weight, held, sems, 0, far_count), far_count, lambda i: None)

    wide = 3 * proj

    def second_far(info, held, down, up, *rest):
        given, rest = rest[: spans * parts + 2], rest[spans * parts + 2 :]
        outs, (x, low, down_buf, up_buf, up_sems) = rest[: len(far_targets)], rest[len(far_targets) :]
        group = info[1]

        @pl.when(info[0] == 2)
        def _():
            ready = lookups(info, up, up_buf, up_sems, far_targets)
            down_copy = pltpu.make_async_copy(down, down_buf, up_sems.at[len(far_targets)])
            down_copy.start()
            for k in range(spans):
                total = given[k * parts][...].astype(F32)
                for value in given[k * parts + 1 : (k + 1) * parts]:
                    total += value[...].astype(F32)
                first = pl.multiple_of(origin_of(group, k) * span, 128)
                x[:proj, pl.ds(first, span)] = total.astype(BF16)
            x[proj : 2 * proj, :] = given[-2][...]
            x[2 * proj :, :] = given[-1][...]
            down_copy.wait()
            low[...] = (ADAPTER_SCALE * nn(x[...], down_buf[...])).astype(BF16)
            finish(ready)
            for i in range(len(far_targets) * per_span):
                at = pl.ds(i % per_span * piece, piece)
                total = nn(x[...], held[i]) + nn(low[...], up_buf[i // per_span, :, at])
                outs[i // per_span][:, at] = total.astype(BF16)

    def second_near(info, weight, up, x, low, *rest):
        outs, (w, up_buf, sems, up_sems) = rest[: len(near_targets)], rest[len(near_targets) :]

        @pl.when(info[0] == 2)
        def _():
            made = fetches(info, weight, w, sems, far_count, far_count + near_count)
            ready = lookups(info, up, up_buf, up_sems, near_targets)

            def use(i):
                if i == 0:
                    finish(ready)
                at = pl.ds(i % per_span * piece, piece)
                total = nn(x[...], w[i % slots]) + nn(low[...], up_buf[i // per_span, :, at])
                outs[i // per_span][:, at] = total.astype(BF16)

            in_turn(made, slots - 1, use)

    def added(values):
        total = values[0].astype(F32)
        for value in values[1:]:
            total += value.astype(F32)
        return total.astype(BF16)

    blocks, ring = local // block, 5

    def stream(weight, ring_buf, sems, count_of, part_of, use):
        def fetch(n):
            i, k = n // count_of, n % count_of
            first = pl.multiple_of(i * block, block)
            slot = lax.rem(n, ring)
            return pltpu.make_async_copy(
                weight.at[pl.ds(first, block), columns(part_of(k))], ring_buf.at[slot], sems.at[slot]
            )

        total_steps = blocks * count_of
        for n in range(min(ring - 1, total_steps)):
            fetch(jnp.int32(n)).start()

        def step(n, _):
            fetch(n).wait()

            @pl.when(n + ring - 1 < total_steps)
            def _():
                fetch(n + ring - 1).start()

            use(n // count_of, n % count_of, lax.rem(n, ring))
            return 0

        return lambda: lax.fori_loop(0, total_steps, step, 0)

    sizes = range(half, tokens + 1, tokens // 8)

    sizes = range(half, tokens + 1, tokens // 8)

    def push_own(info, lengths, raw, bits, weight, up, signs, total, u_part, y_part, both_next, *rest):
        grad, bits_buf, both, ring_buf, sems, ring_sems, tile_sems = rest
        part = info[2]

        @pl.when(info[0] == last)
        def _():
            rows = packed_at(lengths, count)[count]

            def use(i, k, slot):
                at = pl.ds(pl.multiple_of(i * block, block), block)

                def sized(size):
                    total[:size, at] = nt(grad[:size], ring_buf[slot])

                by_rows(rows, sizes, sized)

            starts = packed_at(lengths, count)
            tiles = []
            for e in range(count):
                for j in range(seq // ROWS):
                    there = pl.ds(pl.multiple_of(starts[e] + ROWS * j, ROWS), ROWS)
                    here = pl.ds(e * seq + ROWS * j, ROWS)
                    copy = pltpu.make_async_copy(raw.at[here], grad.at[there], tile_sems.at[len(tiles)])
                    tiles.append((ROWS * j < lengths[e], copy))
            for real, copy in tiles:
                pl.when(real)(copy.start)
            pairs = [(up.at[:, columns(part)], both.at[:rank])]
            for k in range(parts - 1):
                there = columns(target_of(part, k + 1))
                pairs += [(up.at[:, there], both_next.at[k, :rank]), (bits.at[:, there], bits_buf.at[k])]
            made = copies(sems, *pairs)
            go = stream(weight, ring_buf, ring_sems, 1, lambda k: part, use)
            both[rank:, :] = signs[...]
            finish(made)
            for real, copy in tiles:
                pl.when(real)(copy.wait)
            for k in range(parts - 1):
                both_next[k, rank:, :] = signs_of(bits_buf[k]).astype(BF16)
            low = nt(grad[...], both[...])
            u_part[...], y_part[...] = low[:, :rank], low[:, rank:]
            go()

    def push_rest(info, lengths, low_bits, weight, down, total, u_part, y_part, both_next, *rest):
        given, rest = rest[: parts - 1], rest[parts - 1 :]
        below, own, grad, u_all, so_far, ring_buf, ring_sems = rest
        part = info[2]

        @pl.when(info[0] == last)
        def _():
            rows = packed_at(lengths, count)[count]

            def use(i, k, slot):
                at = pl.ds(pl.multiple_of(i * block, block), block)

                def sized(size):
                    for j in range(parts - 1):

                        @pl.when(k == j)
                        def _(j=j):
                            value = nt(grad[j, :size], ring_buf[slot])
                            if j == 0:
                                value += total[:size, at]
                                value += ADAPTER_SCALE * nt(u_all[:size], down[at, :])
                            else:
                                value += so_far[:size]
                            if j == parts - 2:
                                below[:size, at] = value.astype(BF16)
                            else:
                                so_far[:size] = value

                by_rows(rows, sizes, sized)

            go = stream(weight, ring_buf, ring_sems, parts - 1, lambda k: lax.rem(part + k + 1, parts), use)
            u_sum, y_sum = u_part[...], y_part[...]
            for k in range(parts - 1):
                pack(lengths, given[k], grad.at[k])
                low = nt(grad[k], both_next[k])
                u_sum += low[:, :rank]
                y_sum += low[:, rank:]
            u_all[...] = u_sum.astype(BF16)
            low_left = signs_of(low_bits[...]).T[:proj, :].astype(BF16)
            own[:, :proj] = nt(u_all[...], low_left)
            own[:, proj:] = y_sum
            go()

    def inputs_side(info, saved, signs, down, low_bits, *rest):
        outs, (saved_buf, down_buf, low_buf, both, sems) = rest[:parts], rest[parts:]
        finish(copies(sems, (saved, saved_buf), (down, down_buf), (low_bits, low_buf)))
        both[:proj, :] = nt(signs[...], saved_buf[...])
        reduced = nn(saved_buf[...], down_buf[...])
        both[proj:, :] = nt(signs_of(low_buf[...]).T[proj:, :], reduced, BEST)
        for k in range(parts):
            first = pl.multiple_of(target_of(info[2], k) * share, share)
            outs[k][...] = both[pl.ds(first, share), :]

    scale = ADAPTER_SCALE / math.sqrt(seq) / math.sqrt(width) / math.sqrt(rank)

    def features(info, lengths, own, *rest):
        xs, ys, (out, y) = rest[:parts], rest[parts : (last + 1) * parts], rest[(last + 1) * parts :]
        total = ys[0][...].astype(F32)
        for value in ys[1:]:
            total += value[...].astype(F32)
        y[:half, :] = total[:, :proj]
        y[half:, :] = total[:, proj:]

        @pl.when(info[0] == last)
        def _():
            left = side_of(info[2]) == 0
            y[...] = jnp.where(left, own[:, :proj], own[:, proj:])

        x = xs[0][...]
        for value in xs[1:]:
            x += value[...]
        starts = packed_at(lengths, count)
        for e in range(count):
            real = lengths[e]
            left = x[:, e * seq : (e + 1) * seq] * scale
            left = jnp.where(lax.broadcasted_iota(jnp.int32, left.shape, 1) < real, left, 0.0)
            right = y[pl.ds(pl.multiple_of(starts[e], ROWS), seq), :]
            right = jnp.where(lax.broadcasted_iota(jnp.int32, right.shape, 0) < real, right, 0.0)
            out[e] = nn(left, right, BEST)

    signs, up_low = launch(
        prepare,
        [(info, SMEM), (bits, HBM), (rank_sign_bits, HBM), (up, HBM)],
        [((proj, local), BF16, VMEM)] * 2,
        [
            pltpu.VMEM(rank_sign_bits.shape, jnp.int32),
            pltpu.VMEM((proj, local), jnp.int32),
            pltpu.VMEM((rank, local), BF16),
            pltpu.SemaphoreType.DMA((3,)),
        ],
        room=8,
    )
    grad = output_gradient.reshape(tokens, local)
    grad_late, _ = lax.optimization_barrier((grad, up_low))
    others = [shift(grad_late, [(last, last)], same, -k) for k in range(1, parts)]
    below = [None] + [shift(up_low, [(s, s + 1)], same, 0) for s in range(last - 1, -1, -1)][::-1]
    total, u_part, y_part, both_next = launch(
        push_own,
        [(info, SMEM), (lengths, SMEM), (grad, HBM), (bits, HBM), (weight, HBM), (up, HBM), (signs, VMEM)],
        [((tokens, local), F32, VMEM), ((tokens, rank), F32, VMEM), ((tokens, proj), F32, VMEM)]
        + [((parts - 1, rank + proj, local), BF16, VMEM)],
        [
            pltpu.VMEM((tokens, local), BF16),
            pltpu.VMEM((parts - 1, proj, local), jnp.int32),
            pltpu.VMEM((rank + proj, local), BF16),
            pltpu.VMEM((ring, block, local), BF16),
            pltpu.SemaphoreType.DMA((2 * parts,)),
            pltpu.SemaphoreType.DMA((ring,)),
            pltpu.SemaphoreType.DMA((tokens // ROWS,)),
        ],
        room=20,
    )
    *outs, held = launch(
        first_step,
        [(info, SMEM), (weight, HBM), (down, HBM), (up, HBM), (below[1], VMEM), (signs, VMEM)],
        [((proj, span), BF16, VMEM)] * parts + [((far_count, local, piece), BF16, VMEM)],
        [
            pltpu.VMEM((proj, local), BF16),
            pltpu.VMEM((proj, rank), BF16),
            pltpu.VMEM((local, rank), BF16),
            pltpu.VMEM((parts, rank, span), BF16),
            pltpu.SemaphoreType.DMA((far_count,)),
            pltpu.SemaphoreType.DMA((parts + 1,)),
        ],
        [u_part],
        9,
    )
    arrived = [shift(v, [(1, 2)], neighbour(z), k) for z in range(spans) for k, v in enumerate(outs)]
    x_all = launch(
        inputs_side,
        [
            (info, SMEM),
            (acts[:, 0].reshape(tokens, local), HBM),
            (signs, VMEM),
            (down, HBM),
            (rank_sign_bits, HBM),
        ],
        [((share, tokens), F32, VMEM)] * parts,
        [
            pltpu.VMEM((tokens, local), BF16),
            pltpu.VMEM((local, rank), BF16),
            pltpu.VMEM(rank_sign_bits.shape, jnp.int32),
            pltpu.VMEM((2 * proj, tokens), F32),
            pltpu.SemaphoreType.DMA((3,)),
        ],
        [outs[0]],
        10,
    )
    x_all = [
        lax.ppermute(v, "tensor", [(q, (q + k) % parts) for q in range(parts)]) if k else v
        for k, v in enumerate(x_all)
    ]
    *far_outs, x, low = launch(
        second_far,
        [(info, SMEM), (held, VMEM), (down, HBM), (up, HBM)]
        + [(v, VMEM) for v in arrived + [below[2], signs]],
        [((wide, span), BF16, VMEM)] * len(far_targets)
        + [((wide, local), BF16, VMEM), ((wide, rank), BF16, VMEM)],
        [
            pltpu.VMEM((local, rank), BF16),
            pltpu.VMEM((len(far_targets), rank, span), BF16),
            pltpu.SemaphoreType.DMA((len(far_targets) + 1,)),
        ],
        [x_all[0]],
        12,
    )
    near_outs = launch(
        second_near,
        [(info, SMEM), (weight, HBM), (up, HBM), (x, VMEM), (low, VMEM)],
        [((wide, span), BF16, VMEM)] * len(near_targets),
        [
            pltpu.VMEM((slots, local, piece), BF16),
            pltpu.VMEM((len(near_targets), rank, span), BF16),
            pltpu.SemaphoreType.DMA((slots,)),
            pltpu.SemaphoreType.DMA((len(near_targets),)),
        ],
        [far_outs[0]],
        17,
    )
    outs = list(near_outs) + list(far_outs)
    both_reach = added([shift(v, [(2, 2)], same, k) if k else v for k, v in enumerate(outs)])
    reach_zero, reach_one = both_reach[:proj], both_reach[proj:]
    reach_one_kept, reach_zero_kept = reach_one, reach_zero
    reach_one = [shift(reach_one, [(2, last)], neighbour(z), 0) for z in range(1, spans)]
    reach_zero = [shift(reach_zero, [(2, last)], further(k), 0) for k in range(1, groups)]
    below_grad, own = launch(
        push_rest,
        [(info, SMEM), (lengths, SMEM), (rank_sign_bits, VMEM), (weight, HBM), (down, VMEM)]
        + [(v, VMEM) for v in [total, u_part, y_part, both_next] + others],
        [((tokens, local), BF16, VMEM), ((tokens, 2 * proj), F32, VMEM)],
        [
            pltpu.VMEM((parts - 1, tokens, local), BF16),
            pltpu.VMEM((tokens, rank), BF16),
            pltpu.VMEM((tokens, block), F32),
            pltpu.VMEM((ring, block, local), BF16),
            pltpu.SemaphoreType.DMA((ring,)),
        ],
        [reach_one_kept, below[last]],
        18,
    )
    reach_one_kept, reach_zero_kept, reach_one, reach_zero, _ = lax.optimization_barrier(
        (reach_one_kept, reach_zero_kept, reach_one, reach_zero, own)
    )
    reach_zero = [shift(reach_zero_kept, [(2, last)], same, 0)] + reach_zero
    reach_one = [shift(reach_one_kept, [(2, last)], same, 0)] + reach_one

    def meet(info, grad, low_last, signs, *rest):
        ones, zeros = rest[:spans], rest[spans : spans + groups]
        outs, (x,) = rest[spans + groups : -1], rest[-1:]
        group, part = info[1], info[2]

        @pl.when(info[0] == last)
        def _():
            for k in range(groups):
                origin = lax.rem(group + groups - k, groups)
                first = pl.multiple_of(lax.rem(origin, spans) * span, 128)
                row = pl.multiple_of(origin // spans * proj, proj)
                x[pl.ds(row, proj), pl.ds(first, span)] = zeros[k][...]
            for k in range(spans):
                first = pl.multiple_of(origin_of(group, k) * span, 128)
                x[2 * proj : 4 * proj, pl.ds(first, span)] = ones[k][...]
            x[4 * proj : 5 * proj, :] = low_last[...]
            x[5 * proj :, :] = signs[...]
            y = nt(grad[...], x[...])
            for s in range(last):
                left, right = (y[:, (2 * s + i) * proj : (2 * s + i + 1) * proj] for i in range(2))
                for k in range(parts):
                    chosen = jnp.where(side_of(target_of(part, k)) == 0, left, right).astype(BF16)
                    outs[s * parts + k][:, :proj] = chosen[:half]
                    outs[s * parts + k][:, proj:] = chosen[half:]

    y_all = launch(
        meet,
        [(info, SMEM)] + [(v, VMEM) for v in [below_grad, below[last], signs] + reach_one + reach_zero],
        [((half, 2 * proj), BF16, VMEM)] * (last * parts),
        [pltpu.VMEM((2 * last * proj, local), BF16)],
        room=10,
    )
    y_all = [shift(v, [(last, i // parts)], same, i % parts) for i, v in enumerate(y_all)]
    (feats,) = launch(
        features,
        [(info, SMEM), (lengths, SMEM), (own, VMEM)] + [(x, VMEM) for x in x_all] + [(y, VMEM) for y in y_all],
        [((count, share, proj), F32, VMEM)],
        [pltpu.VMEM((tokens, proj), F32)],
        room=8,
    )
    return feats.reshape(count, 1, share * proj)


def solution(mesh):
    placed = (
        P("dp", None, "tensor"),
        P("dp", "pipe", None, "tensor"),
        P("pipe", "tensor", None),
        P("pipe", "tensor", None),
        P("pipe", None, None),
        P(),
        P(),
        P("dp"),
    )
    return jax.shard_map(
        per_device, mesh=mesh, in_specs=placed, out_specs=P("dp", "pipe", "tensor"), check_vma=False
    )
```

time: 129 us -> 101 us (0.78)
  the two profiles are of different devices: /device:TPU:25 before, /device:TPU:12 now
where the time goes in v3:
time: 101 us; the launch traced here: 99.7 us
  waiting for transfers between devices  35.2 us (35%)
  Pallas kernels  32.7 us (32%)
  starting transfers between devices  30 us (30%)
  local copies, waits for them, and re-layouts  1.04 us (1%)
    ppermute x21, waiting for transfers between devices, shift(): return lax.ppermute(value, AXES, pairs)  35 us
    pallas_call x9, Pallas kernels, launch(): pl.pallas_call(kernel, in_specs=[pl.BlockSpec(memory_space=space) for _,...  32.7 us
    ppermute x21, starting transfers between devices, shift(): return lax.ppermute(value, AXES, pairs)  28.4 us
  transfers between devices with their start and end apart: 22, of which 8 were waited for; matrix products, arithmetic and copies ran while one was open for 0% of the time, Pallas kernels for 29%

profile of v3, /device:TPU:12, one launch (start us, length us, event | category | flops | bytes accessed | tf_op | source)
XLA Modules:
  0.0 99.7 jit_solution(17603064985460207583)
XLA Ops:
  0.0 0.0 copy-start.2
  0.0 0.0 copy-start.3
  0.0 0.1 pad_add_fusion.refs_0_
  0.1 2.6 %shard_map.82 = (bf16[64,4096]{1,0:T(8,128)(2,1)S(1)}, bf16[64,4096]{1,0:T(8,128)(2,1)S(1)}) custom-call(s32[3]{0:T(128)S(1)} %pad_add_fusion.refs_0_, s32[64,8192]{1,0:T(8,128)} %bitcast.18, s32[128,128]{1,0:T(8,128)} %refs_2_.3, bf16[128,8192]{1,0:T(8,128)(2,1)} %bitcast.13), custom_call_target="tpu_custom_call" | custom-call | tf_op jit(solution)/shard_map/pallas_call | solution.py:39
  2.7 0.2 copy-done.3
  2.9 0.9 collective-permute-start
  3.8 0.7 collective-permute-start.1
  4.5 1.3 %collective-permute-start.6 = (bf16[64,4096]{1,0:T(8,128)(2,1)S(1)}, bf16[64,4096]{1,0:T(8,128)(2,1)S(1)}, u32[]{:S(2)}, u32[]{:S(2)}) collective-permute-start(bf16[64,4096]{1,0:T(8,128)(2,1)S(1)} %get-tuple-element.39), channel_id=1, source_target_pairs={{8,16},{9,17},{10,18},{11,19},{12,20},{13,21},{14,22},{15,23}} | collective-permute-start | bytes 1572872 | tf_op jit(solution)/shard_map/ppermute | solution.py:66
  5.8 0.0 copy-done.2
  5.8 0.9 shard_map.83
  6.7 0.0 collective-permute-done.1.refs_4_
  6.7 6.5 %shard_map.84 = (bf16[64,2048]{1,0:T(8,128)(2,1)S(1)}, bf16[64,2048]{1,0:T(8,128)(2,1)S(1)}, bf16[4,4096,512]{2,1,0:T(8,128)(2,1)S(1)}) custom-call(s32[3]{0:T(128)S(1)} %pad_add_fusion.refs_0_, bf16[4096,8192]{1,0:T(8,128)(2,1)} %bitcast.3.refs_4_.refs_1_.refs_3_, bf16[4096,128]{1,0:T(8,128)(2,1)} %bitcast.9, bf16[128,8192]{1,0:T(8,128)(2,1)} %bitcast.15, ...), custom_call_target="tpu_custom_call" | custom-call | tf_op jit(solution)/shard_map/pallas_call | solution.py:39
  13.3 1.3 %collective-permute-start.2 = (bf16[64,2048]{1,0:T(8,128)(2,1)S(1)}, bf16[64,2048]{1,0:T(8,128)(2,1)S(1)}, u32[]{:S(2)}, u32[]{:S(2)}) collective-permute-start(bf16[64,2048]{1,0:T(8,128)(2,1)S(1)} %get-tuple-element.42.refs_5_), channel_id=1, source_target_pairs={{8,16},{9,17},{10,18},{11,19},{12,20},{13,21},{14,22},{15,23}} | collective-permute-start | bytes 786440 | tf_op jit(solution)/shard_map/ppermute | solution.py:66
  14.6 1.3 %collective-permute-start.4 = (bf16[64,2048]{1,0:T(8,128)(2,1)S(1)}, bf16[64,2048]{1,0:T(8,128)(2,1)S(1)}, u32[]{:S(2)}, u32[]{:S(2)}) collective-permute-start(bf16[64,2048]{1,0:T(8,128)(2,1)S(1)} %get-tuple-element.42.refs_5_), channel_id=1, source_target_pairs={{8,18},{9,19},{10,16},{11,17},{12,22},{13,23},{14,20},{15,21}} | collective-permute-start | bytes 786440 | tf_op jit(solution)/shard_map/ppermute | solution.py:66
  15.9 1.3 %collective-permute-start.3 = (bf16[64,2048]{1,0:T(8,128)(2,1)S(1)}, bf16[64,2048]{1,0:T(8,128)(2,1)S(1)}, u32[]{:S(2)}, u32[]{:S(2)}) collective-permute-start(bf16[64,2048]{1,0:T(8,128)(2,1)S(1)} %get-tuple-element.43), channel_id=1, source_target_pairs={{8,17},{9,16},{10,19},{11,18},{12,21},{13,20},{14,23},{15,22}} | collective-permute-start | bytes 786440 | tf_op jit(solution)/shard_map/ppermute | solution.py:66
  17.2 0.0 collective-permute-done.6.refs_8_
  17.2 1.5 %collective-permute-start.5 = (bf16[64,2048]{1,0:T(8,128)(2,1)S(1)}, bf16[64,2048]{1,0:T(8,128)(2,1)S(1)}, u32[]{:S(2)}, u32[]{:S(2)}) collective-permute-start(bf16[64,2048]{1,0:T(8,128)(2,1)S(1)} %get-tuple-element.43), channel_id=1, source_target_pairs={{8,19},{9,18},{10,17},{11,16},{12,23},{13,22},{14,21},{15,20}} | collective-permute-start | bytes 786440 | tf_op jit(solution)/shard_map/ppermute | solution.py:66
  18.7 6.2 %shard_map.85 = (f32[64,512]{1,0:T(8,128)S(1)}, f32[64,512]{1,0:T(8,128)S(1)}) custom-call(s32[3]{0:T(128)S(1)} %pad_add_fusion.refs_0_, bf16[512,4096]{1,0:T(8,128)(2,1)} %bitcast.22, bf16[64,4096]{1,0:T(8,128)(2,1)S(1)} %get-tuple-element.34.refs_6_.refs_5_.refs_2_.refs_9_.refs_3_, bf16[4096,128]{1,0:T(8,128)(2,1)} %bitcast.10, s32[128,128]{1,0:T(8,128)} %refs_2_.3, ...), custom_call_target="tpu_custom_call" | custom-call | tf_op jit(solution)/shard_map/pallas_call | solution.py:39
  24.9 11.1 %collective-permute-done.2.refs_4_ = bf16[64,2048]{1,0:T(8,128)(2,1)S(1)} collective-permute-done((bf16[64,2048]{1,0:T(8,128)(2,1)S(1)}, bf16[64,2048]{1,0:T(8,128)(2,1)S(1)}, u32[]{:S(2)}, u32[]{:S(2)}) %collective-permute-start.2) | collective-permute-done | bytes 262176 | tf_op jit(solution)/shard_map/ppermute | solution.py:66
  36.0 0.0 collective-permute-done.3.refs_5_
  36.0 0.0 collective-permute-done.4.refs_6_
  36.0 0.0 collective-permute-done.5.refs_7_
  36.0 6.2 %shard_map.86 = (bf16[192,2048]{1,0:T(8,128)(2,1)S(1)}, bf16[192,4096]{1,0:T(8,128)(2,1)S(1)}, bf16[192,128]{1,0:T(8,128)(2,1)S(1)}) custom-call(s32[3]{0:T(128)S(1)} %pad_add_fusion.refs_0_, bf16[4,4096,512]{2,1,0:T(8,128)(2,1)S(1)} %get-tuple-element.41.refs_1_, bf16[4096,128]{1,0:T(8,128)(2,1)} %bitcast.11, bf16[128,8192]{1,0:T(8,128)(2,1)} %bitcast.16, ...), custom_call_target="tpu_custom_call" | custom-call | tf_op jit(solution)/shard_map/pallas_call | solution.py:39
  42.2 3.4 %collective-permute-start.7 = (bf16[192,2048]{1,0:T(8,128)(2,1)S(1)}, bf16[192,2048]{1,0:T(8,128)(2,1)S(1)}, u32[]{:S(2)}, u32[]{:S(2)}) collective-permute-start(bf16[192,2048]{1,0:T(8,128)(2,1)S(1)} %get-tuple-element.47.refs_5_), channel_id=1, source_target_pairs={{16,17},{17,16},{18,19},{19,18},{20,21},{21,20},{22,23},{23,22}} | collective-permute-start | bytes 2359304 | tf_op jit(solution)/shard_map/ppermute | solution.py:66
  45.6 1.3 %collective-permute-start.8 = (bf16[64,4096]{1,0:T(8,128)(2,1)S(1)}, bf16[64,4096]{1,0:T(8,128)(2,1)S(1)}, u32[]{:S(2)}, u32[]{:S(2)}) collective-permute-start(bf16[64,4096]{1,0:T(8,128)(2,1)S(1)} %get-tuple-element.39), channel_id=1, source_target_pairs={{16,24},{17,25},{18,26},{19,27},{20,28},{21,29},{22,30},{23,31}} | collective-permute-start | bytes 1572872 | tf_op jit(solution)/shard_map/ppermute | solution.py:66
  46.9 0.0 copy-start.1
  46.9 7.9 %shard_map.87 = bf16[192,2048]{1,0:T(8,128)(2,1)S(1)} custom-call(s32[3]{0:T(128)S(1)} %pad_add_fusion.refs_0_, bf16[4096,8192]{1,0:T(8,128)(2,1)} %bitcast.3.refs_4_.refs_1_.refs_3_, bf16[128,8192]{1,0:T(8,128)(2,1)} %bitcast.17, bf16[192,4096]{1,0:T(8,128)(2,1)S(1)} %get-tuple-element.45.refs_3_, bf16[192,128]{1,0:T(8,128)(2,1)S(1)} %get-tuple-element.46.refs_4_, ...), custom_call_target="tpu_custom_call" | custom-call | tf_op jit(solution)/shard_map/pallas_call | solution.py:39
  54.8 0.0 copy-start
  54.8 5.7 %collective-permute-done.7 = bf16[192,2048]{1,0:T(8,128)(2,1)S(1)} collective-permute-done((bf16[192,2048]{1,0:T(8,128)(2,1)S(1)}, bf16[192,2048]{1,0:T(8,128)(2,1)S(1)}, u32[]{:S(2)}, u32[]{:S(2)}) %collective-permute-start.7) | collective-permute-done | bytes 786464 | tf_op jit(solution)/shard_map/ppermute | solution.py:66
  60.5 0.3 add_convert_fusion
  60.9 1.3 %collective-permute-start.10 = (bf16[128,2048]{1,0:T(8,128)(2,1)S(1)}, bf16[128,2048]{1,0:T(8,128)(2,1)S(1)}, u32[]{:S(2)}, u32[]{:S(2)}) collective-permute-start(bf16[128,2048]{1,0:T(8,128)(2,1)S(1)} %slice.8.refs_10_), channel_id=1, source_target_pairs={{16,26},{17,27},{18,24},{19,25},{20,30},{21,31},{22,28},{23,29}} | collective-permute-start | bytes 1572872 | tf_op jit(solution)/shard_map/ppermute | solution.py:66
  62.2 1.3 %collective-permute-start.11 = (bf16[64,2048]{1,0:T(8,128)(2,1)S(1)}, bf16[64,2048]{1,0:T(8,128)(2,1)S(1)}, u32[]{:S(2)}, u32[]{:S(2)}) collective-permute-start(bf16[64,2048]{1,0:T(8,128)(2,1)S(1)} %slice.9), channel_id=1, source_target_pairs={{16,26},{17,27},{18,28},{19,29},{20,30},{21,31},{22,24},{23,25}} | collective-permute-start | bytes 786440 | tf_op jit(solution)/shard_map/ppermute | solution.py:66
  63.5 1.3 %collective-permute-start.12 = (bf16[64,2048]{1,0:T(8,128)(2,1)S(1)}, bf16[64,2048]{1,0:T(8,128)(2,1)S(1)}, u32[]{:S(2)}, u32[]{:S(2)}) collective-permute-start(bf16[64,2048]{1,0:T(8,128)(2,1)S(1)} %slice.9), channel_id=1, source_target_pairs={{16,28},{17,29},{18,30},{19,31},{20,24},{21,25},{22,26},{23,27}} | collective-permute-start | bytes 786440 | tf_op jit(solution)/shard_map/ppermute | solution.py:66
  64.9 0.0 collective-permute-done.8.refs_11_.refs_2_
  64.9 1.3 %collective-permute-start.13 = (bf16[64,2048]{1,0:T(8,128)(2,1)S(1)}, bf16[64,2048]{1,0:T(8,128)(2,1)S(1)}, u32[]{:S(2)}, u32[]{:S(2)}) collective-permute-start(bf16[64,2048]{1,0:T(8,128)(2,1)S(1)} %slice.9), channel_id=1, source_target_pairs={{16,30},{17,31},{18,24},{19,25},{20,26},{21,27},{22,28},{23,29}} | collective-permute-start | bytes 786440 | tf_op jit(solution)/shard_map/ppermute | solution.py:66
  66.2 0.0 collective-permute-done.refs_9_
  66.2 0.0 copy-done.1
  66.2 0.0 copy-done
  66.2 0.8 shard_map.88
  67.0 0.4 collective-permute-done.11.refs_7_
  67.4 2.9 %collective-permute-done.12.refs_8_ = bf16[64,2048]{1,0:T(8,128)(2,1)S(1)} collective-permute-done((bf16[64,2048]{1,0:T(8,128)(2,1)S(1)}, bf16[64,2048]{1,0:T(8,128)(2,1)S(1)}, u32[]{:S(2)}, u32[]{:S(2)}) %collective-permute-start.12) | collective-permute-done | bytes 262176 | tf_op jit(solution)/shard_map/ppermute | solution.py:66
  70.2 7.0 %collective-permute-done.13.refs_9_ = bf16[64,2048]{1,0:T(8,128)(2,1)S(1)} collective-permute-done((bf16[64,2048]{1,0:T(8,128)(2,1)S(1)}, bf16[64,2048]{1,0:T(8,128)(2,1)S(1)}, u32[]{:S(2)}, u32[]{:S(2)}) %collective-permute-start.13) | collective-permute-done | bytes 262176 | tf_op jit(solution)/shard_map/ppermute | solution.py:66
  77.3 0.0 collective-permute-done.10.refs_5_
  77.3 3.7 %collective-permute-start.14 = (bf16[128,2048]{1,0:T(8,128)(2,1)S(1)}, bf16[128,2048]{1,0:T(8,128)(2,1)S(1)}, u32[]{:S(2)}, u32[]{:S(2)}) collective-permute-start(bf16[128,2048]{1,0:T(8,128)(2,1)S(1)} %slice.8.refs_10_), channel_id=1, source_target_pairs={{16,24},{17,25},{18,26},{19,27},{20,28},{21,29},{22,30},{23,31}} | collective-permute-start | bytes 1572872 | tf_op jit(solution)/shard_map/ppermute | solution.py:66
  81.0 1.3 %collective-permute-start.15 = (bf16[64,2048]{1,0:T(8,128)(2,1)S(1)}, bf16[64,2048]{1,0:T(8,128)(2,1)S(1)}, u32[]{:S(2)}, u32[]{:S(2)}) collective-permute-start(bf16[64,2048]{1,0:T(8,128)(2,1)S(1)} %slice.9), channel_id=1, source_target_pairs={{16,24},{17,25},{18,26},{19,27},{20,28},{21,29},{22,30},{23,31}} | collective-permute-start | bytes 786440 | tf_op jit(solution)/shard_map/ppermute | solution.py:66
  82.3 1.6 %collective-permute-start.9 = (f32[64,512]{1,0:T(8,128)S(1)}, f32[64,512]{1,0:T(8,128)S(1)}, u32[]{:S(2)}, u32[]{:S(2)}) collective-permute-start(f32[64,512]{1,0:T(8,128)S(1)} %get-tuple-element.49), channel_id=1, source_target_pairs={{0,1},{1,0},{2,3},{3,2},{4,5},{5,4},{6,7},{7,6},{8,9},{9,8},{10,11... | collective-permute-start | bytes 393224 | tf_op jit(solution)/shard_map/ppermute | solution.py:498
  83.8 0.0 collective-permute-done.15.refs_6_
  83.8 0.0 collective-permute-done.14.refs_4_
  83.8 0.6 shard_map.89
  84.4 0.7 collective-permute-start.16
  85.1 0.7 collective-permute-start.17
  85.8 0.7 collective-permute-start.18
  86.4 0.7 collective-permute-start.19
  87.1 0.2 collective-permute-done.9.refs_4_
  87.3 1.3 %collective-permute-start.20 = (bf16[256,128]{1,0:T(8,128)(2,1)S(1)}, bf16[256,128]{1,0:T(8,128)(2,1)S(1)}, u32[]{:S(2)}, u32[]{:S(2)}) collective-permute-start(bf16[256,128]{1,0:T(8,128)(2,1)S(1)} %get-tuple-element.61), channel_id=1, source_target_pairs={{24,16},{25,17},{26,18},{27,19},{28,20},{29,21},{30,22},{31,23}} | collective-permute-start | bytes 196616 | tf_op jit(solution)/shard_map/ppermute | solution.py:66
  88.6 0.0 collective-permute-done.16.refs_5_
  88.6 1.3 %collective-permute-start.21 = (bf16[256,128]{1,0:T(8,128)(2,1)S(1)}, bf16[256,128]{1,0:T(8,128)(2,1)S(1)}, u32[]{:S(2)}, u32[]{:S(2)}) collective-permute-start(bf16[256,128]{1,0:T(8,128)(2,1)S(1)} %get-tuple-element.62), channel_id=1, source_target_pairs={{24,17},{25,16},{26,19},{27,18},{28,21},{29,20},{30,23},{31,22}} | collective-permute-start | bytes 196616 | tf_op jit(solution)/shard_map/ppermute | solution.py:66
  89.9 0.0 collective-permute-done.17.refs_6_
  89.9 0.0 collective-permute-done.18.refs_7_
  89.9 0.0 collective-permute-done.19.refs_8_
  89.9 4.4 %collective-permute-done.20.refs_9_ = bf16[256,128]{1,0:T(8,128)(2,1)S(1)} collective-permute-done((bf16[256,128]{1,0:T(8,128)(2,1)S(1)}, bf16[256,128]{1,0:T(8,128)(2,1)S(1)}, u32[]{:S(2)}, u32[]{:S(2)}) %collective-permute-start.20) | collective-permute-done | bytes 65568 | tf_op jit(solution)/shard_map/ppermute | solution.py:66
  94.3 3.6 %collective-permute-done.21.refs_10_ = bf16[256,128]{1,0:T(8,128)(2,1)S(1)} collective-permute-done((bf16[256,128]{1,0:T(8,128)(2,1)S(1)}, bf16[256,128]{1,0:T(8,128)(2,1)S(1)}, u32[]{:S(2)}, u32[]{:S(2)}) %collective-permute-start.21) | collective-permute-done | bytes 65568 | tf_op jit(solution)/shard_map/ppermute | solution.py:66
  97.9 1.0 %shard_map.90 = f32[4,64,64]{2,1,0:T(8,128)S(1)} custom-call(s32[3]{0:T(128)S(1)} %pad_add_fusion.refs_0_, s32[4]{0:T(128)S(1)} %copy-done.2, f32[512,128]{1,0:T(8,128)S(1)} %get-tuple-element.48.refs_2_, f32[64,512]{1,0:T(8,128)S(1)} %get-tuple-element.44.refs_10_.refs_3_, f32[64,512]{1,0:T(8,128)S(1)} %collective-permute-done.9.refs_4_, ...), custom_call_target="tpu_custom_call" | custom-call | tf_op jit(solution)/shard_map/pallas_call | solution.py:39
  98.9 0.8 reshape.8
  (2 shorter events, 0.1 us)
Async XLA Ops:
  0.0 5.8 %copy-start.2 = (s32[4]{0:T(128)S(1)}, s32[4]{0:T(128)}, u32[]{:S(2)}) copy-start(s32[4]{0:T(128)} %refs_1_.5) | copy-start | bytes 52
  0.0 2.9 %copy-start.3 = (bf16[4,128,4096]{2,1,0:T(8,128)(2,1)S(1)}, bf16[4,128,4096]{2,1,0:T(8,128)(2,1)}, u32[]{:S(2)}) copy-start(bf16[4,128,4096]{2,1,0:T(8,128)(2,1)} %param.8) | copy-start | bytes 12582916
  2.9 63.3 %collective-permute-start = (bf16[512,4096]{1,0:T(8,128)(2,1)S(1)}, bf16[512,4096]{1,0:T(8,128)(2,1)S(1)}, u32[]{:S(2)}, u32[]{:S(2)}) collective-permute-start(bf16[512,4096]{1,0:T(8,128)(2,1)S(1)} %bitcast.21), channel_id=1, source_target_pairs={{24,25},{25,24},{26,27},{27,26},{28,29},{29,28},{30,31},{31,30}} | collective-permute-start | bytes 12582920 | tf_op jit(solution)/shard_map/ppermute | solution.py:66
  3.8 2.9 %collective-permute-start.1 = (bf16[64,4096]{1,0:T(8,128)(2,1)S(1)}, bf16[64,4096]{1,0:T(8,128)(2,1)S(1)}, u32[]{:S(2)}, u32[]{:S(2)}) collective-permute-start(bf16[64,4096]{1,0:T(8,128)(2,1)S(1)} %get-tuple-element.39), channel_id=1, source_target_pairs={{0,8},{1,9},{2,10},{3,11},{4,12},{5,13},{6,14},{7,15}} | collective-permute-start | bytes 1572872 | tf_op jit(solution)/shard_map/ppermute | solution.py:66
  4.5 12.7 %collective-permute-start.6 = (bf16[64,4096]{1,0:T(8,128)(2,1)S(1)}, bf16[64,4096]{1,0:T(8,128)(2,1)S(1)}, u32[]{:S(2)}, u32[]{:S(2)}) collective-permute-start(bf16[64,4096]{1,0:T(8,128)(2,1)S(1)} %get-tuple-element.39), channel_id=1, source_target_pairs={{8,16},{9,17},{10,18},{11,19},{12,20},{13,21},{14,22},{15,23}} | collective-permute-start | bytes 1572872 | tf_op jit(solution)/shard_map/ppermute | solution.py:66
  13.3 22.7 %collective-permute-start.2 = (bf16[64,2048]{1,0:T(8,128)(2,1)S(1)}, bf16[64,2048]{1,0:T(8,128)(2,1)S(1)}, u32[]{:S(2)}, u32[]{:S(2)}) collective-permute-start(bf16[64,2048]{1,0:T(8,128)(2,1)S(1)} %get-tuple-element.42.refs_5_), channel_id=1, source_target_pairs={{8,16},{9,17},{10,18},{11,19},{12,20},{13,21},{14,22},{15,23}} | collective-permute-start | bytes 786440 | tf_op jit(solution)/shard_map/ppermute | solution.py:66
  14.6 21.4 %collective-permute-start.4 = (bf16[64,2048]{1,0:T(8,128)(2,1)S(1)}, bf16[64,2048]{1,0:T(8,128)(2,1)S(1)}, u32[]{:S(2)}, u32[]{:S(2)}) collective-permute-start(bf16[64,2048]{1,0:T(8,128)(2,1)S(1)} %get-tuple-element.42.refs_5_), channel_id=1, source_target_pairs={{8,18},{9,19},{10,16},{11,17},{12,22},{13,23},{14,20},{15,21}} | collective-permute-start | bytes 786440 | tf_op jit(solution)/shard_map/ppermute | solution.py:66
  15.9 20.1 %collective-permute-start.3 = (bf16[64,2048]{1,0:T(8,128)(2,1)S(1)}, bf16[64,2048]{1,0:T(8,128)(2,1)S(1)}, u32[]{:S(2)}, u32[]{:S(2)}) collective-permute-start(bf16[64,2048]{1,0:T(8,128)(2,1)S(1)} %get-tuple-element.43), channel_id=1, source_target_pairs={{8,17},{9,16},{10,19},{11,18},{12,21},{13,20},{14,23},{15,22}} | collective-permute-start | bytes 786440 | tf_op jit(solution)/shard_map/ppermute | solution.py:66
  17.2 18.8 %collective-permute-start.5 = (bf16[64,2048]{1,0:T(8,128)(2,1)S(1)}, bf16[64,2048]{1,0:T(8,128)(2,1)S(1)}, u32[]{:S(2)}, u32[]{:S(2)}) collective-permute-start(bf16[64,2048]{1,0:T(8,128)(2,1)S(1)} %get-tuple-element.43), channel_id=1, source_target_pairs={{8,19},{9,18},{10,17},{11,16},{12,23},{13,22},{14,21},{15,20}} | collective-permute-start | bytes 786440 | tf_op jit(solution)/shard_map/ppermute | solution.py:66
  42.2 18.4 %collective-permute-start.7 = (bf16[192,2048]{1,0:T(8,128)(2,1)S(1)}, bf16[192,2048]{1,0:T(8,128)(2,1)S(1)}, u32[]{:S(2)}, u32[]{:S(2)}) collective-permute-start(bf16[192,2048]{1,0:T(8,128)(2,1)S(1)} %get-tuple-element.47.refs_5_), channel_id=1, source_target_pairs={{16,17},{17,16},{18,19},{19,18},{20,21},{21,20},{22,23},{23,22}} | collective-permute-start | bytes 2359304 | tf_op jit(solution)/shard_map/ppermute | solution.py:66
  45.6 19.3 %collective-permute-start.8 = (bf16[64,4096]{1,0:T(8,128)(2,1)S(1)}, bf16[64,4096]{1,0:T(8,128)(2,1)S(1)}, u32[]{:S(2)}, u32[]{:S(2)}) collective-permute-start(bf16[64,4096]{1,0:T(8,128)(2,1)S(1)} %get-tuple-element.39), channel_id=1, source_target_pairs={{16,24},{17,25},{18,26},{19,27},{20,28},{21,29},{22,30},{23,31}} | collective-permute-start | bytes 1572872 | tf_op jit(solution)/shard_map/ppermute | solution.py:66
  46.9 19.3 %copy-start.1 = (s32[128,128]{1,0:T(8,128)S(1)}, s32[128,128]{1,0:T(8,128)}, u32[]{:S(2)}) copy-start(s32[128,128]{1,0:T(8,128)} %refs_2_.3) | copy-start | bytes 196612
  54.8 11.4 %copy-start = (bf16[1,4096,128]{2,1,0:T(8,128)(2,1)S(1)}, bf16[1,4096,128]{2,1,0:T(8,128)(2,1)}, u32[]{:S(2)}) copy-start(bf16[1,4096,128]{2,1,0:T(8,128)(2,1)} %param.11) | copy-start | bytes 3145732
  60.9 16.4 %collective-permute-start.10 = (bf16[128,2048]{1,0:T(8,128)(2,1)S(1)}, bf16[128,2048]{1,0:T(8,128)(2,1)S(1)}, u32[]{:S(2)}, u32[]{:S(2)}) collective-permute-start(bf16[128,2048]{1,0:T(8,128)(2,1)S(1)} %slice.8.refs_10_), channel_id=1, source_target_pairs={{16,26},{17,27},{18,24},{19,25},{20,30},{21,31},{22,28},{23,29}} | collective-permute-start | bytes 1572872 | tf_op jit(solution)/shard_map/ppermute | solution.py:66
  62.2 5.2 %collective-permute-start.11 = (bf16[64,2048]{1,0:T(8,128)(2,1)S(1)}, bf16[64,2048]{1,0:T(8,128)(2,1)S(1)}, u32[]{:S(2)}, u32[]{:S(2)}) collective-permute-start(bf16[64,2048]{1,0:T(8,128)(2,1)S(1)} %slice.9), channel_id=1, source_target_pairs={{16,26},{17,27},{18,28},{19,29},{20,30},{21,31},{22,24},{23,25}} | collective-permute-start | bytes 786440 | tf_op jit(solution)/shard_map/ppermute | solution.py:66
  63.5 6.7 %collective-permute-start.12 = (bf16[64,2048]{1,0:T(8,128)(2,1)S(1)}, bf16[64,2048]{1,0:T(8,128)(2,1)S(1)}, u32[]{:S(2)}, u32[]{:S(2)}) collective-permute-start(bf16[64,2048]{1,0:T(8,128)(2,1)S(1)} %slice.9), channel_id=1, source_target_pairs={{16,28},{17,29},{18,30},{19,31},{20,24},{21,25},{22,26},{23,27}} | collective-permute-start | bytes 786440 | tf_op jit(solution)/shard_map/ppermute | solution.py:66
  64.9 12.4 %collective-permute-start.13 = (bf16[64,2048]{1,0:T(8,128)(2,1)S(1)}, bf16[64,2048]{1,0:T(8,128)(2,1)S(1)}, u32[]{:S(2)}, u32[]{:S(2)}) collective-permute-start(bf16[64,2048]{1,0:T(8,128)(2,1)S(1)} %slice.9), channel_id=1, source_target_pairs={{16,30},{17,31},{18,24},{19,25},{20,26},{21,27},{22,28},{23,29}} | collective-permute-start | bytes 786440 | tf_op jit(solution)/shard_map/ppermute | solution.py:66
  77.3 6.6 %collective-permute-start.14 = (bf16[128,2048]{1,0:T(8,128)(2,1)S(1)}, bf16[128,2048]{1,0:T(8,128)(2,1)S(1)}, u32[]{:S(2)}, u32[]{:S(2)}) collective-permute-start(bf16[128,2048]{1,0:T(8,128)(2,1)S(1)} %slice.8.refs_10_), channel_id=1, source_target_pairs={{16,24},{17,25},{18,26},{19,27},{20,28},{21,29},{22,30},{23,31}} | collective-permute-start | bytes 1572872 | tf_op jit(solution)/shard_map/ppermute | solution.py:66
  81.0 2.9 %collective-permute-start.15 = (bf16[64,2048]{1,0:T(8,128)(2,1)S(1)}, bf16[64,2048]{1,0:T(8,128)(2,1)S(1)}, u32[]{:S(2)}, u32[]{:S(2)}) collective-permute-start(bf16[64,2048]{1,0:T(8,128)(2,1)S(1)} %slice.9), channel_id=1, source_target_pairs={{16,24},{17,25},{18,26},{19,27},{20,28},{21,29},{22,30},{23,31}} | collective-permute-start | bytes 786440 | tf_op jit(solution)/shard_map/ppermute | solution.py:66
  82.3 5.0 %collective-permute-start.9 = (f32[64,512]{1,0:T(8,128)S(1)}, f32[64,512]{1,0:T(8,128)S(1)}, u32[]{:S(2)}, u32[]{:S(2)}) collective-permute-start(f32[64,512]{1,0:T(8,128)S(1)} %get-tuple-element.49), channel_id=1, source_target_pairs={{0,1},{1,0},{2,3},{3,2},{4,5},{5,4},{6,7},{7,6},{8,9},{9,8},{10,11... | collective-permute-start | bytes 393224 | tf_op jit(solution)/shard_map/ppermute | solution.py:498
  84.4 4.2 %collective-permute-start.16 = (bf16[256,128]{1,0:T(8,128)(2,1)S(1)}, bf16[256,128]{1,0:T(8,128)(2,1)S(1)}, u32[]{:S(2)}, u32[]{:S(2)}) collective-permute-start(bf16[256,128]{1,0:T(8,128)(2,1)S(1)} %get-tuple-element.57), channel_id=1, source_target_pairs={{24,0},{25,1},{26,2},{27,3},{28,4},{29,5},{30,6},{31,7}} | collective-permute-start | bytes 196616 | tf_op jit(solution)/shard_map/ppermute | solution.py:66
  85.1 4.8 %collective-permute-start.17 = (bf16[256,128]{1,0:T(8,128)(2,1)S(1)}, bf16[256,128]{1,0:T(8,128)(2,1)S(1)}, u32[]{:S(2)}, u32[]{:S(2)}) collective-permute-start(bf16[256,128]{1,0:T(8,128)(2,1)S(1)} %get-tuple-element.58), channel_id=1, source_target_pairs={{24,1},{25,0},{26,3},{27,2},{28,5},{29,4},{30,7},{31,6}} | collective-permute-start | bytes 196616 | tf_op jit(solution)/shard_map/ppermute | solution.py:66
  85.8 4.2 %collective-permute-start.18 = (bf16[256,128]{1,0:T(8,128)(2,1)S(1)}, bf16[256,128]{1,0:T(8,128)(2,1)S(1)}, u32[]{:S(2)}, u32[]{:S(2)}) collective-permute-start(bf16[256,128]{1,0:T(8,128)(2,1)S(1)} %get-tuple-element.59), channel_id=1, source_target_pairs={{24,8},{25,9},{26,10},{27,11},{28,12},{29,13},{30,14},{31,15}} | collective-permute-start | bytes 196616 | tf_op jit(solution)/shard_map/ppermute | solution.py:66
  86.4 3.5 %collective-permute-start.19 = (bf16[256,128]{1,0:T(8,128)(2,1)S(1)}, bf16[256,128]{1,0:T(8,128)(2,1)S(1)}, u32[]{:S(2)}, u32[]{:S(2)}) collective-permute-start(bf16[256,128]{1,0:T(8,128)(2,1)S(1)} %get-tuple-element.60), channel_id=1, source_target_pairs={{24,9},{25,8},{26,11},{27,10},{28,13},{29,12},{30,15},{31,14}} | collective-permute-start | bytes 196616 | tf_op jit(solution)/shard_map/ppermute | solution.py:66
  87.3 7.0 %collective-permute-start.20 = (bf16[256,128]{1,0:T(8,128)(2,1)S(1)}, bf16[256,128]{1,0:T(8,128)(2,1)S(1)}, u32[]{:S(2)}, u32[]{:S(2)}) collective-permute-start(bf16[256,128]{1,0:T(8,128)(2,1)S(1)} %get-tuple-element.61), channel_id=1, source_target_pairs={{24,16},{25,17},{26,18},{27,19},{28,20},{29,21},{30,22},{31,23}} | collective-permute-start | bytes 196616 | tf_op jit(solution)/shard_map/ppermute | solution.py:66
  88.6 9.3 %collective-permute-start.21 = (bf16[256,128]{1,0:T(8,128)(2,1)S(1)}, bf16[256,128]{1,0:T(8,128)(2,1)S(1)}, u32[]{:S(2)}, u32[]{:S(2)}) collective-permute-start(bf16[256,128]{1,0:T(8,128)(2,1)S(1)} %get-tuple-element.62), channel_id=1, source_target_pairs={{24,17},{25,16},{26,19},{27,18},{28,21},{29,20},{30,23},{31,22}} | collective-permute-start | bytes 196616 | tf_op jit(solution)/shard_map/ppermute | solution.py:66

commit v4 on v3

--- a/solution.py
+++ b/solution.py
@@ -107,12 +107,13 @@
     count, seq, local = output_gradient.shape
     tokens = count * seq
     half = tokens // 2
+    near_rows = tokens - seq // 2
     width = local * parts
     rank = adapter_up_factors.shape[1]
     proj = feature_sign_bits.shape[1]
     share = 2 * proj // parts
     block = min(256, local)
-    assert local % block == 0 and seq % ROWS == 0
+    assert stages == 4 and groups == 4 and parts % 2 == 0 and local % block == 0 and seq % ROWS == 0
     spans = groups // 2
     span = local // spans
     piece = min(512, span)
@@ -130,8 +131,8 @@
     def neighbour(k):
         return lambda g: g // spans * spans + (g + k) % spans
 
-    def further(k):
-        return lambda g: (g + k) % groups
+    def across(k):
+        return lambda g: g ^ k
 
     def same(g):
         return g
@@ -145,20 +146,30 @@
     def signs_of(values):
         return (2 * values - 1).astype(F32)
 
-    def prepare(info, bits, low_bits, up, signs, up_low, low_buf, bits_buf, up_buf, sems):
+    def prepare(info, bits, low_bits, up, grad, signs, up_low, near, far, low_buf, bits_buf, up_buf, sems):
         mine = columns(info[2])
         made = copies(sems, (low_bits, low_buf), (up.at[:, mine], up_buf), (bits.at[:, mine], bits_buf))
+        near_copy = pltpu.make_async_copy(grad.at[:near_rows], near, sems.at[3])
+        far_copy = pltpu.make_async_copy(grad.at[near_rows:], far, sems.at[4])
+        pl.when(info[0] == last)(near_copy.start)
+        pl.when(info[0] == 0)(far_copy.start)
         made[0].wait()
         low_left = signs_of(low_buf[...]).T[:proj, :].astype(BF16)
         made[1].wait()
         up_low[...] = nn(low_left, up_buf[...]).astype(BF16)
         made[2].wait()
         signs[...] = signs_of(bits_buf[...]).astype(BF16)
-
-    def pack(lengths, source, target):
+        pl.when(info[0] == last)(near_copy.wait)
+        pl.when(info[0] == 0)(far_copy.wait)
+
+    def pack(lengths, near, far, target):
         starts = packed_at(lengths, count)
         for e in range(count):
-            target[pl.ds(pl.multiple_of(starts[e], ROWS), seq), :] = source[e * seq : (e + 1) * seq, :]
+            first, end = e * seq, (e + 1) * seq
+            for source, begin, low, high in ((near, 0, first, min(end, near_rows)), (far, near_rows, max(first, near_rows), end)):
+                if low < high:
+                    there = pl.ds(pl.multiple_of(starts[e] + (low - first), ROWS), high - low)
+                    target[there, :] = source[low - begin : high - begin, :]
 
     near_targets, far_targets = list(range(max(1, parts // 2))), list(range(max(1, parts // 2), parts))
     slots = 3
@@ -300,9 +311,9 @@
 
         return lambda: lax.fori_loop(0, total_steps, step, 0)
 
-    sizes = range(half, tokens + 1, tokens // 8)
-
-    sizes = range(half, tokens + 1, tokens // 8)
+    sizes = range(half, tokens + 1, tokens // 16)
+
+    sizes = range(half, tokens + 1, tokens // 16)
 
     def push_own(info, lengths, raw, bits, weight, up, signs, total, u_part, y_part, both_next, *rest):
         grad, bits_buf, both, ring_buf, sems, ring_sems, tile_sems = rest
@@ -347,7 +358,7 @@
             go()
 
     def push_rest(info, lengths, low_bits, weight, down, total, u_part, y_part, both_next, *rest):
-        given, rest = rest[: parts - 1], rest[parts - 1 :]
+        given, rest = rest[: 2 * (parts - 1)], rest[2 * (parts - 1) :]
         below, own, grad, u_all, so_far, ring_buf, ring_sems = rest
         part = info[2]
 
@@ -379,7 +390,7 @@
             go = stream(weight, ring_buf, ring_sems, parts - 1, lambda k: lax.rem(part + k + 1, parts), use)
             u_sum, y_sum = u_part[...], y_part[...]
             for k in range(parts - 1):
-                pack(lengths, given[k], grad.at[k])
+                pack(lengths, given[2 * k], given[2 * k + 1], grad.at[k])
                 low = nt(grad[k], both_next[k])
                 u_sum += low[:, :rank]
                 y_sum += low[:, rank:]
@@ -390,11 +401,18 @@
             go()
 
     def inputs_side(info, saved, signs, down, low_bits, *rest):
-        outs, (saved_buf, down_buf, low_buf, both, sems) = rest[:parts], rest[parts:]
-        finish(copies(sems, (saved, saved_buf), (down, down_buf), (low_bits, low_buf)))
-        both[:proj, :] = nt(signs[...], saved_buf[...])
-        reduced = nn(saved_buf[...], down_buf[...])
-        both[proj:, :] = nt(signs_of(low_buf[...]).T[proj:, :], reduced, BEST)
+        outs, (saved_buf, down_buf, low_buf, right, both, sems) = rest[:parts], rest[parts:]
+        made = copies(sems, (low_bits, low_buf), (down, down_buf), (saved, saved_buf))
+        right[:proj, :] = signs[...]
+        finish(made[:2])
+        turned = nt(signs_of(low_buf[...]).T[proj:, :].astype(BF16), down_buf[...])
+        rounded = turned.astype(BF16)
+        right[proj : 2 * proj, :] = rounded
+        right[2 * proj :, :] = (turned - rounded.astype(F32)).astype(BF16)
+        made[2].wait()
+        total = nt(right[...], saved_buf[...])
+        both[:proj, :] = total[:proj]
+        both[proj:, :] = total[proj : 2 * proj] + total[2 * proj :]
         for k in range(parts):
             first = pl.multiple_of(target_of(info[2], k) * share, share)
             outs[k][...] = both[pl.ds(first, share), :]
@@ -426,22 +444,24 @@
             right = jnp.where(lax.broadcasted_iota(jnp.int32, right.shape, 0) < real, right, 0.0)
             out[e] = nn(left, right, BEST)
 
-    signs, up_low = launch(
+    grad = output_gradient.reshape(tokens, local)
+    signs, up_low, near, far = launch(
         prepare,
-        [(info, SMEM), (bits, HBM), (rank_sign_bits, HBM), (up, HBM)],
-        [((proj, local), BF16, VMEM)] * 2,
+        [(info, SMEM), (bits, HBM), (rank_sign_bits, HBM), (up, HBM), (grad, HBM)],
+        [((proj, local), BF16, VMEM)] * 2
+        + [((near_rows, local), BF16, VMEM), ((tokens - near_rows, local), BF16, VMEM)],
         [
             pltpu.VMEM(rank_sign_bits.shape, jnp.int32),
             pltpu.VMEM((proj, local), jnp.int32),
             pltpu.VMEM((rank, local), BF16),
-            pltpu.SemaphoreType.DMA((3,)),
+            pltpu.SemaphoreType.DMA((5,)),
         ],
         room=8,
     )
-    grad = output_gradient.reshape(tokens, local)
-    grad_late, _ = lax.optimization_barrier((grad, up_low))
-    others = [shift(grad_late, [(last, last)], same, -k) for k in range(1, parts)]
     below = [None] + [shift(up_low, [(s, s + 1)], same, 0) for s in range(last - 1, -1, -1)][::-1]
+    far, _ = lax.optimization_barrier((far, below[1]))
+    fars = [shift(far, [(0, last)], same, -k) for k in range(1, parts)]
+    nears = [shift(near, [(last, last)], same, -k) for k in range(1, parts)]
     total, u_part, y_part, both_next = launch(
         push_own,
         [(info, SMEM), (lengths, SMEM), (grad, HBM), (bits, HBM), (weight, HBM), (up, HBM), (signs, VMEM)],
@@ -456,6 +476,7 @@
             pltpu.SemaphoreType.DMA((ring,)),
             pltpu.SemaphoreType.DMA((tokens // ROWS,)),
         ],
+        [below[1]],
         room=20,
     )
     *outs, held = launch(
@@ -470,7 +491,7 @@
             pltpu.SemaphoreType.DMA((far_count,)),
             pltpu.SemaphoreType.DMA((parts + 1,)),
         ],
-        [u_part],
+        [u_part] + fars,
         9,
     )
     arrived = [shift(v, [(1, 2)], neighbour(z), k) for z in range(spans) for k, v in enumerate(outs)]
@@ -488,11 +509,12 @@
             pltpu.VMEM((tokens, local), BF16),
             pltpu.VMEM((local, rank), BF16),
             pltpu.VMEM(rank_sign_bits.shape, jnp.int32),
+            pltpu.VMEM((3 * proj, local), BF16),
             pltpu.VMEM((2 * proj, tokens), F32),
             pltpu.SemaphoreType.DMA((3,)),
         ],
         [outs[0]],
-        10,
+        12,
     )
     x_all = [
         lax.ppermute(v, "tensor", [(q, (q + k) % parts) for q in range(parts)]) if k else v
@@ -527,14 +549,13 @@
     )
     outs = list(near_outs) + list(far_outs)
     both_reach = added([shift(v, [(2, 2)], same, k) if k else v for k, v in enumerate(outs)])
-    reach_zero, reach_one = both_reach[:proj], both_reach[proj:]
-    reach_one_kept, reach_zero_kept = reach_one, reach_zero
-    reach_one = [shift(reach_one, [(2, last)], neighbour(z), 0) for z in range(1, spans)]
-    reach_zero = [shift(reach_zero, [(2, last)], further(k), 0) for k in range(1, groups)]
+    turns = list(range(2, groups)) + [1, 0]
+    reach = [shift(both_reach[:proj] if k >= spans else both_reach, [(2, last)], across(k), 0) for k in range(groups)]
     below_grad, own = launch(
         push_rest,
         [(info, SMEM), (lengths, SMEM), (rank_sign_bits, VMEM), (weight, HBM), (down, VMEM)]
-        + [(v, VMEM) for v in [total, u_part, y_part, both_next] + others],
+        + [(v, VMEM) for v in [total, u_part, y_part, both_next]]
+        + [(v, VMEM) for pair in zip(nears, fars) for v in pair],
         [((tokens, local), BF16, VMEM), ((tokens, 2 * proj), F32, VMEM)],
         [
             pltpu.VMEM((parts - 1, tokens, local), BF16),
@@ -543,30 +564,22 @@
             pltpu.VMEM((ring, block, local), BF16),
             pltpu.SemaphoreType.DMA((ring,)),
         ],
-        [reach_one_kept, below[last]],
+        [both_reach, below[last]],
         18,
     )
-    reach_one_kept, reach_zero_kept, reach_one, reach_zero, _ = lax.optimization_barrier(
-        (reach_one_kept, reach_zero_kept, reach_one, reach_zero, own)
-    )
-    reach_zero = [shift(reach_zero_kept, [(2, last)], same, 0)] + reach_zero
-    reach_one = [shift(reach_one_kept, [(2, last)], same, 0)] + reach_one
 
     def meet(info, grad, low_last, signs, *rest):
-        ones, zeros = rest[:spans], rest[spans : spans + groups]
-        outs, (x,) = rest[spans + groups : -1], rest[-1:]
+        given, outs, (x,) = dict(zip(turns, rest)), rest[groups:-1], rest[-1:]
         group, part = info[1], info[2]
 
         @pl.when(info[0] == last)
         def _():
             for k in range(groups):
-                origin = lax.rem(group + groups - k, groups)
-                first = pl.multiple_of(lax.rem(origin, spans) * span, 128)
-                row = pl.multiple_of(origin // spans * proj, proj)
-                x[pl.ds(row, proj), pl.ds(first, span)] = zeros[k][...]
-            for k in range(spans):
-                first = pl.multiple_of(origin_of(group, k) * span, 128)
-                x[2 * proj : 4 * proj, pl.ds(first, span)] = ones[k][...]
+                origin = group ^ k
+                there = pl.ds(pl.multiple_of(lax.rem(origin, spans) * span, 128), span)
+                x[pl.ds(pl.multiple_of(origin // spans * proj, proj), proj), there] = given[k][:proj, :]
+                if k < spans:
+                    x[2 * proj : 4 * proj, there] = given[k][proj:, :]
             x[4 * proj : 5 * proj, :] = low_last[...]
             x[5 * proj :, :] = signs[...]
             y = nt(grad[...], x[...])
@@ -579,7 +592,7 @@
 
     y_all = launch(
         meet,
-        [(info, SMEM)] + [(v, VMEM) for v in [below_grad, below[last], signs] + reach_one + reach_zero],
+        [(info, SMEM)] + [(v, VMEM) for v in [below_grad, below[last], signs] + [reach[k] for k in turns]],
         [((half, 2 * proj), BF16, VMEM)] * (last * parts),
         [pltpu.VMEM((2 * last * proj, local), BF16)],
         room=10,

time: 101 us -> 95.7 us (0.948)
  starting transfers between devices: 30 us -> 22.6 us
  waiting for transfers between devices: 35.2 us -> 40.1 us
  Pallas kernels: 32.7 us -> 31 us
    ppermute x21 -> x20, starting transfers between devices: 28.4 us -> 22.5 us  [shift(): return lax.ppermute(value, AXES, pairs)]
    ppermute x21 -> x20, waiting for transfers between devices: 35 us -> 40.1 us  [shift(): return lax.ppermute(value, AXES, pairs)]
    pallas_call x9, Pallas kernels: 32.7 us -> 31 us  [launch(): pl.pallas_call(kernel, in_specs=[pl.BlockSpec(memory_space=space) for _,...]
    ppermute x1, starting transfers between devices: 1.56 us -> 0.08 us  [per_device(): lax.ppermute(v, 'tensor', [(q, (q + k) % parts) for q in range(parts)])]
  transfers between devices with their start and end apart: 22 -> 21, of which waited for: 8 -> 10; matrix products, arithmetic and copies ran while one was open for 0% -> 0% of each run, Pallas kernels for 29% -> 29%
where the time goes in v4:
time: 95.7 us; the launch traced here: 95.2 us
  waiting for transfers between devices  40.1 us (42%)
  Pallas kernels  31 us (32%)
  starting transfers between devices  22.6 us (24%)
    ppermute x20, waiting for transfers between devices, shift(): return lax.ppermute(value, AXES, pairs)  40.1 us
    pallas_call x9, Pallas kernels, launch(): pl.pallas_call(kernel, in_specs=[pl.BlockSpec(memory_space=space) for _,...  31 us
    ppermute x20, starting transfers between devices, shift(): return lax.ppermute(value, AXES, pairs)  22.5 us
  transfers between devices with their start and end apart: 21, of which 10 were waited for; matrix products, arithmetic and copies ran while one was open for 0% of the time, Pallas kernels for 29%

profile of v4, /device:TPU:12, one launch (start us, length us, event | category | flops | bytes accessed | tf_op | source)
XLA Modules:
  0.0 95.2 jit_solution(16811620231014020223)
XLA Ops:
  0.0 0.1 pad_add_fusion.refs_0_
  0.1 0.0 copy-start.2
  0.1 2.3 %shard_map.82 = (bf16[64,4096]{1,0:T(8,128)(2,1)S(1)}, bf16[64,4096]{1,0:T(8,128)(2,1)S(1)}, bf16[448,4096]{1,0:T(8,128)(2,1)S(1)}, bf16[64,4096]{1,0:T(8,128)(2,1)S(1)}) custom-call(s32[3]{0:T(128)S(1)} %pad_add_fusion.refs_0_, s32[64,8192]{1,0:T(8,128)} %bitcast.20, s32[128,128]{1,0:T(8,128)} %refs_2_.3, bf16[128,8192]{1,0:T(8,128)(2,1)} %bitcast.13, ...), custom_call_target="tpu_custom_call" | custom-call | tf_op jit(solution)/shard_map/pallas_call | solution.py:39
  2.4 0.9 collective-permute-start.1
  3.3 0.7 collective-permute-start
  4.0 0.0 collective-permute-done.refs_7_.refs_4_
  4.0 0.7 collective-permute-start.2
  4.7 1.3 %collective-permute-start.7 = (bf16[64,4096]{1,0:T(8,128)(2,1)S(1)}, bf16[64,4096]{1,0:T(8,128)(2,1)S(1)}, u32[]{:S(2)}, u32[]{:S(2)}) collective-permute-start(bf16[64,4096]{1,0:T(8,128)(2,1)S(1)} %get-tuple-element.31), channel_id=1, source_target_pairs={{8,16},{9,17},{10,18},{11,19},{12,20},{13,21},{14,22},{15,23}} | collective-permute-start | bytes 1572872 | tf_op jit(solution)/shard_map/ppermute | solution.py:66
  6.0 0.0 copy-done.2
  6.0 0.9 shard_map.83
  6.9 0.0 collective-permute-done.2.refs_7_.refs_10_
  6.9 6.7 %shard_map.84 = (bf16[64,2048]{1,0:T(8,128)(2,1)S(1)}, bf16[64,2048]{1,0:T(8,128)(2,1)S(1)}, bf16[4,4096,512]{2,1,0:T(8,128)(2,1)S(1)}) custom-call(s32[3]{0:T(128)S(1)} %pad_add_fusion.refs_0_, bf16[4096,8192]{1,0:T(8,128)(2,1)} %bitcast.3.refs_4_.refs_1_.refs_3_, bf16[4096,128]{1,0:T(8,128)(2,1)} %bitcast.9, bf16[128,8192]{1,0:T(8,128)(2,1)} %bitcast.15, ...), custom_call_target="tpu_custom_call" | custom-call | tf_op jit(solution)/shard_map/pallas_call | solution.py:39
  13.7 1.3 %collective-permute-start.6 = (bf16[64,2048]{1,0:T(8,128)(2,1)S(1)}, bf16[64,2048]{1,0:T(8,128)(2,1)S(1)}, u32[]{:S(2)}, u32[]{:S(2)}) collective-permute-start(bf16[64,2048]{1,0:T(8,128)(2,1)S(1)} %get-tuple-element.41), channel_id=1, source_target_pairs={{8,19},{9,18},{10,17},{11,16},{12,23},{13,22},{14,21},{15,20}} | collective-permute-start | bytes 786440 | tf_op jit(solution)/shard_map/ppermute | solution.py:66
  15.0 1.3 %collective-permute-start.4 = (bf16[64,2048]{1,0:T(8,128)(2,1)S(1)}, bf16[64,2048]{1,0:T(8,128)(2,1)S(1)}, u32[]{:S(2)}, u32[]{:S(2)}) collective-permute-start(bf16[64,2048]{1,0:T(8,128)(2,1)S(1)} %get-tuple-element.41), channel_id=1, source_target_pairs={{8,17},{9,16},{10,19},{11,18},{12,21},{13,20},{14,23},{15,22}} | collective-permute-start | bytes 786440 | tf_op jit(solution)/shard_map/ppermute | solution.py:66
  16.3 1.3 %collective-permute-start.5 = (bf16[64,2048]{1,0:T(8,128)(2,1)S(1)}, bf16[64,2048]{1,0:T(8,128)(2,1)S(1)}, u32[]{:S(2)}, u32[]{:S(2)}) collective-permute-start(bf16[64,2048]{1,0:T(8,128)(2,1)S(1)} %get-tuple-element.40.refs_5_), channel_id=1, source_target_pairs={{8,18},{9,19},{10,16},{11,17},{12,22},{13,23},{14,20},{15,21}} | collective-permute-start | bytes 786440 | tf_op jit(solution)/shard_map/ppermute | solution.py:66
  17.6 3.9 %collective-permute-done.7.refs_8_ = bf16[64,4096]{1,0:T(8,128)(2,1)S(1)} collective-permute-done((bf16[64,4096]{1,0:T(8,128)(2,1)S(1)}, bf16[64,4096]{1,0:T(8,128)(2,1)S(1)}, u32[]{:S(2)}, u32[]{:S(2)}) %collective-permute-start.7) | collective-permute-done | bytes 524320 | tf_op jit(solution)/shard_map/ppermute | solution.py:66
  21.5 1.3 %collective-permute-start.3 = (bf16[64,2048]{1,0:T(8,128)(2,1)S(1)}, bf16[64,2048]{1,0:T(8,128)(2,1)S(1)}, u32[]{:S(2)}, u32[]{:S(2)}) collective-permute-start(bf16[64,2048]{1,0:T(8,128)(2,1)S(1)} %get-tuple-element.40.refs_5_), channel_id=1, source_target_pairs={{8,16},{9,17},{10,18},{11,19},{12,20},{13,21},{14,22},{15,23}} | collective-permute-start | bytes 786440 | tf_op jit(solution)/shard_map/ppermute | solution.py:66
  22.8 4.7 %shard_map.85 = (f32[64,512]{1,0:T(8,128)S(1)}, f32[64,512]{1,0:T(8,128)S(1)}) custom-call(s32[3]{0:T(128)S(1)} %pad_add_fusion.refs_0_, bf16[512,4096]{1,0:T(8,128)(2,1)} %bitcast.22, bf16[64,4096]{1,0:T(8,128)(2,1)S(1)} %get-tuple-element.30.refs_6_.refs_5_.refs_2_.refs_9_.refs_3_, bf16[4096,128]{1,0:T(8,128)(2,1)} %bitcast.10, s32[128,128]{1,0:T(8,128)} %refs_2_.3, ...), custom_call_target="tpu_custom_call" | custom-call | tf_op jit(solution)/shard_map/pallas_call | solution.py:39
  27.4 3.6 %collective-permute-done.6.refs_7_ = bf16[64,2048]{1,0:T(8,128)(2,1)S(1)} collective-permute-done((bf16[64,2048]{1,0:T(8,128)(2,1)S(1)}, bf16[64,2048]{1,0:T(8,128)(2,1)S(1)}, u32[]{:S(2)}, u32[]{:S(2)}) %collective-permute-start.6) | collective-permute-done | bytes 262176 | tf_op jit(solution)/shard_map/ppermute | solution.py:66
  31.1 4.5 %collective-permute-done.4.refs_5_ = bf16[64,2048]{1,0:T(8,128)(2,1)S(1)} collective-permute-done((bf16[64,2048]{1,0:T(8,128)(2,1)S(1)}, bf16[64,2048]{1,0:T(8,128)(2,1)S(1)}, u32[]{:S(2)}, u32[]{:S(2)}) %collective-permute-start.4) | collective-permute-done | bytes 262176 | tf_op jit(solution)/shard_map/ppermute | solution.py:66
  35.6 0.0 collective-permute-done.5.refs_6_
  35.6 2.2 %collective-permute-done.3.refs_4_ = bf16[64,2048]{1,0:T(8,128)(2,1)S(1)} collective-permute-done((bf16[64,2048]{1,0:T(8,128)(2,1)S(1)}, bf16[64,2048]{1,0:T(8,128)(2,1)S(1)}, u32[]{:S(2)}, u32[]{:S(2)}) %collective-permute-start.3) | collective-permute-done | bytes 262176 | tf_op jit(solution)/shard_map/ppermute | solution.py:66
  37.8 6.2 %shard_map.86 = (bf16[192,2048]{1,0:T(8,128)(2,1)S(1)}, bf16[192,4096]{1,0:T(8,128)(2,1)S(1)}, bf16[192,128]{1,0:T(8,128)(2,1)S(1)}) custom-call(s32[3]{0:T(128)S(1)} %pad_add_fusion.refs_0_, bf16[4,4096,512]{2,1,0:T(8,128)(2,1)S(1)} %get-tuple-element.39.refs_1_, bf16[4096,128]{1,0:T(8,128)(2,1)} %bitcast.11, bf16[128,8192]{1,0:T(8,128)(2,1)} %bitcast.16, ...), custom_call_target="tpu_custom_call" | custom-call | tf_op jit(solution)/shard_map/pallas_call | solution.py:39
  44.0 1.9 %collective-permute-start.8 = (bf16[192,2048]{1,0:T(8,128)(2,1)S(1)}, bf16[192,2048]{1,0:T(8,128)(2,1)S(1)}, u32[]{:S(2)}, u32[]{:S(2)}) collective-permute-start(bf16[192,2048]{1,0:T(8,128)(2,1)S(1)} %get-tuple-element.45.refs_5_), channel_id=1, source_target_pairs={{16,17},{17,16},{18,19},{19,18},{20,21},{21,20},{22,23},{23,22}} | collective-permute-start | bytes 2359304 | tf_op jit(solution)/shard_map/ppermute | solution.py:66
  45.9 1.3 %collective-permute-start.9 = (bf16[64,4096]{1,0:T(8,128)(2,1)S(1)}, bf16[64,4096]{1,0:T(8,128)(2,1)S(1)}, u32[]{:S(2)}, u32[]{:S(2)}) collective-permute-start(bf16[64,4096]{1,0:T(8,128)(2,1)S(1)} %get-tuple-element.31), channel_id=1, source_target_pairs={{16,24},{17,25},{18,26},{19,27},{20,28},{21,29},{22,30},{23,31}} | collective-permute-start | bytes 1572872 | tf_op jit(solution)/shard_map/ppermute | solution.py:66
  47.3 0.0 copy-start
  47.3 0.0 copy-start.1
  47.3 7.9 %shard_map.87 = bf16[192,2048]{1,0:T(8,128)(2,1)S(1)} custom-call(s32[3]{0:T(128)S(1)} %pad_add_fusion.refs_0_, bf16[4096,8192]{1,0:T(8,128)(2,1)} %bitcast.3.refs_4_.refs_1_.refs_3_, bf16[128,8192]{1,0:T(8,128)(2,1)} %bitcast.17, bf16[192,4096]{1,0:T(8,128)(2,1)S(1)} %get-tuple-element.43.refs_3_, bf16[192,128]{1,0:T(8,128)(2,1)S(1)} %get-tuple-element.44.refs_4_, ...), custom_call_target="tpu_custom_call" | custom-call | tf_op jit(solution)/shard_map/pallas_call | solution.py:39
  55.2 4.1 %collective-permute-done.8 = bf16[192,2048]{1,0:T(8,128)(2,1)S(1)} collective-permute-done((bf16[192,2048]{1,0:T(8,128)(2,1)S(1)}, bf16[192,2048]{1,0:T(8,128)(2,1)S(1)}, u32[]{:S(2)}, u32[]{:S(2)}) %collective-permute-start.8) | collective-permute-done | bytes 786464 | tf_op jit(solution)/shard_map/ppermute | solution.py:66
  59.3 0.3 add_convert_fusion.refs_11_
  59.6 1.3 %collective-permute-start.14 = (bf16[192,2048]{1,0:T(8,128)(2,1)S(1)}, bf16[192,2048]{1,0:T(8,128)(2,1)S(1)}, u32[]{:S(2)}, u32[]{:S(2)}) collective-permute-start(bf16[192,2048]{1,0:T(8,128)(2,1)S(1)} %add_convert_fusion.refs_11_), channel_id=1, source_target_pairs={{16,24},{17,25},{18,26},{19,27},{20,28},{21,29},{22,30},{23,31}} | collective-permute-start | bytes 2359304 | tf_op jit(solution)/shard_map/ppermute | solution.py:66
  60.9 1.3 %collective-permute-start.13 = (bf16[192,2048]{1,0:T(8,128)(2,1)S(1)}, bf16[192,2048]{1,0:T(8,128)(2,1)S(1)}, u32[]{:S(2)}, u32[]{:S(2)}) collective-permute-start(bf16[192,2048]{1,0:T(8,128)(2,1)S(1)} %add_convert_fusion.refs_11_), channel_id=1, source_target_pairs={{16,26},{17,27},{18,24},{19,25},{20,30},{21,31},{22,28},{23,29}} | collective-permute-start | bytes 2359304 | tf_op jit(solution)/shard_map/ppermute | solution.py:66
  62.3 1.3 %collective-permute-start.12 = (bf16[64,2048]{1,0:T(8,128)(2,1)S(1)}, bf16[64,2048]{1,0:T(8,128)(2,1)S(1)}, u32[]{:S(2)}, u32[]{:S(2)}) collective-permute-start(bf16[64,2048]{1,0:T(8,128)(2,1)S(1)} %slice.5), channel_id=1, source_target_pairs={{16,30},{17,31},{18,28},{19,29},{20,26},{21,27},{22,24},{23,25}} | collective-permute-start | bytes 786440 | tf_op jit(solution)/shard_map/ppermute | solution.py:66
  63.6 0.0 collective-permute-done.9.refs_12_.refs_2_
  63.6 1.3 %collective-permute-start.11 = (bf16[64,2048]{1,0:T(8,128)(2,1)S(1)}, bf16[64,2048]{1,0:T(8,128)(2,1)S(1)}, u32[]{:S(2)}, u32[]{:S(2)}) collective-permute-start(bf16[64,2048]{1,0:T(8,128)(2,1)S(1)} %slice.5), channel_id=1, source_target_pairs={{16,28},{17,29},{18,30},{19,31},{20,24},{21,25},{22,26},{23,27}} | collective-permute-start | bytes 786440 | tf_op jit(solution)/shard_map/ppermute | solution.py:66
  64.9 0.0 collective-permute-done.1.refs_9_
  64.9 0.1 collective-permute-start.10
  65.0 0.0 copy-done
  65.0 0.0 copy-done.1
  65.0 0.8 shard_map.88
  65.9 1.6 %collective-permute-done.12.refs_5_ = bf16[64,2048]{1,0:T(8,128)(2,1)S(1)} collective-permute-done((bf16[64,2048]{1,0:T(8,128)(2,1)S(1)}, bf16[64,2048]{1,0:T(8,128)(2,1)S(1)}, u32[]{:S(2)}, u32[]{:S(2)}) %collective-permute-start.12) | collective-permute-done | bytes 262176 | tf_op jit(solution)/shard_map/ppermute | solution.py:66
  67.5 2.9 %collective-permute-done.11.refs_4_ = bf16[64,2048]{1,0:T(8,128)(2,1)S(1)} collective-permute-done((bf16[64,2048]{1,0:T(8,128)(2,1)S(1)}, bf16[64,2048]{1,0:T(8,128)(2,1)S(1)}, u32[]{:S(2)}, u32[]{:S(2)}) %collective-permute-start.11) | collective-permute-done | bytes 262176 | tf_op jit(solution)/shard_map/ppermute | solution.py:66
  70.3 0.0 collective-permute-done.14.refs_7_
  70.3 7.0 %collective-permute-done.13.refs_6_ = bf16[192,2048]{1,0:T(8,128)(2,1)S(1)} collective-permute-done((bf16[192,2048]{1,0:T(8,128)(2,1)S(1)}, bf16[192,2048]{1,0:T(8,128)(2,1)S(1)}, u32[]{:S(2)}, u32[]{:S(2)}) %collective-permute-start.13) | collective-permute-done | bytes 786464 | tf_op jit(solution)/shard_map/ppermute | solution.py:66
  77.3 0.5 shard_map.89
  77.9 0.7 collective-permute-start.15
  78.5 0.7 collective-permute-start.16
  79.2 0.7 collective-permute-start.17
  79.9 0.7 collective-permute-start.18
  80.6 0.0 collective-permute-done.10.refs_4_
  80.6 1.3 %collective-permute-start.19 = (bf16[256,128]{1,0:T(8,128)(2,1)S(1)}, bf16[256,128]{1,0:T(8,128)(2,1)S(1)}, u32[]{:S(2)}, u32[]{:S(2)}) collective-permute-start(bf16[256,128]{1,0:T(8,128)(2,1)S(1)} %get-tuple-element.53), channel_id=1, source_target_pairs={{24,16},{25,17},{26,18},{27,19},{28,20},{29,21},{30,22},{31,23}} | collective-permute-start | bytes 196616 | tf_op jit(solution)/shard_map/ppermute | solution.py:66
  81.9 0.0 collective-permute-done.15.refs_5_
  81.9 1.3 %collective-permute-start.20 = (bf16[256,128]{1,0:T(8,128)(2,1)S(1)}, bf16[256,128]{1,0:T(8,128)(2,1)S(1)}, u32[]{:S(2)}, u32[]{:S(2)}) collective-permute-start(bf16[256,128]{1,0:T(8,128)(2,1)S(1)} %get-tuple-element.54), channel_id=1, source_target_pairs={{24,17},{25,16},{26,19},{27,18},{28,21},{29,20},{30,23},{31,22}} | collective-permute-start | bytes 196616 | tf_op jit(solution)/shard_map/ppermute | solution.py:66
  83.2 0.0 collective-permute-done.16.refs_6_
  83.2 0.0 collective-permute-done.17.refs_7_
  83.2 0.0 collective-permute-done.18.refs_8_
  83.2 7.6 %collective-permute-done.19.refs_9_ = bf16[256,128]{1,0:T(8,128)(2,1)S(1)} collective-permute-done((bf16[256,128]{1,0:T(8,128)(2,1)S(1)}, bf16[256,128]{1,0:T(8,128)(2,1)S(1)}, u32[]{:S(2)}, u32[]{:S(2)}) %collective-permute-start.19) | collective-permute-done | bytes 65568 | tf_op jit(solution)/shard_map/ppermute | solution.py:66
  90.8 2.7 %collective-permute-done.20.refs_10_ = bf16[256,128]{1,0:T(8,128)(2,1)S(1)} collective-permute-done((bf16[256,128]{1,0:T(8,128)(2,1)S(1)}, bf16[256,128]{1,0:T(8,128)(2,1)S(1)}, u32[]{:S(2)}, u32[]{:S(2)}) %collective-permute-start.20) | collective-permute-done | bytes 65568 | tf_op jit(solution)/shard_map/ppermute | solution.py:66
  93.5 1.0 %shard_map.90 = f32[4,64,64]{2,1,0:T(8,128)S(1)} custom-call(s32[3]{0:T(128)S(1)} %pad_add_fusion.refs_0_, s32[4]{0:T(128)S(1)} %copy-done.2, f32[512,128]{1,0:T(8,128)S(1)} %get-tuple-element.46.refs_2_, f32[64,512]{1,0:T(8,128)S(1)} %get-tuple-element.42.refs_10_.refs_3_, f32[64,512]{1,0:T(8,128)S(1)} %collective-permute-done.10.refs_4_, ...), custom_call_target="tpu_custom_call" | custom-call | tf_op jit(solution)/shard_map/pallas_call | solution.py:39
  94.5 0.8 reshape.8
  (1 shorter events, 0.0 us)
Async XLA Ops:
  0.1 5.9 %copy-start.2 = (s32[4]{0:T(128)S(1)}, s32[4]{0:T(128)}, u32[]{:S(2)}) copy-start(s32[4]{0:T(128)} %refs_1_.5) | copy-start | bytes 52
  2.4 62.6 %collective-permute-start.1 = (bf16[448,4096]{1,0:T(8,128)(2,1)S(1)}, bf16[448,4096]{1,0:T(8,128)(2,1)S(1)}, u32[]{:S(2)}, u32[]{:S(2)}) collective-permute-start(bf16[448,4096]{1,0:T(8,128)(2,1)S(1)} %get-tuple-element.36), channel_id=1, source_target_pairs={{24,25},{25,24},{26,27},{27,26},{28,29},{29,28},{30,31},{31,30}} | collective-permute-start | bytes 11010056 | tf_op jit(solution)/shard_map/ppermute | solution.py:66
  3.3 0.7 collective-permute-start
  4.0 2.9 %collective-permute-start.2 = (bf16[64,4096]{1,0:T(8,128)(2,1)S(1)}, bf16[64,4096]{1,0:T(8,128)(2,1)S(1)}, u32[]{:S(2)}, u32[]{:S(2)}) collective-permute-start(bf16[64,4096]{1,0:T(8,128)(2,1)S(1)} %get-tuple-element.38), channel_id=1, source_target_pairs={{0,25},{1,24},{2,27},{3,26},{4,29},{5,28},{6,31},{7,30}} | collective-permute-start | bytes 1572872 | tf_op jit(solution)/shard_map/ppermute | solution.py:66
  4.7 16.8 %collective-permute-start.7 = (bf16[64,4096]{1,0:T(8,128)(2,1)S(1)}, bf16[64,4096]{1,0:T(8,128)(2,1)S(1)}, u32[]{:S(2)}, u32[]{:S(2)}) collective-permute-start(bf16[64,4096]{1,0:T(8,128)(2,1)S(1)} %get-tuple-element.31), channel_id=1, source_target_pairs={{8,16},{9,17},{10,18},{11,19},{12,20},{13,21},{14,22},{15,23}} | collective-permute-start | bytes 1572872 | tf_op jit(solution)/shard_map/ppermute | solution.py:66
  13.7 17.4 %collective-permute-start.6 = (bf16[64,2048]{1,0:T(8,128)(2,1)S(1)}, bf16[64,2048]{1,0:T(8,128)(2,1)S(1)}, u32[]{:S(2)}, u32[]{:S(2)}) collective-permute-start(bf16[64,2048]{1,0:T(8,128)(2,1)S(1)} %get-tuple-element.41), channel_id=1, source_target_pairs={{8,19},{9,18},{10,17},{11,16},{12,23},{13,22},{14,21},{15,20}} | collective-permute-start | bytes 786440 | tf_op jit(solution)/shard_map/ppermute | solution.py:66
  15.0 20.7 %collective-permute-start.4 = (bf16[64,2048]{1,0:T(8,128)(2,1)S(1)}, bf16[64,2048]{1,0:T(8,128)(2,1)S(1)}, u32[]{:S(2)}, u32[]{:S(2)}) collective-permute-start(bf16[64,2048]{1,0:T(8,128)(2,1)S(1)} %get-tuple-element.41), channel_id=1, source_target_pairs={{8,17},{9,16},{10,19},{11,18},{12,21},{13,20},{14,23},{15,22}} | collective-permute-start | bytes 786440 | tf_op jit(solution)/shard_map/ppermute | solution.py:66
  16.3 19.4 %collective-permute-start.5 = (bf16[64,2048]{1,0:T(8,128)(2,1)S(1)}, bf16[64,2048]{1,0:T(8,128)(2,1)S(1)}, u32[]{:S(2)}, u32[]{:S(2)}) collective-permute-start(bf16[64,2048]{1,0:T(8,128)(2,1)S(1)} %get-tuple-element.40.refs_5_), channel_id=1, source_target_pairs={{8,18},{9,19},{10,16},{11,17},{12,22},{13,23},{14,20},{15,21}} | collective-permute-start | bytes 786440 | tf_op jit(solution)/shard_map/ppermute | solution.py:66
  21.5 16.3 %collective-permute-start.3 = (bf16[64,2048]{1,0:T(8,128)(2,1)S(1)}, bf16[64,2048]{1,0:T(8,128)(2,1)S(1)}, u32[]{:S(2)}, u32[]{:S(2)}) collective-permute-start(bf16[64,2048]{1,0:T(8,128)(2,1)S(1)} %get-tuple-element.40.refs_5_), channel_id=1, source_target_pairs={{8,16},{9,17},{10,18},{11,19},{12,20},{13,21},{14,22},{15,23}} | collective-permute-start | bytes 786440 | tf_op jit(solution)/shard_map/ppermute | solution.py:66
  44.0 15.3 %collective-permute-start.8 = (bf16[192,2048]{1,0:T(8,128)(2,1)S(1)}, bf16[192,2048]{1,0:T(8,128)(2,1)S(1)}, u32[]{:S(2)}, u32[]{:S(2)}) collective-permute-start(bf16[192,2048]{1,0:T(8,128)(2,1)S(1)} %get-tuple-element.45.refs_5_), channel_id=1, source_target_pairs={{16,17},{17,16},{18,19},{19,18},{20,21},{21,20},{22,23},{23,22}} | collective-permute-start | bytes 2359304 | tf_op jit(solution)/shard_map/ppermute | solution.py:66
  45.9 17.7 %collective-permute-start.9 = (bf16[64,4096]{1,0:T(8,128)(2,1)S(1)}, bf16[64,4096]{1,0:T(8,128)(2,1)S(1)}, u32[]{:S(2)}, u32[]{:S(2)}) collective-permute-start(bf16[64,4096]{1,0:T(8,128)(2,1)S(1)} %get-tuple-element.31), channel_id=1, source_target_pairs={{16,24},{17,25},{18,26},{19,27},{20,28},{21,29},{22,30},{23,31}} | collective-permute-start | bytes 1572872 | tf_op jit(solution)/shard_map/ppermute | solution.py:66
  47.3 17.8 %copy-start = (bf16[1,4096,128]{2,1,0:T(8,128)(2,1)S(1)}, bf16[1,4096,128]{2,1,0:T(8,128)(2,1)}, u32[]{:S(2)}) copy-start(bf16[1,4096,128]{2,1,0:T(8,128)(2,1)} %param.11) | copy-start | bytes 3145732
  47.3 17.8 %copy-start.1 = (s32[128,128]{1,0:T(8,128)S(1)}, s32[128,128]{1,0:T(8,128)}, u32[]{:S(2)}) copy-start(s32[128,128]{1,0:T(8,128)} %refs_2_.3) | copy-start | bytes 196612
  59.6 10.7 %collective-permute-start.14 = (bf16[192,2048]{1,0:T(8,128)(2,1)S(1)}, bf16[192,2048]{1,0:T(8,128)(2,1)S(1)}, u32[]{:S(2)}, u32[]{:S(2)}) collective-permute-start(bf16[192,2048]{1,0:T(8,128)(2,1)S(1)} %add_convert_fusion.refs_11_), channel_id=1, source_target_pairs={{16,24},{17,25},{18,26},{19,27},{20,28},{21,29},{22,30},{23,31}} | collective-permute-start | bytes 2359304 | tf_op jit(solution)/shard_map/ppermute | solution.py:66
  60.9 16.4 %collective-permute-start.13 = (bf16[192,2048]{1,0:T(8,128)(2,1)S(1)}, bf16[192,2048]{1,0:T(8,128)(2,1)S(1)}, u32[]{:S(2)}, u32[]{:S(2)}) collective-permute-start(bf16[192,2048]{1,0:T(8,128)(2,1)S(1)} %add_convert_fusion.refs_11_), channel_id=1, source_target_pairs={{16,26},{17,27},{18,24},{19,25},{20,30},{21,31},{22,28},{23,29}} | collective-permute-start | bytes 2359304 | tf_op jit(solution)/shard_map/ppermute | solution.py:66
  62.3 5.2 %collective-permute-start.12 = (bf16[64,2048]{1,0:T(8,128)(2,1)S(1)}, bf16[64,2048]{1,0:T(8,128)(2,1)S(1)}, u32[]{:S(2)}, u32[]{:S(2)}) collective-permute-start(bf16[64,2048]{1,0:T(8,128)(2,1)S(1)} %slice.5), channel_id=1, source_target_pairs={{16,30},{17,31},{18,28},{19,29},{20,26},{21,27},{22,24},{23,25}} | collective-permute-start | bytes 786440 | tf_op jit(solution)/shard_map/ppermute | solution.py:66
  63.6 6.7 %collective-permute-start.11 = (bf16[64,2048]{1,0:T(8,128)(2,1)S(1)}, bf16[64,2048]{1,0:T(8,128)(2,1)S(1)}, u32[]{:S(2)}, u32[]{:S(2)}) collective-permute-start(bf16[64,2048]{1,0:T(8,128)(2,1)S(1)} %slice.5), channel_id=1, source_target_pairs={{16,28},{17,29},{18,30},{19,31},{20,24},{21,25},{22,26},{23,27}} | collective-permute-start | bytes 786440 | tf_op jit(solution)/shard_map/ppermute | solution.py:66
  64.9 15.6 %collective-permute-start.10 = (f32[64,512]{1,0:T(8,128)S(1)}, f32[64,512]{1,0:T(8,128)S(1)}, u32[]{:S(2)}, u32[]{:S(2)}) collective-permute-start(f32[64,512]{1,0:T(8,128)S(1)} %get-tuple-element.47), channel_id=1, source_target_pairs={{0,1},{1,0},{2,3},{3,2},{4,5},{5,4},{6,7},{7,6},{8,9},{9,8},{10,11... | collective-permute-start | bytes 393224 | tf_op jit(solution)/shard_map/ppermute | solution.py:520
  77.9 4.0 %collective-permute-start.15 = (bf16[256,128]{1,0:T(8,128)(2,1)S(1)}, bf16[256,128]{1,0:T(8,128)(2,1)S(1)}, u32[]{:S(2)}, u32[]{:S(2)}) collective-permute-start(bf16[256,128]{1,0:T(8,128)(2,1)S(1)} %get-tuple-element.49), channel_id=1, source_target_pairs={{24,0},{25,1},{26,2},{27,3},{28,4},{29,5},{30,6},{31,7}} | collective-permute-start | bytes 196616 | tf_op jit(solution)/shard_map/ppermute | solution.py:66
  78.5 4.6 %collective-permute-start.16 = (bf16[256,128]{1,0:T(8,128)(2,1)S(1)}, bf16[256,128]{1,0:T(8,128)(2,1)S(1)}, u32[]{:S(2)}, u32[]{:S(2)}) collective-permute-start(bf16[256,128]{1,0:T(8,128)(2,1)S(1)} %get-tuple-element.50), channel_id=1, source_target_pairs={{24,1},{25,0},{26,3},{27,2},{28,5},{29,4},{30,7},{31,6}} | collective-permute-start | bytes 196616 | tf_op jit(solution)/shard_map/ppermute | solution.py:66
  79.2 4.0 %collective-permute-start.17 = (bf16[256,128]{1,0:T(8,128)(2,1)S(1)}, bf16[256,128]{1,0:T(8,128)(2,1)S(1)}, u32[]{:S(2)}, u32[]{:S(2)}) collective-permute-start(bf16[256,128]{1,0:T(8,128)(2,1)S(1)} %get-tuple-element.51), channel_id=1, source_target_pairs={{24,8},{25,9},{26,10},{27,11},{28,12},{29,13},{30,14},{31,15}} | collective-permute-start | bytes 196616 | tf_op jit(solution)/shard_map/ppermute | solution.py:66
  79.9 3.3 %collective-permute-start.18 = (bf16[256,128]{1,0:T(8,128)(2,1)S(1)}, bf16[256,128]{1,0:T(8,128)(2,1)S(1)}, u32[]{:S(2)}, u32[]{:S(2)}) collective-permute-start(bf16[256,128]{1,0:T(8,128)(2,1)S(1)} %get-tuple-element.52), channel_id=1, source_target_pairs={{24,9},{25,8},{26,11},{27,10},{28,13},{29,12},{30,15},{31,14}} | collective-permute-start | bytes 196616 | tf_op jit(solution)/shard_map/ppermute | solution.py:66
  80.6 10.2 %collective-permute-start.19 = (bf16[256,128]{1,0:T(8,128)(2,1)S(1)}, bf16[256,128]{1,0:T(8,128)(2,1)S(1)}, u32[]{:S(2)}, u32[]{:S(2)}) collective-permute-start(bf16[256,128]{1,0:T(8,128)(2,1)S(1)} %get-tuple-element.53), channel_id=1, source_target_pairs={{24,16},{25,17},{26,18},{27,19},{28,20},{29,21},{30,22},{31,23}} | collective-permute-start | bytes 196616 | tf_op jit(solution)/shard_map/ppermute | solution.py:66
  81.9 11.6 %collective-permute-start.20 = (bf16[256,128]{1,0:T(8,128)(2,1)S(1)}, bf16[256,128]{1,0:T(8,128)(2,1)S(1)}, u32[]{:S(2)}, u32[]{:S(2)}) collective-permute-start(bf16[256,128]{1,0:T(8,128)(2,1)S(1)} %get-tuple-element.54), channel_id=1, source_target_pairs={{24,17},{25,16},{26,19},{27,18},{28,21},{29,20},{30,23},{31,22}} | collective-permute-start | bytes 196616 | tf_op jit(solution)/shard_map/ppermute | solution.py:66

commit v5 on v4

--- a/solution.py
+++ b/solution.py
@@ -58,8 +58,8 @@
         return (stage * groups + group) * parts + part % parts
 
     pairs = [
-        (place(source, g, k), place(target, to_group(g), k + by_tensor))
-        for source, target in routes
+        (place(source, g, k), place(target, to_group(g), k + (by_tensor if not more else more[0])))
+        for source, target, *more in routes
         for g in range(groups)
         for k in range(parts)
     ]
@@ -107,12 +107,12 @@
     count, seq, local = output_gradient.shape
     tokens = count * seq
     half = tokens // 2
-    near_rows = tokens - seq // 2
     width = local * parts
     rank = adapter_up_factors.shape[1]
     proj = feature_sign_bits.shape[1]
     share = 2 * proj // parts
-    block = min(256, local)
+    near_rows = tokens - proj
+    block = min(512, local)
     assert stages == 4 and groups == 4 and parts % 2 == 0 and local % block == 0 and seq % ROWS == 0
     spans = groups // 2
     span = local // spans
@@ -146,17 +146,22 @@
     def signs_of(values):
         return (2 * values - 1).astype(F32)
 
-    def prepare(info, bits, low_bits, up, grad, signs, up_low, near, far, low_buf, bits_buf, up_buf, sems):
+    def prepare(info, bits, low_bits, up, grad, signs, up_low, near, side, low_buf, bits_buf, up_buf, sems):
         mine = columns(info[2])
         made = copies(sems, (low_bits, low_buf), (up.at[:, mine], up_buf), (bits.at[:, mine], bits_buf))
         near_copy = pltpu.make_async_copy(grad.at[:near_rows], near, sems.at[3])
-        far_copy = pltpu.make_async_copy(grad.at[near_rows:], far, sems.at[4])
+        far_copy = pltpu.make_async_copy(grad.at[near_rows:], side, sems.at[4])
         pl.when(info[0] == last)(near_copy.start)
         pl.when(info[0] == 0)(far_copy.start)
         made[0].wait()
         low_left = signs_of(low_buf[...]).T[:proj, :].astype(BF16)
         made[1].wait()
         up_low[...] = nn(low_left, up_buf[...]).astype(BF16)
+
+        @pl.when(info[0] != 0)
+        def _():
+            side[...] = up_low[...]
+
         made[2].wait()
         signs[...] = signs_of(bits_buf[...]).astype(BF16)
         pl.when(info[0] == last)(near_copy.wait)
@@ -284,7 +289,7 @@
             total += value.astype(F32)
         return total.astype(BF16)
 
-    blocks, ring = local // block, 5
+    blocks, ring = local // block, 3
 
     def stream(weight, ring_buf, sems, count_of, part_of, use):
         def fetch(n):
@@ -311,9 +316,9 @@
 
         return lambda: lax.fori_loop(0, total_steps, step, 0)
 
-    sizes = range(half, tokens + 1, tokens // 16)
-
-    sizes = range(half, tokens + 1, tokens // 16)
+    sizes = range(half, tokens + 1, tokens // 8)
+
+    sizes = range(half, tokens + 1, tokens // 8)
 
     def push_own(info, lengths, raw, bits, weight, up, signs, total, u_part, y_part, both_next, *rest):
         grad, bits_buf, both, ring_buf, sems, ring_sems, tile_sems = rest
@@ -445,11 +450,11 @@
             out[e] = nn(left, right, BEST)
 
     grad = output_gradient.reshape(tokens, local)
-    signs, up_low, near, far = launch(
+    signs, up_low, near, side = launch(
         prepare,
         [(info, SMEM), (bits, HBM), (rank_sign_bits, HBM), (up, HBM), (grad, HBM)],
         [((proj, local), BF16, VMEM)] * 2
-        + [((near_rows, local), BF16, VMEM), ((tokens - near_rows, local), BF16, VMEM)],
+        + [((near_rows, local), BF16, VMEM), ((proj, local), BF16, VMEM)],
         [
             pltpu.VMEM(rank_sign_bits.shape, jnp.int32),
             pltpu.VMEM((proj, local), jnp.int32),
@@ -458,10 +463,11 @@
         ],
         room=8,
     )
-    below = [None] + [shift(up_low, [(s, s + 1)], same, 0) for s in range(last - 1, -1, -1)][::-1]
-    far, _ = lax.optimization_barrier((far, below[1]))
-    fars = [shift(far, [(0, last)], same, -k) for k in range(1, parts)]
+    below = [None, shift(up_low, [(0, 1)], same, 0), None, None]
     nears = [shift(near, [(last, last)], same, -k) for k in range(1, parts)]
+    fars = [shift(side, [(0, last, -k)] + ([(1, 2, 0)] if k == 1 else []), same, 0) for k in range(1, parts)]
+    below[2] = fars[0]
+    below[last] = shift(up_low, [(2, last)], same, 0)
     total, u_part, y_part, both_next = launch(
         push_own,
         [(info, SMEM), (lengths, SMEM), (grad, HBM), (bits, HBM), (weight, HBM), (up, HBM), (signs, VMEM)],
@@ -476,8 +482,7 @@
             pltpu.SemaphoreType.DMA((ring,)),
             pltpu.SemaphoreType.DMA((tokens // ROWS,)),
         ],
-        [below[1]],
-        room=20,
+        room=21,
     )
     *outs, held = launch(
         first_step,
@@ -491,7 +496,7 @@
             pltpu.SemaphoreType.DMA((far_count,)),
             pltpu.SemaphoreType.DMA((parts + 1,)),
         ],
-        [u_part] + fars,
+        [u_part],
         9,
     )
     arrived = [shift(v, [(1, 2)], neighbour(z), k) for z in range(spans) for k, v in enumerate(outs)]
@@ -560,12 +565,12 @@
         [
             pltpu.VMEM((parts - 1, tokens, local), BF16),
             pltpu.VMEM((tokens, rank), BF16),
-            pltpu.VMEM((tokens, block), F32),
+            pltpu.VMEM((tokens if parts > 2 else ROWS, block), F32),
             pltpu.VMEM((ring, block, local), BF16),
             pltpu.SemaphoreType.DMA((ring,)),
         ],
         [both_reach, below[last]],
-        18,
+        21,
     )
 
     def meet(info, grad, low_last, signs, *rest):
@@ -582,6 +587,7 @@
                     x[2 * proj : 4 * proj, there] = given[k][proj:, :]
             x[4 * proj : 5 * proj, :] = low_last[...]
             x[5 * proj :, :] = signs[...]
+
             y = nt(grad[...], x[...])
             for s in range(last):
                 left, right = (y[:, (2 * s + i) * proj : (2 * s + i + 1) * proj] for i in range(2))

time: 95.7 us -> 94.3 us (0.985)
  waiting for transfers between devices: 40.1 us -> 38.4 us
    ppermute x20 -> x19, waiting for transfers between devices: 40.1 us -> 38.4 us  [shift(): return lax.ppermute(value, AXES, pairs)]
    ppermute x20 -> x19, starting transfers between devices: 22.5 us -> 22.3 us  [shift(): return lax.ppermute(value, AXES, pairs)]
  transfers between devices with their start and end apart: 21 -> 20, of which waited for: 10 -> 10; matrix products, arithmetic and copies ran while one was open for 0% -> 0% of each run, Pallas kernels for 29% -> 30%
where the time goes in v5:
time: 94.3 us; the launch traced here: 93.8 us
  waiting for transfers between devices  38.4 us (41%)
  Pallas kernels  31 us (33%)
  starting transfers between devices  22.9 us (24%)
    ppermute x19, waiting for transfers between devices, shift(): return lax.ppermute(value, AXES, pairs)  38.4 us
    pallas_call x9, Pallas kernels, launch(): pl.pallas_call(kernel, in_specs=[pl.BlockSpec(memory_space=space) for _,...  31 us
    ppermute x19, starting transfers between devices, shift(): return lax.ppermute(value, AXES, pairs)  22.3 us
  transfers between devices with their start and end apart: 20, of which 10 were waited for; matrix products, arithmetic and copies ran while one was open for 0% of the time, Pallas kernels for 30%

profile of v5, /device:TPU:12, one launch (start us, length us, event | category | flops | bytes accessed | tf_op | source)
XLA Modules:
  0.0 93.8 jit_solution(17707914993713330189)
XLA Ops:
  0.0 0.1 pad_add_fusion.refs_0_
  0.1 0.0 copy-start.2
  0.1 2.3 %shard_map.82 = (bf16[64,4096]{1,0:T(8,128)(2,1)S(1)}, bf16[64,4096]{1,0:T(8,128)(2,1)S(1)}, bf16[448,4096]{1,0:T(8,128)(2,1)S(1)}, bf16[64,4096]{1,0:T(8,128)(2,1)S(1)}) custom-call(s32[3]{0:T(128)S(1)} %pad_add_fusion.refs_0_, s32[64,8192]{1,0:T(8,128)} %bitcast.20, s32[128,128]{1,0:T(8,128)} %refs_2_.3, bf16[128,8192]{1,0:T(8,128)(2,1)} %bitcast.13, ...), custom_call_target="tpu_custom_call" | custom-call | tf_op jit(solution)/shard_map/pallas_call | solution.py:39
  2.4 0.9 collective-permute-start
  3.3 0.7 collective-permute-start.2
  4.0 1.3 %collective-permute-start.1 = (bf16[64,4096]{1,0:T(8,128)(2,1)S(1)}, bf16[64,4096]{1,0:T(8,128)(2,1)S(1)}, u32[]{:S(2)}, u32[]{:S(2)}) collective-permute-start(bf16[64,4096]{1,0:T(8,128)(2,1)S(1)} %get-tuple-element.35), channel_id=1, source_target_pairs={{0,25},{1,24},{2,27},{3,26},{4,29},{5,28},{6,31},{7,30},{8,16},{9,... | collective-permute-start | bytes 1572872 | tf_op jit(solution)/shard_map/ppermute | solution.py:66
  5.3 0.0 copy-done.2
  5.3 0.9 shard_map.83
  6.2 0.0 collective-permute-done.2.refs_4_
  6.2 6.7 %shard_map.84 = (bf16[64,2048]{1,0:T(8,128)(2,1)S(1)}, bf16[64,2048]{1,0:T(8,128)(2,1)S(1)}, bf16[4,4096,512]{2,1,0:T(8,128)(2,1)S(1)}) custom-call(s32[3]{0:T(128)S(1)} %pad_add_fusion.refs_0_, bf16[4096,8192]{1,0:T(8,128)(2,1)} %bitcast.3.refs_4_.refs_1_.refs_3_, bf16[4096,128]{1,0:T(8,128)(2,1)} %bitcast.9, bf16[128,8192]{1,0:T(8,128)(2,1)} %bitcast.15, ...), custom_call_target="tpu_custom_call" | custom-call | tf_op jit(solution)/shard_map/pallas_call | solution.py:39
  12.9 1.3 %collective-permute-start.6 = (bf16[64,2048]{1,0:T(8,128)(2,1)S(1)}, bf16[64,2048]{1,0:T(8,128)(2,1)S(1)}, u32[]{:S(2)}, u32[]{:S(2)}) collective-permute-start(bf16[64,2048]{1,0:T(8,128)(2,1)S(1)} %get-tuple-element.39), channel_id=1, source_target_pairs={{8,19},{9,18},{10,17},{11,16},{12,23},{13,22},{14,21},{15,20}} | collective-permute-start | bytes 786440 | tf_op jit(solution)/shard_map/ppermute | solution.py:66
  14.2 1.3 %collective-permute-start.4 = (bf16[64,2048]{1,0:T(8,128)(2,1)S(1)}, bf16[64,2048]{1,0:T(8,128)(2,1)S(1)}, u32[]{:S(2)}, u32[]{:S(2)}) collective-permute-start(bf16[64,2048]{1,0:T(8,128)(2,1)S(1)} %get-tuple-element.39), channel_id=1, source_target_pairs={{8,17},{9,16},{10,19},{11,18},{12,21},{13,20},{14,23},{15,22}} | collective-permute-start | bytes 786440 | tf_op jit(solution)/shard_map/ppermute | solution.py:66
  15.5 1.3 %collective-permute-start.5 = (bf16[64,2048]{1,0:T(8,128)(2,1)S(1)}, bf16[64,2048]{1,0:T(8,128)(2,1)S(1)}, u32[]{:S(2)}, u32[]{:S(2)}) collective-permute-start(bf16[64,2048]{1,0:T(8,128)(2,1)S(1)} %get-tuple-element.38.refs_5_), channel_id=1, source_target_pairs={{8,18},{9,19},{10,16},{11,17},{12,22},{13,23},{14,20},{15,21}} | collective-permute-start | bytes 786440 | tf_op jit(solution)/shard_map/ppermute | solution.py:66
  16.8 3.3 %collective-permute-done.1.refs_8_.refs_10_ = bf16[64,4096]{1,0:T(8,128)(2,1)S(1)} collective-permute-done((bf16[64,4096]{1,0:T(8,128)(2,1)S(1)}, bf16[64,4096]{1,0:T(8,128)(2,1)S(1)}, u32[]{:S(2)}, u32[]{:S(2)}) %collective-permute-start.1) | collective-permute-done | bytes 524320 | tf_op jit(solution)/shard_map/ppermute | solution.py:66
  20.1 1.3 %collective-permute-start.3 = (bf16[64,2048]{1,0:T(8,128)(2,1)S(1)}, bf16[64,2048]{1,0:T(8,128)(2,1)S(1)}, u32[]{:S(2)}, u32[]{:S(2)}) collective-permute-start(bf16[64,2048]{1,0:T(8,128)(2,1)S(1)} %get-tuple-element.38.refs_5_), channel_id=1, source_target_pairs={{8,16},{9,17},{10,18},{11,19},{12,20},{13,21},{14,22},{15,23}} | collective-permute-start | bytes 786440 | tf_op jit(solution)/shard_map/ppermute | solution.py:66
  21.4 4.7 %shard_map.85 = (f32[64,512]{1,0:T(8,128)S(1)}, f32[64,512]{1,0:T(8,128)S(1)}) custom-call(s32[3]{0:T(128)S(1)} %pad_add_fusion.refs_0_, bf16[512,4096]{1,0:T(8,128)(2,1)} %bitcast.22, bf16[64,4096]{1,0:T(8,128)(2,1)S(1)} %get-tuple-element.29.refs_6_.refs_5_.refs_2_.refs_9_.refs_3_, bf16[4096,128]{1,0:T(8,128)(2,1)} %bitcast.10, s32[128,128]{1,0:T(8,128)} %refs_2_.3, ...), custom_call_target="tpu_custom_call" | custom-call | tf_op jit(solution)/shard_map/pallas_call | solution.py:39
  26.1 3.1 %collective-permute-done.6.refs_7_ = bf16[64,2048]{1,0:T(8,128)(2,1)S(1)} collective-permute-done((bf16[64,2048]{1,0:T(8,128)(2,1)S(1)}, bf16[64,2048]{1,0:T(8,128)(2,1)S(1)}, u32[]{:S(2)}, u32[]{:S(2)}) %collective-permute-start.6) | collective-permute-done | bytes 262176 | tf_op jit(solution)/shard_map/ppermute | solution.py:66
  29.2 4.6 %collective-permute-done.4.refs_5_ = bf16[64,2048]{1,0:T(8,128)(2,1)S(1)} collective-permute-done((bf16[64,2048]{1,0:T(8,128)(2,1)S(1)}, bf16[64,2048]{1,0:T(8,128)(2,1)S(1)}, u32[]{:S(2)}, u32[]{:S(2)}) %collective-permute-start.4) | collective-permute-done | bytes 262176 | tf_op jit(solution)/shard_map/ppermute | solution.py:66
  33.7 0.0 collective-permute-done.5.refs_6_
  33.7 2.7 %collective-permute-done.3.refs_4_ = bf16[64,2048]{1,0:T(8,128)(2,1)S(1)} collective-permute-done((bf16[64,2048]{1,0:T(8,128)(2,1)S(1)}, bf16[64,2048]{1,0:T(8,128)(2,1)S(1)}, u32[]{:S(2)}, u32[]{:S(2)}) %collective-permute-start.3) | collective-permute-done | bytes 262176 | tf_op jit(solution)/shard_map/ppermute | solution.py:66
  36.4 6.2 %shard_map.86 = (bf16[192,2048]{1,0:T(8,128)(2,1)S(1)}, bf16[192,4096]{1,0:T(8,128)(2,1)S(1)}, bf16[192,128]{1,0:T(8,128)(2,1)S(1)}) custom-call(s32[3]{0:T(128)S(1)} %pad_add_fusion.refs_0_, bf16[4,4096,512]{2,1,0:T(8,128)(2,1)S(1)} %get-tuple-element.37.refs_1_, bf16[4096,128]{1,0:T(8,128)(2,1)} %bitcast.11, bf16[128,8192]{1,0:T(8,128)(2,1)} %bitcast.16, ...), custom_call_target="tpu_custom_call" | custom-call | tf_op jit(solution)/shard_map/pallas_call | solution.py:39
  42.6 2.4 %collective-permute-start.7 = (bf16[192,2048]{1,0:T(8,128)(2,1)S(1)}, bf16[192,2048]{1,0:T(8,128)(2,1)S(1)}, u32[]{:S(2)}, u32[]{:S(2)}) collective-permute-start(bf16[192,2048]{1,0:T(8,128)(2,1)S(1)} %get-tuple-element.43.refs_5_), channel_id=1, source_target_pairs={{16,17},{17,16},{18,19},{19,18},{20,21},{21,20},{22,23},{23,22}} | collective-permute-start | bytes 2359304 | tf_op jit(solution)/shard_map/ppermute | solution.py:66
  45.1 1.3 %collective-permute-start.8 = (bf16[64,4096]{1,0:T(8,128)(2,1)S(1)}, bf16[64,4096]{1,0:T(8,128)(2,1)S(1)}, u32[]{:S(2)}, u32[]{:S(2)}) collective-permute-start(bf16[64,4096]{1,0:T(8,128)(2,1)S(1)} %get-tuple-element.36), channel_id=1, source_target_pairs={{16,24},{17,25},{18,26},{19,27},{20,28},{21,29},{22,30},{23,31}} | collective-permute-start | bytes 1572872 | tf_op jit(solution)/shard_map/ppermute | solution.py:66
  46.4 0.0 copy-start
  46.4 0.0 copy-start.1
  46.4 7.9 %shard_map.87 = bf16[192,2048]{1,0:T(8,128)(2,1)S(1)} custom-call(s32[3]{0:T(128)S(1)} %pad_add_fusion.refs_0_, bf16[4096,8192]{1,0:T(8,128)(2,1)} %bitcast.3.refs_4_.refs_1_.refs_3_, bf16[128,8192]{1,0:T(8,128)(2,1)} %bitcast.17, bf16[192,4096]{1,0:T(8,128)(2,1)S(1)} %get-tuple-element.41.refs_3_, bf16[192,128]{1,0:T(8,128)(2,1)S(1)} %get-tuple-element.42.refs_4_, ...), custom_call_target="tpu_custom_call" | custom-call | tf_op jit(solution)/shard_map/pallas_call | solution.py:39
  54.3 3.6 %collective-permute-done.7 = bf16[192,2048]{1,0:T(8,128)(2,1)S(1)} collective-permute-done((bf16[192,2048]{1,0:T(8,128)(2,1)S(1)}, bf16[192,2048]{1,0:T(8,128)(2,1)S(1)}, u32[]{:S(2)}, u32[]{:S(2)}) %collective-permute-start.7) | collective-permute-done | bytes 786464 | tf_op jit(solution)/shard_map/ppermute | solution.py:66
  57.9 0.3 add_convert_fusion.refs_11_
  58.2 1.3 %collective-permute-start.13 = (bf16[192,2048]{1,0:T(8,128)(2,1)S(1)}, bf16[192,2048]{1,0:T(8,128)(2,1)S(1)}, u32[]{:S(2)}, u32[]{:S(2)}) collective-permute-start(bf16[192,2048]{1,0:T(8,128)(2,1)S(1)} %add_convert_fusion.refs_11_), channel_id=1, source_target_pairs={{16,24},{17,25},{18,26},{19,27},{20,28},{21,29},{22,30},{23,31}} | collective-permute-start | bytes 2359304 | tf_op jit(solution)/shard_map/ppermute | solution.py:66
  59.5 1.3 %collective-permute-start.12 = (bf16[192,2048]{1,0:T(8,128)(2,1)S(1)}, bf16[192,2048]{1,0:T(8,128)(2,1)S(1)}, u32[]{:S(2)}, u32[]{:S(2)}) collective-permute-start(bf16[192,2048]{1,0:T(8,128)(2,1)S(1)} %add_convert_fusion.refs_11_), channel_id=1, source_target_pairs={{16,26},{17,27},{18,24},{19,25},{20,30},{21,31},{22,28},{23,29}} | collective-permute-start | bytes 2359304 | tf_op jit(solution)/shard_map/ppermute | solution.py:66
  60.9 1.3 %collective-permute-start.11 = (bf16[64,2048]{1,0:T(8,128)(2,1)S(1)}, bf16[64,2048]{1,0:T(8,128)(2,1)S(1)}, u32[]{:S(2)}, u32[]{:S(2)}) collective-permute-start(bf16[64,2048]{1,0:T(8,128)(2,1)S(1)} %slice.5), channel_id=1, source_target_pairs={{16,30},{17,31},{18,28},{19,29},{20,26},{21,27},{22,24},{23,25}} | collective-permute-start | bytes 786440 | tf_op jit(solution)/shard_map/ppermute | solution.py:66
  62.2 0.0 collective-permute-done.8.refs_12_.refs_2_
  62.2 1.3 %collective-permute-start.10 = (bf16[64,2048]{1,0:T(8,128)(2,1)S(1)}, bf16[64,2048]{1,0:T(8,128)(2,1)S(1)}, u32[]{:S(2)}, u32[]{:S(2)}) collective-permute-start(bf16[64,2048]{1,0:T(8,128)(2,1)S(1)} %slice.5), channel_id=1, source_target_pairs={{16,28},{17,29},{18,30},{19,31},{20,24},{21,25},{22,26},{23,27}} | collective-permute-start | bytes 786440 | tf_op jit(solution)/shard_map/ppermute | solution.py:66
  63.5 0.0 collective-permute-done.refs_9_
  63.5 0.6 collective-permute-start.9
  64.1 0.0 copy-done
  64.1 0.0 copy-done.1
  64.2 0.8 shard_map.88
  65.0 1.1 %collective-permute-done.11.refs_5_ = bf16[64,2048]{1,0:T(8,128)(2,1)S(1)} collective-permute-done((bf16[64,2048]{1,0:T(8,128)(2,1)S(1)}, bf16[64,2048]{1,0:T(8,128)(2,1)S(1)}, u32[]{:S(2)}, u32[]{:S(2)}) %collective-permute-start.11) | collective-permute-done | bytes 262176 | tf_op jit(solution)/shard_map/ppermute | solution.py:66
  66.1 2.9 %collective-permute-done.10.refs_4_ = bf16[64,2048]{1,0:T(8,128)(2,1)S(1)} collective-permute-done((bf16[64,2048]{1,0:T(8,128)(2,1)S(1)}, bf16[64,2048]{1,0:T(8,128)(2,1)S(1)}, u32[]{:S(2)}, u32[]{:S(2)}) %collective-permute-start.10) | collective-permute-done | bytes 262176 | tf_op jit(solution)/shard_map/ppermute | solution.py:66
  68.9 0.0 collective-permute-done.13.refs_7_
  68.9 7.0 %collective-permute-done.12.refs_6_ = bf16[192,2048]{1,0:T(8,128)(2,1)S(1)} collective-permute-done((bf16[192,2048]{1,0:T(8,128)(2,1)S(1)}, bf16[192,2048]{1,0:T(8,128)(2,1)S(1)}, u32[]{:S(2)}, u32[]{:S(2)}) %collective-permute-start.12) | collective-permute-done | bytes 786464 | tf_op jit(solution)/shard_map/ppermute | solution.py:66
  75.9 0.5 shard_map.89
  76.5 0.7 collective-permute-start.14
  77.2 0.7 collective-permute-start.15
  77.8 0.7 collective-permute-start.16
  78.5 0.7 collective-permute-start.17
  79.2 0.0 collective-permute-done.9.refs_4_
  79.2 1.3 %collective-permute-start.18 = (bf16[256,128]{1,0:T(8,128)(2,1)S(1)}, bf16[256,128]{1,0:T(8,128)(2,1)S(1)}, u32[]{:S(2)}, u32[]{:S(2)}) collective-permute-start(bf16[256,128]{1,0:T(8,128)(2,1)S(1)} %get-tuple-element.51), channel_id=1, source_target_pairs={{24,16},{25,17},{26,18},{27,19},{28,20},{29,21},{30,22},{31,23}} | collective-permute-start | bytes 196616 | tf_op jit(solution)/shard_map/ppermute | solution.py:66
  80.5 0.0 collective-permute-done.14.refs_5_
  80.5 1.3 %collective-permute-start.19 = (bf16[256,128]{1,0:T(8,128)(2,1)S(1)}, bf16[256,128]{1,0:T(8,128)(2,1)S(1)}, u32[]{:S(2)}, u32[]{:S(2)}) collective-permute-start(bf16[256,128]{1,0:T(8,128)(2,1)S(1)} %get-tuple-element.52), channel_id=1, source_target_pairs={{24,17},{25,16},{26,19},{27,18},{28,21},{29,20},{30,23},{31,22}} | collective-permute-start | bytes 196616 | tf_op jit(solution)/shard_map/ppermute | solution.py:66
  81.8 0.0 collective-permute-done.15.refs_6_
  81.8 0.0 collective-permute-done.16.refs_7_
  81.8 0.0 collective-permute-done.17.refs_8_
  81.8 7.6 %collective-permute-done.18.refs_9_ = bf16[256,128]{1,0:T(8,128)(2,1)S(1)} collective-permute-done((bf16[256,128]{1,0:T(8,128)(2,1)S(1)}, bf16[256,128]{1,0:T(8,128)(2,1)S(1)}, u32[]{:S(2)}, u32[]{:S(2)}) %collective-permute-start.18) | collective-permute-done | bytes 65568 | tf_op jit(solution)/shard_map/ppermute | solution.py:66
  89.4 2.6 %collective-permute-done.19.refs_10_ = bf16[256,128]{1,0:T(8,128)(2,1)S(1)} collective-permute-done((bf16[256,128]{1,0:T(8,128)(2,1)S(1)}, bf16[256,128]{1,0:T(8,128)(2,1)S(1)}, u32[]{:S(2)}, u32[]{:S(2)}) %collective-permute-start.19) | collective-permute-done | bytes 65568 | tf_op jit(solution)/shard_map/ppermute | solution.py:66
  92.0 1.0 %shard_map.90 = f32[4,64,64]{2,1,0:T(8,128)S(1)} custom-call(s32[3]{0:T(128)S(1)} %pad_add_fusion.refs_0_, s32[4]{0:T(128)S(1)} %copy-done.2, f32[512,128]{1,0:T(8,128)S(1)} %get-tuple-element.44.refs_2_, f32[64,512]{1,0:T(8,128)S(1)} %get-tuple-element.40.refs_10_.refs_3_, f32[64,512]{1,0:T(8,128)S(1)} %collective-permute-done.9.refs_4_, ...), custom_call_target="tpu_custom_call" | custom-call | tf_op jit(solution)/shard_map/pallas_call | solution.py:39
  93.1 0.8 reshape.8
  (1 shorter events, 0.0 us)
Async XLA Ops:
  0.1 5.2 %copy-start.2 = (s32[4]{0:T(128)S(1)}, s32[4]{0:T(128)}, u32[]{:S(2)}) copy-start(s32[4]{0:T(128)} %refs_1_.5) | copy-start | bytes 52
  2.4 61.2 %collective-permute-start = (bf16[448,4096]{1,0:T(8,128)(2,1)S(1)}, bf16[448,4096]{1,0:T(8,128)(2,1)S(1)}, u32[]{:S(2)}, u32[]{:S(2)}) collective-permute-start(bf16[448,4096]{1,0:T(8,128)(2,1)S(1)} %get-tuple-element.34), channel_id=1, source_target_pairs={{24,25},{25,24},{26,27},{27,26},{28,29},{29,28},{30,31},{31,30}} | collective-permute-start | bytes 11010056 | tf_op jit(solution)/shard_map/ppermute | solution.py:66
  3.3 2.9 %collective-permute-start.2 = (bf16[64,4096]{1,0:T(8,128)(2,1)S(1)}, bf16[64,4096]{1,0:T(8,128)(2,1)S(1)}, u32[]{:S(2)}, u32[]{:S(2)}) collective-permute-start(bf16[64,4096]{1,0:T(8,128)(2,1)S(1)} %get-tuple-element.36), channel_id=1, source_target_pairs={{0,8},{1,9},{2,10},{3,11},{4,12},{5,13},{6,14},{7,15}} | collective-permute-start | bytes 1572872 | tf_op jit(solution)/shard_map/ppermute | solution.py:66
  4.0 16.1 %collective-permute-start.1 = (bf16[64,4096]{1,0:T(8,128)(2,1)S(1)}, bf16[64,4096]{1,0:T(8,128)(2,1)S(1)}, u32[]{:S(2)}, u32[]{:S(2)}) collective-permute-start(bf16[64,4096]{1,0:T(8,128)(2,1)S(1)} %get-tuple-element.35), channel_id=1, source_target_pairs={{0,25},{1,24},{2,27},{3,26},{4,29},{5,28},{6,31},{7,30},{8,16},{9,... | collective-permute-start | bytes 1572872 | tf_op jit(solution)/shard_map/ppermute | solution.py:66
  12.9 16.2 %collective-permute-start.6 = (bf16[64,2048]{1,0:T(8,128)(2,1)S(1)}, bf16[64,2048]{1,0:T(8,128)(2,1)S(1)}, u32[]{:S(2)}, u32[]{:S(2)}) collective-permute-start(bf16[64,2048]{1,0:T(8,128)(2,1)S(1)} %get-tuple-element.39), channel_id=1, source_target_pairs={{8,19},{9,18},{10,17},{11,16},{12,23},{13,22},{14,21},{15,20}} | collective-permute-start | bytes 786440 | tf_op jit(solution)/shard_map/ppermute | solution.py:66
  14.2 19.5 %collective-permute-start.4 = (bf16[64,2048]{1,0:T(8,128)(2,1)S(1)}, bf16[64,2048]{1,0:T(8,128)(2,1)S(1)}, u32[]{:S(2)}, u32[]{:S(2)}) collective-permute-start(bf16[64,2048]{1,0:T(8,128)(2,1)S(1)} %get-tuple-element.39), channel_id=1, source_target_pairs={{8,17},{9,16},{10,19},{11,18},{12,21},{13,20},{14,23},{15,22}} | collective-permute-start | bytes 786440 | tf_op jit(solution)/shard_map/ppermute | solution.py:66
  15.5 18.2 %collective-permute-start.5 = (bf16[64,2048]{1,0:T(8,128)(2,1)S(1)}, bf16[64,2048]{1,0:T(8,128)(2,1)S(1)}, u32[]{:S(2)}, u32[]{:S(2)}) collective-permute-start(bf16[64,2048]{1,0:T(8,128)(2,1)S(1)} %get-tuple-element.38.refs_5_), channel_id=1, source_target_pairs={{8,18},{9,19},{10,16},{11,17},{12,22},{13,23},{14,20},{15,21}} | collective-permute-start | bytes 786440 | tf_op jit(solution)/shard_map/ppermute | solution.py:66
  20.1 16.3 %collective-permute-start.3 = (bf16[64,2048]{1,0:T(8,128)(2,1)S(1)}, bf16[64,2048]{1,0:T(8,128)(2,1)S(1)}, u32[]{:S(2)}, u32[]{:S(2)}) collective-permute-start(bf16[64,2048]{1,0:T(8,128)(2,1)S(1)} %get-tuple-element.38.refs_5_), channel_id=1, source_target_pairs={{8,16},{9,17},{10,18},{11,19},{12,20},{13,21},{14,22},{15,23}} | collective-permute-start | bytes 786440 | tf_op jit(solution)/shard_map/ppermute | solution.py:66
  42.6 15.3 %collective-permute-start.7 = (bf16[192,2048]{1,0:T(8,128)(2,1)S(1)}, bf16[192,2048]{1,0:T(8,128)(2,1)S(1)}, u32[]{:S(2)}, u32[]{:S(2)}) collective-permute-start(bf16[192,2048]{1,0:T(8,128)(2,1)S(1)} %get-tuple-element.43.refs_5_), channel_id=1, source_target_pairs={{16,17},{17,16},{18,19},{19,18},{20,21},{21,20},{22,23},{23,22}} | collective-permute-start | bytes 2359304 | tf_op jit(solution)/shard_map/ppermute | solution.py:66
  45.1 17.1 %collective-permute-start.8 = (bf16[64,4096]{1,0:T(8,128)(2,1)S(1)}, bf16[64,4096]{1,0:T(8,128)(2,1)S(1)}, u32[]{:S(2)}, u32[]{:S(2)}) collective-permute-start(bf16[64,4096]{1,0:T(8,128)(2,1)S(1)} %get-tuple-element.36), channel_id=1, source_target_pairs={{16,24},{17,25},{18,26},{19,27},{20,28},{21,29},{22,30},{23,31}} | collective-permute-start | bytes 1572872 | tf_op jit(solution)/shard_map/ppermute | solution.py:66
  46.4 17.8 %copy-start = (bf16[1,4096,128]{2,1,0:T(8,128)(2,1)S(1)}, bf16[1,4096,128]{2,1,0:T(8,128)(2,1)}, u32[]{:S(2)}) copy-start(bf16[1,4096,128]{2,1,0:T(8,128)(2,1)} %param.11) | copy-start | bytes 3145732
  46.4 17.7 %copy-start.1 = (s32[128,128]{1,0:T(8,128)S(1)}, s32[128,128]{1,0:T(8,128)}, u32[]{:S(2)}) copy-start(s32[128,128]{1,0:T(8,128)} %refs_2_.3) | copy-start | bytes 196612
  58.2 10.7 %collective-permute-start.13 = (bf16[192,2048]{1,0:T(8,128)(2,1)S(1)}, bf16[192,2048]{1,0:T(8,128)(2,1)S(1)}, u32[]{:S(2)}, u32[]{:S(2)}) collective-permute-start(bf16[192,2048]{1,0:T(8,128)(2,1)S(1)} %add_convert_fusion.refs_11_), channel_id=1, source_target_pairs={{16,24},{17,25},{18,26},{19,27},{20,28},{21,29},{22,30},{23,31}} | collective-permute-start | bytes 2359304 | tf_op jit(solution)/shard_map/ppermute | solution.py:66
  59.5 16.4 %collective-permute-start.12 = (bf16[192,2048]{1,0:T(8,128)(2,1)S(1)}, bf16[192,2048]{1,0:T(8,128)(2,1)S(1)}, u32[]{:S(2)}, u32[]{:S(2)}) collective-permute-start(bf16[192,2048]{1,0:T(8,128)(2,1)S(1)} %add_convert_fusion.refs_11_), channel_id=1, source_target_pairs={{16,26},{17,27},{18,24},{19,25},{20,30},{21,31},{22,28},{23,29}} | collective-permute-start | bytes 2359304 | tf_op jit(solution)/shard_map/ppermute | solution.py:66
  60.9 5.2 %collective-permute-start.11 = (bf16[64,2048]{1,0:T(8,128)(2,1)S(1)}, bf16[64,2048]{1,0:T(8,128)(2,1)S(1)}, u32[]{:S(2)}, u32[]{:S(2)}) collective-permute-start(bf16[64,2048]{1,0:T(8,128)(2,1)S(1)} %slice.5), channel_id=1, source_target_pairs={{16,30},{17,31},{18,28},{19,29},{20,26},{21,27},{22,24},{23,25}} | collective-permute-start | bytes 786440 | tf_op jit(solution)/shard_map/ppermute | solution.py:66
  62.2 6.7 %collective-permute-start.10 = (bf16[64,2048]{1,0:T(8,128)(2,1)S(1)}, bf16[64,2048]{1,0:T(8,128)(2,1)S(1)}, u32[]{:S(2)}, u32[]{:S(2)}) collective-permute-start(bf16[64,2048]{1,0:T(8,128)(2,1)S(1)} %slice.5), channel_id=1, source_target_pairs={{16,28},{17,29},{18,30},{19,31},{20,24},{21,25},{22,26},{23,27}} | collective-permute-start | bytes 786440 | tf_op jit(solution)/shard_map/ppermute | solution.py:66
  63.5 15.6 %collective-permute-start.9 = (f32[64,512]{1,0:T(8,128)S(1)}, f32[64,512]{1,0:T(8,128)S(1)}, u32[]{:S(2)}, u32[]{:S(2)}) collective-permute-start(f32[64,512]{1,0:T(8,128)S(1)} %get-tuple-element.45), channel_id=1, source_target_pairs={{0,1},{1,0},{2,3},{3,2},{4,5},{5,4},{6,7},{7,6},{8,9},{9,8},{10,11... | collective-permute-start | bytes 393224 | tf_op jit(solution)/shard_map/ppermute | solution.py:525
  76.5 4.0 %collective-permute-start.14 = (bf16[256,128]{1,0:T(8,128)(2,1)S(1)}, bf16[256,128]{1,0:T(8,128)(2,1)S(1)}, u32[]{:S(2)}, u32[]{:S(2)}) collective-permute-start(bf16[256,128]{1,0:T(8,128)(2,1)S(1)} %get-tuple-element.47), channel_id=1, source_target_pairs={{24,0},{25,1},{26,2},{27,3},{28,4},{29,5},{30,6},{31,7}} | collective-permute-start | bytes 196616 | tf_op jit(solution)/shard_map/ppermute | solution.py:66
  77.2 4.6 %collective-permute-start.15 = (bf16[256,128]{1,0:T(8,128)(2,1)S(1)}, bf16[256,128]{1,0:T(8,128)(2,1)S(1)}, u32[]{:S(2)}, u32[]{:S(2)}) collective-permute-start(bf16[256,128]{1,0:T(8,128)(2,1)S(1)} %get-tuple-element.48), channel_id=1, source_target_pairs={{24,1},{25,0},{26,3},{27,2},{28,5},{29,4},{30,7},{31,6}} | collective-permute-start | bytes 196616 | tf_op jit(solution)/shard_map/ppermute | solution.py:66
  77.8 4.0 %collective-permute-start.16 = (bf16[256,128]{1,0:T(8,128)(2,1)S(1)}, bf16[256,128]{1,0:T(8,128)(2,1)S(1)}, u32[]{:S(2)}, u32[]{:S(2)}) collective-permute-start(bf16[256,128]{1,0:T(8,128)(2,1)S(1)} %get-tuple-element.49), channel_id=1, source_target_pairs={{24,8},{25,9},{26,10},{27,11},{28,12},{29,13},{30,14},{31,15}} | collective-permute-start | bytes 196616 | tf_op jit(solution)/shard_map/ppermute | solution.py:66
  78.5 3.3 %collective-permute-start.17 = (bf16[256,128]{1,0:T(8,128)(2,1)S(1)}, bf16[256,128]{1,0:T(8,128)(2,1)S(1)}, u32[]{:S(2)}, u32[]{:S(2)}) collective-permute-start(bf16[256,128]{1,0:T(8,128)(2,1)S(1)} %get-tuple-element.50), channel_id=1, source_target_pairs={{24,9},{25,8},{26,11},{27,10},{28,13},{29,12},{30,15},{31,14}} | collective-permute-start | bytes 196616 | tf_op jit(solution)/shard_map/ppermute | solution.py:66
  79.2 10.2 %collective-permute-start.18 = (bf16[256,128]{1,0:T(8,128)(2,1)S(1)}, bf16[256,128]{1,0:T(8,128)(2,1)S(1)}, u32[]{:S(2)}, u32[]{:S(2)}) collective-permute-start(bf16[256,128]{1,0:T(8,128)(2,1)S(1)} %get-tuple-element.51), channel_id=1, source_target_pairs={{24,16},{25,17},{26,18},{27,19},{28,20},{29,21},{30,22},{31,23}} | collective-permute-start | bytes 196616 | tf_op jit(solution)/shard_map/ppermute | solution.py:66
  80.5 11.5 %collective-permute-start.19 = (bf16[256,128]{1,0:T(8,128)(2,1)S(1)}, bf16[256,128]{1,0:T(8,128)(2,1)S(1)}, u32[]{:S(2)}, u32[]{:S(2)}) collective-permute-start(bf16[256,128]{1,0:T(8,128)(2,1)S(1)} %get-tuple-element.52), channel_id=1, source_target_pairs={{24,17},{25,16},{26,19},{27,18},{28,21},{29,20},{30,23},{31,22}} | collective-permute-start | bytes 196616 | tf_op jit(solution)/shard_map/ppermute | solution.py:66

commit v6 on v5

--- a/solution.py
+++ b/solution.py
@@ -603,7 +603,9 @@
         [pltpu.VMEM((2 * last * proj, local), BF16)],
         room=10,
     )
-    y_all = [shift(v, [(last, i // parts)], same, i % parts) for i, v in enumerate(y_all)]
+    y_all = [
+        shift(y_all[s * parts + k], [(last, s)], same, k) for s in range(last) for k in reversed(range(parts))
+    ]
     (feats,) = launch(
         features,
         [(info, SMEM), (lengths, SMEM), (own, VMEM)] + [(x, VMEM) for x in x_all] + [(y, VMEM) for y in y_all],

time: 94.3 us -> 93.4 us (level)
  waiting for transfers between devices: 38.4 us -> 37.1 us
    ppermute x19, waiting for transfers between devices: 38.4 us -> 37.1 us  [shift(): return lax.ppermute(value, AXES, pairs)]
  transfers between devices with their start and end apart: 20 -> 20, of which waited for: 10 -> 9; matrix products, arithmetic and copies ran while one was open for 0% -> 0% of each run, Pallas kernels for 30% -> 30%
where the time goes in v6:
time: 93.4 us; the launch traced here: 92.5 us
  waiting for transfers between devices  37.1 us (40%)
  Pallas kernels  31 us (33%)
  starting transfers between devices  22.9 us (25%)
    ppermute x19, waiting for transfers between devices, shift(): return lax.ppermute(value, AXES, pairs)  37.1 us
    pallas_call x9, Pallas kernels, launch(): pl.pallas_call(kernel, in_specs=[pl.BlockSpec(memory_space=space) for _,...  31 us
    ppermute x19, starting transfers between devices, shift(): return lax.ppermute(value, AXES, pairs)  22.3 us
  transfers between devices with their start and end apart: 20, of which 9 were waited for; matrix products, arithmetic and copies ran while one was open for 0% of the time, Pallas kernels for 30%

profile of v6, /device:TPU:12, one launch (start us, length us, event | category | flops | bytes accessed | tf_op | source)
XLA Modules:
  0.0 92.5 jit_solution(12140819014280732145)
XLA Ops:
  0.0 0.1 pad_add_fusion.refs_0_
  0.1 0.0 copy-start.2
  0.1 2.3 %shard_map.82 = (bf16[64,4096]{1,0:T(8,128)(2,1)S(1)}, bf16[64,4096]{1,0:T(8,128)(2,1)S(1)}, bf16[448,4096]{1,0:T(8,128)(2,1)S(1)}, bf16[64,4096]{1,0:T(8,128)(2,1)S(1)}) custom-call(s32[3]{0:T(128)S(1)} %pad_add_fusion.refs_0_, s32[64,8192]{1,0:T(8,128)} %bitcast.20, s32[128,128]{1,0:T(8,128)} %refs_2_.3, bf16[128,8192]{1,0:T(8,128)(2,1)} %bitcast.13, ...), custom_call_target="tpu_custom_call" | custom-call | tf_op jit(solution)/shard_map/pallas_call | solution.py:39
  2.4 0.9 collective-permute-start
  3.3 0.7 collective-permute-start.2
  4.0 1.3 %collective-permute-start.1 = (bf16[64,4096]{1,0:T(8,128)(2,1)S(1)}, bf16[64,4096]{1,0:T(8,128)(2,1)S(1)}, u32[]{:S(2)}, u32[]{:S(2)}) collective-permute-start(bf16[64,4096]{1,0:T(8,128)(2,1)S(1)} %get-tuple-element.35), channel_id=1, source_target_pairs={{0,25},{1,24},{2,27},{3,26},{4,29},{5,28},{6,31},{7,30},{8,16},{9,... | collective-permute-start | bytes 1572872 | tf_op jit(solution)/shard_map/ppermute | solution.py:66
  5.3 0.0 copy-done.2
  5.3 0.9 shard_map.83
  6.2 0.0 collective-permute-done.2.refs_4_
  6.2 6.7 %shard_map.84 = (bf16[64,2048]{1,0:T(8,128)(2,1)S(1)}, bf16[64,2048]{1,0:T(8,128)(2,1)S(1)}, bf16[4,4096,512]{2,1,0:T(8,128)(2,1)S(1)}) custom-call(s32[3]{0:T(128)S(1)} %pad_add_fusion.refs_0_, bf16[4096,8192]{1,0:T(8,128)(2,1)} %bitcast.3.refs_4_.refs_1_.refs_3_, bf16[4096,128]{1,0:T(8,128)(2,1)} %bitcast.9, bf16[128,8192]{1,0:T(8,128)(2,1)} %bitcast.15, ...), custom_call_target="tpu_custom_call" | custom-call | tf_op jit(solution)/shard_map/pallas_call | solution.py:39
  12.9 1.3 %collective-permute-start.6 = (bf16[64,2048]{1,0:T(8,128)(2,1)S(1)}, bf16[64,2048]{1,0:T(8,128)(2,1)S(1)}, u32[]{:S(2)}, u32[]{:S(2)}) collective-permute-start(bf16[64,2048]{1,0:T(8,128)(2,1)S(1)} %get-tuple-element.39), channel_id=1, source_target_pairs={{8,19},{9,18},{10,17},{11,16},{12,23},{13,22},{14,21},{15,20}} | collective-permute-start | bytes 786440 | tf_op jit(solution)/shard_map/ppermute | solution.py:66
  14.2 1.3 %collective-permute-start.4 = (bf16[64,2048]{1,0:T(8,128)(2,1)S(1)}, bf16[64,2048]{1,0:T(8,128)(2,1)S(1)}, u32[]{:S(2)}, u32[]{:S(2)}) collective-permute-start(bf16[64,2048]{1,0:T(8,128)(2,1)S(1)} %get-tuple-element.39), channel_id=1, source_target_pairs={{8,17},{9,16},{10,19},{11,18},{12,21},{13,20},{14,23},{15,22}} | collective-permute-start | bytes 786440 | tf_op jit(solution)/shard_map/ppermute | solution.py:66
  15.5 1.3 %collective-permute-start.5 = (bf16[64,2048]{1,0:T(8,128)(2,1)S(1)}, bf16[64,2048]{1,0:T(8,128)(2,1)S(1)}, u32[]{:S(2)}, u32[]{:S(2)}) collective-permute-start(bf16[64,2048]{1,0:T(8,128)(2,1)S(1)} %get-tuple-element.38.refs_5_), channel_id=1, source_target_pairs={{8,18},{9,19},{10,16},{11,17},{12,22},{13,23},{14,20},{15,21}} | collective-permute-start | bytes 786440 | tf_op jit(solution)/shard_map/ppermute | solution.py:66
  16.8 3.3 %collective-permute-done.1.refs_8_.refs_10_ = bf16[64,4096]{1,0:T(8,128)(2,1)S(1)} collective-permute-done((bf16[64,4096]{1,0:T(8,128)(2,1)S(1)}, bf16[64,4096]{1,0:T(8,128)(2,1)S(1)}, u32[]{:S(2)}, u32[]{:S(2)}) %collective-permute-start.1) | collective-permute-done | bytes 524320 | tf_op jit(solution)/shard_map/ppermute | solution.py:66
  20.1 1.3 %collective-permute-start.3 = (bf16[64,2048]{1,0:T(8,128)(2,1)S(1)}, bf16[64,2048]{1,0:T(8,128)(2,1)S(1)}, u32[]{:S(2)}, u32[]{:S(2)}) collective-permute-start(bf16[64,2048]{1,0:T(8,128)(2,1)S(1)} %get-tuple-element.38.refs_5_), channel_id=1, source_target_pairs={{8,16},{9,17},{10,18},{11,19},{12,20},{13,21},{14,22},{15,23}} | collective-permute-start | bytes 786440 | tf_op jit(solution)/shard_map/ppermute | solution.py:66
  21.4 4.7 %shard_map.85 = (f32[64,512]{1,0:T(8,128)S(1)}, f32[64,512]{1,0:T(8,128)S(1)}) custom-call(s32[3]{0:T(128)S(1)} %pad_add_fusion.refs_0_, bf16[512,4096]{1,0:T(8,128)(2,1)} %bitcast.22, bf16[64,4096]{1,0:T(8,128)(2,1)S(1)} %get-tuple-element.29.refs_6_.refs_5_.refs_2_.refs_9_.refs_3_, bf16[4096,128]{1,0:T(8,128)(2,1)} %bitcast.10, s32[128,128]{1,0:T(8,128)} %refs_2_.3, ...), custom_call_target="tpu_custom_call" | custom-call | tf_op jit(solution)/shard_map/pallas_call | solution.py:39
  26.1 3.1 %collective-permute-done.6.refs_7_ = bf16[64,2048]{1,0:T(8,128)(2,1)S(1)} collective-permute-done((bf16[64,2048]{1,0:T(8,128)(2,1)S(1)}, bf16[64,2048]{1,0:T(8,128)(2,1)S(1)}, u32[]{:S(2)}, u32[]{:S(2)}) %collective-permute-start.6) | collective-permute-done | bytes 262176 | tf_op jit(solution)/shard_map/ppermute | solution.py:66
  29.2 4.6 %collective-permute-done.4.refs_5_ = bf16[64,2048]{1,0:T(8,128)(2,1)S(1)} collective-permute-done((bf16[64,2048]{1,0:T(8,128)(2,1)S(1)}, bf16[64,2048]{1,0:T(8,128)(2,1)S(1)}, u32[]{:S(2)}, u32[]{:S(2)}) %collective-permute-start.4) | collective-permute-done | bytes 262176 | tf_op jit(solution)/shard_map/ppermute | solution.py:66
  33.7 0.0 collective-permute-done.5.refs_6_
  33.7 2.7 %collective-permute-done.3.refs_4_ = bf16[64,2048]{1,0:T(8,128)(2,1)S(1)} collective-permute-done((bf16[64,2048]{1,0:T(8,128)(2,1)S(1)}, bf16[64,2048]{1,0:T(8,128)(2,1)S(1)}, u32[]{:S(2)}, u32[]{:S(2)}) %collective-permute-start.3) | collective-permute-done | bytes 262176 | tf_op jit(solution)/shard_map/ppermute | solution.py:66
  36.4 6.2 %shard_map.86 = (bf16[192,2048]{1,0:T(8,128)(2,1)S(1)}, bf16[192,4096]{1,0:T(8,128)(2,1)S(1)}, bf16[192,128]{1,0:T(8,128)(2,1)S(1)}) custom-call(s32[3]{0:T(128)S(1)} %pad_add_fusion.refs_0_, bf16[4,4096,512]{2,1,0:T(8,128)(2,1)S(1)} %get-tuple-element.37.refs_1_, bf16[4096,128]{1,0:T(8,128)(2,1)} %bitcast.11, bf16[128,8192]{1,0:T(8,128)(2,1)} %bitcast.16, ...), custom_call_target="tpu_custom_call" | custom-call | tf_op jit(solution)/shard_map/pallas_call | solution.py:39
  42.6 2.4 %collective-permute-start.7 = (bf16[192,2048]{1,0:T(8,128)(2,1)S(1)}, bf16[192,2048]{1,0:T(8,128)(2,1)S(1)}, u32[]{:S(2)}, u32[]{:S(2)}) collective-permute-start(bf16[192,2048]{1,0:T(8,128)(2,1)S(1)} %get-tuple-element.43.refs_5_), channel_id=1, source_target_pairs={{16,17},{17,16},{18,19},{19,18},{20,21},{21,20},{22,23},{23,22}} | collective-permute-start | bytes 2359304 | tf_op jit(solution)/shard_map/ppermute | solution.py:66
  45.1 1.3 %collective-permute-start.8 = (bf16[64,4096]{1,0:T(8,128)(2,1)S(1)}, bf16[64,4096]{1,0:T(8,128)(2,1)S(1)}, u32[]{:S(2)}, u32[]{:S(2)}) collective-permute-start(bf16[64,4096]{1,0:T(8,128)(2,1)S(1)} %get-tuple-element.36), channel_id=1, source_target_pairs={{16,24},{17,25},{18,26},{19,27},{20,28},{21,29},{22,30},{23,31}} | collective-permute-start | bytes 1572872 | tf_op jit(solution)/shard_map/ppermute | solution.py:66
  46.4 0.0 copy-start
  46.4 0.0 copy-start.1
  46.4 7.9 %shard_map.87 = bf16[192,2048]{1,0:T(8,128)(2,1)S(1)} custom-call(s32[3]{0:T(128)S(1)} %pad_add_fusion.refs_0_, bf16[4096,8192]{1,0:T(8,128)(2,1)} %bitcast.3.refs_4_.refs_1_.refs_3_, bf16[128,8192]{1,0:T(8,128)(2,1)} %bitcast.17, bf16[192,4096]{1,0:T(8,128)(2,1)S(1)} %get-tuple-element.41.refs_3_, bf16[192,128]{1,0:T(8,128)(2,1)S(1)} %get-tuple-element.42.refs_4_, ...), custom_call_target="tpu_custom_call" | custom-call | tf_op jit(solution)/shard_map/pallas_call | solution.py:39
  54.3 3.6 %collective-permute-done.7 = bf16[192,2048]{1,0:T(8,128)(2,1)S(1)} collective-permute-done((bf16[192,2048]{1,0:T(8,128)(2,1)S(1)}, bf16[192,2048]{1,0:T(8,128)(2,1)S(1)}, u32[]{:S(2)}, u32[]{:S(2)}) %collective-permute-start.7) | collective-permute-done | bytes 786464 | tf_op jit(solution)/shard_map/ppermute | solution.py:66
  57.9 0.3 add_convert_fusion.refs_11_
  58.2 1.3 %collective-permute-start.13 = (bf16[192,2048]{1,0:T(8,128)(2,1)S(1)}, bf16[192,2048]{1,0:T(8,128)(2,1)S(1)}, u32[]{:S(2)}, u32[]{:S(2)}) collective-permute-start(bf16[192,2048]{1,0:T(8,128)(2,1)S(1)} %add_convert_fusion.refs_11_), channel_id=1, source_target_pairs={{16,24},{17,25},{18,26},{19,27},{20,28},{21,29},{22,30},{23,31}} | collective-permute-start | bytes 2359304 | tf_op jit(solution)/shard_map/ppermute | solution.py:66
  59.5 1.3 %collective-permute-start.12 = (bf16[192,2048]{1,0:T(8,128)(2,1)S(1)}, bf16[192,2048]{1,0:T(8,128)(2,1)S(1)}, u32[]{:S(2)}, u32[]{:S(2)}) collective-permute-start(bf16[192,2048]{1,0:T(8,128)(2,1)S(1)} %add_convert_fusion.refs_11_), channel_id=1, source_target_pairs={{16,26},{17,27},{18,24},{19,25},{20,30},{21,31},{22,28},{23,29}} | collective-permute-start | bytes 2359304 | tf_op jit(solution)/shard_map/ppermute | solution.py:66
  60.9 1.3 %collective-permute-start.11 = (bf16[64,2048]{1,0:T(8,128)(2,1)S(1)}, bf16[64,2048]{1,0:T(8,128)(2,1)S(1)}, u32[]{:S(2)}, u32[]{:S(2)}) collective-permute-start(bf16[64,2048]{1,0:T(8,128)(2,1)S(1)} %slice.5), channel_id=1, source_target_pairs={{16,30},{17,31},{18,28},{19,29},{20,26},{21,27},{22,24},{23,25}} | collective-permute-start | bytes 786440 | tf_op jit(solution)/shard_map/ppermute | solution.py:66
  62.2 0.0 collective-permute-done.8.refs_12_.refs_2_
  62.2 1.3 %collective-permute-start.10 = (bf16[64,2048]{1,0:T(8,128)(2,1)S(1)}, bf16[64,2048]{1,0:T(8,128)(2,1)S(1)}, u32[]{:S(2)}, u32[]{:S(2)}) collective-permute-start(bf16[64,2048]{1,0:T(8,128)(2,1)S(1)} %slice.5), channel_id=1, source_target_pairs={{16,28},{17,29},{18,30},{19,31},{20,24},{21,25},{22,26},{23,27}} | collective-permute-start | bytes 786440 | tf_op jit(solution)/shard_map/ppermute | solution.py:66
  63.5 0.0 collective-permute-done.refs_9_
  63.5 0.6 collective-permute-start.9
  64.1 0.0 copy-done
  64.1 0.0 copy-done.1
  64.2 0.8 shard_map.88
  65.0 1.1 %collective-permute-done.11.refs_5_ = bf16[64,2048]{1,0:T(8,128)(2,1)S(1)} collective-permute-done((bf16[64,2048]{1,0:T(8,128)(2,1)S(1)}, bf16[64,2048]{1,0:T(8,128)(2,1)S(1)}, u32[]{:S(2)}, u32[]{:S(2)}) %collective-permute-start.11) | collective-permute-done | bytes 262176 | tf_op jit(solution)/shard_map/ppermute | solution.py:66
  66.1 2.9 %collective-permute-done.10.refs_4_ = bf16[64,2048]{1,0:T(8,128)(2,1)S(1)} collective-permute-done((bf16[64,2048]{1,0:T(8,128)(2,1)S(1)}, bf16[64,2048]{1,0:T(8,128)(2,1)S(1)}, u32[]{:S(2)}, u32[]{:S(2)}) %collective-permute-start.10) | collective-permute-done | bytes 262176 | tf_op jit(solution)/shard_map/ppermute | solution.py:66
  68.9 0.0 collective-permute-done.13.refs_7_
  68.9 7.0 %collective-permute-done.12.refs_6_ = bf16[192,2048]{1,0:T(8,128)(2,1)S(1)} collective-permute-done((bf16[192,2048]{1,0:T(8,128)(2,1)S(1)}, bf16[192,2048]{1,0:T(8,128)(2,1)S(1)}, u32[]{:S(2)}, u32[]{:S(2)}) %collective-permute-start.12) | collective-permute-done | bytes 786464 | tf_op jit(solution)/shard_map/ppermute | solution.py:66
  75.9 0.5 shard_map.89
  76.5 0.7 collective-permute-start.14
  77.2 0.7 collective-permute-start.15
  77.8 0.7 collective-permute-start.16
  78.5 0.7 collective-permute-start.17
  79.2 0.0 collective-permute-done.9.refs_4_
  79.2 1.3 %collective-permute-start.18 = (bf16[256,128]{1,0:T(8,128)(2,1)S(1)}, bf16[256,128]{1,0:T(8,128)(2,1)S(1)}, u32[]{:S(2)}, u32[]{:S(2)}) collective-permute-start(bf16[256,128]{1,0:T(8,128)(2,1)S(1)} %get-tuple-element.51), channel_id=1, source_target_pairs={{24,17},{25,16},{26,19},{27,18},{28,21},{29,20},{30,23},{31,22}} | collective-permute-start | bytes 196616 | tf_op jit(solution)/shard_map/ppermute | solution.py:66
  80.5 0.0 collective-permute-done.14.refs_5_
  80.5 1.3 %collective-permute-start.19 = (bf16[256,128]{1,0:T(8,128)(2,1)S(1)}, bf16[256,128]{1,0:T(8,128)(2,1)S(1)}, u32[]{:S(2)}, u32[]{:S(2)}) collective-permute-start(bf16[256,128]{1,0:T(8,128)(2,1)S(1)} %get-tuple-element.52), channel_id=1, source_target_pairs={{24,16},{25,17},{26,18},{27,19},{28,20},{29,21},{30,22},{31,23}} | collective-permute-start | bytes 196616 | tf_op jit(solution)/shard_map/ppermute | solution.py:66
  81.8 0.0 collective-permute-done.15.refs_6_
  81.8 0.0 collective-permute-done.16.refs_7_
  81.8 0.0 collective-permute-done.17.refs_8_
  81.8 8.9 %collective-permute-done.18.refs_9_ = bf16[256,128]{1,0:T(8,128)(2,1)S(1)} collective-permute-done((bf16[256,128]{1,0:T(8,128)(2,1)S(1)}, bf16[256,128]{1,0:T(8,128)(2,1)S(1)}, u32[]{:S(2)}, u32[]{:S(2)}) %collective-permute-start.18) | collective-permute-done | bytes 65568 | tf_op jit(solution)/shard_map/ppermute | solution.py:66
  90.7 0.0 collective-permute-done.19.refs_10_
  90.7 1.0 %shard_map.90 = f32[4,64,64]{2,1,0:T(8,128)S(1)} custom-call(s32[3]{0:T(128)S(1)} %pad_add_fusion.refs_0_, s32[4]{0:T(128)S(1)} %copy-done.2, f32[512,128]{1,0:T(8,128)S(1)} %get-tuple-element.44.refs_2_, f32[64,512]{1,0:T(8,128)S(1)} %get-tuple-element.40.refs_10_.refs_3_, f32[64,512]{1,0:T(8,128)S(1)} %collective-permute-done.9.refs_4_, ...), custom_call_target="tpu_custom_call" | custom-call | tf_op jit(solution)/shard_map/pallas_call | solution.py:39
  91.8 0.8 reshape.8
  (1 shorter events, 0.0 us)
Async XLA Ops:
  0.1 5.2 %copy-start.2 = (s32[4]{0:T(128)S(1)}, s32[4]{0:T(128)}, u32[]{:S(2)}) copy-start(s32[4]{0:T(128)} %refs_1_.5) | copy-start | bytes 52
  2.4 61.2 %collective-permute-start = (bf16[448,4096]{1,0:T(8,128)(2,1)S(1)}, bf16[448,4096]{1,0:T(8,128)(2,1)S(1)}, u32[]{:S(2)}, u32[]{:S(2)}) collective-permute-start(bf16[448,4096]{1,0:T(8,128)(2,1)S(1)} %get-tuple-element.34), channel_id=1, source_target_pairs={{24,25},{25,24},{26,27},{27,26},{28,29},{29,28},{30,31},{31,30}} | collective-permute-start | bytes 11010056 | tf_op jit(solution)/shard_map/ppermute | solution.py:66
  3.3 2.9 %collective-permute-start.2 = (bf16[64,4096]{1,0:T(8,128)(2,1)S(1)}, bf16[64,4096]{1,0:T(8,128)(2,1)S(1)}, u32[]{:S(2)}, u32[]{:S(2)}) collective-permute-start(bf16[64,4096]{1,0:T(8,128)(2,1)S(1)} %get-tuple-element.36), channel_id=1, source_target_pairs={{0,8},{1,9},{2,10},{3,11},{4,12},{5,13},{6,14},{7,15}} | collective-permute-start | bytes 1572872 | tf_op jit(solution)/shard_map/ppermute | solution.py:66
  4.0 16.1 %collective-permute-start.1 = (bf16[64,4096]{1,0:T(8,128)(2,1)S(1)}, bf16[64,4096]{1,0:T(8,128)(2,1)S(1)}, u32[]{:S(2)}, u32[]{:S(2)}) collective-permute-start(bf16[64,4096]{1,0:T(8,128)(2,1)S(1)} %get-tuple-element.35), channel_id=1, source_target_pairs={{0,25},{1,24},{2,27},{3,26},{4,29},{5,28},{6,31},{7,30},{8,16},{9,... | collective-permute-start | bytes 1572872 | tf_op jit(solution)/shard_map/ppermute | solution.py:66
  12.9 16.2 %collective-permute-start.6 = (bf16[64,2048]{1,0:T(8,128)(2,1)S(1)}, bf16[64,2048]{1,0:T(8,128)(2,1)S(1)}, u32[]{:S(2)}, u32[]{:S(2)}) collective-permute-start(bf16[64,2048]{1,0:T(8,128)(2,1)S(1)} %get-tuple-element.39), channel_id=1, source_target_pairs={{8,19},{9,18},{10,17},{11,16},{12,23},{13,22},{14,21},{15,20}} | collective-permute-start | bytes 786440 | tf_op jit(solution)/shard_map/ppermute | solution.py:66
  14.2 19.5 %collective-permute-start.4 = (bf16[64,2048]{1,0:T(8,128)(2,1)S(1)}, bf16[64,2048]{1,0:T(8,128)(2,1)S(1)}, u32[]{:S(2)}, u32[]{:S(2)}) collective-permute-start(bf16[64,2048]{1,0:T(8,128)(2,1)S(1)} %get-tuple-element.39), channel_id=1, source_target_pairs={{8,17},{9,16},{10,19},{11,18},{12,21},{13,20},{14,23},{15,22}} | collective-permute-start | bytes 786440 | tf_op jit(solution)/shard_map/ppermute | solution.py:66
  15.5 18.2 %collective-permute-start.5 = (bf16[64,2048]{1,0:T(8,128)(2,1)S(1)}, bf16[64,2048]{1,0:T(8,128)(2,1)S(1)}, u32[]{:S(2)}, u32[]{:S(2)}) collective-permute-start(bf16[64,2048]{1,0:T(8,128)(2,1)S(1)} %get-tuple-element.38.refs_5_), channel_id=1, source_target_pairs={{8,18},{9,19},{10,16},{11,17},{12,22},{13,23},{14,20},{15,21}} | collective-permute-start | bytes 786440 | tf_op jit(solution)/shard_map/ppermute | solution.py:66
  20.1 16.3 %collective-permute-start.3 = (bf16[64,2048]{1,0:T(8,128)(2,1)S(1)}, bf16[64,2048]{1,0:T(8,128)(2,1)S(1)}, u32[]{:S(2)}, u32[]{:S(2)}) collective-permute-start(bf16[64,2048]{1,0:T(8,128)(2,1)S(1)} %get-tuple-element.38.refs_5_), channel_id=1, source_target_pairs={{8,16},{9,17},{10,18},{11,19},{12,20},{13,21},{14,22},{15,23}} | collective-permute-start | bytes 786440 | tf_op jit(solution)/shard_map/ppermute | solution.py:66
  42.6 15.3 %collective-permute-start.7 = (bf16[192,2048]{1,0:T(8,128)(2,1)S(1)}, bf16[192,2048]{1,0:T(8,128)(2,1)S(1)}, u32[]{:S(2)}, u32[]{:S(2)}) collective-permute-start(bf16[192,2048]{1,0:T(8,128)(2,1)S(1)} %get-tuple-element.43.refs_5_), channel_id=1, source_target_pairs={{16,17},{17,16},{18,19},{19,18},{20,21},{21,20},{22,23},{23,22}} | collective-permute-start | bytes 2359304 | tf_op jit(solution)/shard_map/ppermute | solution.py:66
  45.1 17.1 %collective-permute-start.8 = (bf16[64,4096]{1,0:T(8,128)(2,1)S(1)}, bf16[64,4096]{1,0:T(8,128)(2,1)S(1)}, u32[]{:S(2)}, u32[]{:S(2)}) collective-permute-start(bf16[64,4096]{1,0:T(8,128)(2,1)S(1)} %get-tuple-element.36), channel_id=1, source_target_pairs={{16,24},{17,25},{18,26},{19,27},{20,28},{21,29},{22,30},{23,31}} | collective-permute-start | bytes 1572872 | tf_op jit(solution)/shard_map/ppermute | solution.py:66
  46.4 17.8 %copy-start = (bf16[1,4096,128]{2,1,0:T(8,128)(2,1)S(1)}, bf16[1,4096,128]{2,1,0:T(8,128)(2,1)}, u32[]{:S(2)}) copy-start(bf16[1,4096,128]{2,1,0:T(8,128)(2,1)} %param.11) | copy-start | bytes 3145732
  46.4 17.7 %copy-start.1 = (s32[128,128]{1,0:T(8,128)S(1)}, s32[128,128]{1,0:T(8,128)}, u32[]{:S(2)}) copy-start(s32[128,128]{1,0:T(8,128)} %refs_2_.3) | copy-start | bytes 196612
  58.2 10.7 %collective-permute-start.13 = (bf16[192,2048]{1,0:T(8,128)(2,1)S(1)}, bf16[192,2048]{1,0:T(8,128)(2,1)S(1)}, u32[]{:S(2)}, u32[]{:S(2)}) collective-permute-start(bf16[192,2048]{1,0:T(8,128)(2,1)S(1)} %add_convert_fusion.refs_11_), channel_id=1, source_target_pairs={{16,24},{17,25},{18,26},{19,27},{20,28},{21,29},{22,30},{23,31}} | collective-permute-start | bytes 2359304 | tf_op jit(solution)/shard_map/ppermute | solution.py:66
  59.5 16.4 %collective-permute-start.12 = (bf16[192,2048]{1,0:T(8,128)(2,1)S(1)}, bf16[192,2048]{1,0:T(8,128)(2,1)S(1)}, u32[]{:S(2)}, u32[]{:S(2)}) collective-permute-start(bf16[192,2048]{1,0:T(8,128)(2,1)S(1)} %add_convert_fusion.refs_11_), channel_id=1, source_target_pairs={{16,26},{17,27},{18,24},{19,25},{20,30},{21,31},{22,28},{23,29}} | collective-permute-start | bytes 2359304 | tf_op jit(solution)/shard_map/ppermute | solution.py:66
  60.9 5.2 %collective-permute-start.11 = (bf16[64,2048]{1,0:T(8,128)(2,1)S(1)}, bf16[64,2048]{1,0:T(8,128)(2,1)S(1)}, u32[]{:S(2)}, u32[]{:S(2)}) collective-permute-start(bf16[64,2048]{1,0:T(8,128)(2,1)S(1)} %slice.5), channel_id=1, source_target_pairs={{16,30},{17,31},{18,28},{19,29},{20,26},{21,27},{22,24},{23,25}} | collective-permute-start | bytes 786440 | tf_op jit(solution)/shard_map/ppermute | solution.py:66
  62.2 6.7 %collective-permute-start.10 = (bf16[64,2048]{1,0:T(8,128)(2,1)S(1)}, bf16[64,2048]{1,0:T(8,128)(2,1)S(1)}, u32[]{:S(2)}, u32[]{:S(2)}) collective-permute-start(bf16[64,2048]{1,0:T(8,128)(2,1)S(1)} %slice.5), channel_id=1, source_target_pairs={{16,28},{17,29},{18,30},{19,31},{20,24},{21,25},{22,26},{23,27}} | collective-permute-start | bytes 786440 | tf_op jit(solution)/shard_map/ppermute | solution.py:66
  63.5 15.6 %collective-permute-start.9 = (f32[64,512]{1,0:T(8,128)S(1)}, f32[64,512]{1,0:T(8,128)S(1)}, u32[]{:S(2)}, u32[]{:S(2)}) collective-permute-start(f32[64,512]{1,0:T(8,128)S(1)} %get-tuple-element.45), channel_id=1, source_target_pairs={{0,1},{1,0},{2,3},{3,2},{4,5},{5,4},{6,7},{7,6},{8,9},{9,8},{10,11... | collective-permute-start | bytes 393224 | tf_op jit(solution)/shard_map/ppermute | solution.py:525
  76.5 4.0 %collective-permute-start.14 = (bf16[256,128]{1,0:T(8,128)(2,1)S(1)}, bf16[256,128]{1,0:T(8,128)(2,1)S(1)}, u32[]{:S(2)}, u32[]{:S(2)}) collective-permute-start(bf16[256,128]{1,0:T(8,128)(2,1)S(1)} %get-tuple-element.47), channel_id=1, source_target_pairs={{24,1},{25,0},{26,3},{27,2},{28,5},{29,4},{30,7},{31,6}} | collective-permute-start | bytes 196616 | tf_op jit(solution)/shard_map/ppermute | solution.py:66
  77.2 4.6 %collective-permute-start.15 = (bf16[256,128]{1,0:T(8,128)(2,1)S(1)}, bf16[256,128]{1,0:T(8,128)(2,1)S(1)}, u32[]{:S(2)}, u32[]{:S(2)}) collective-permute-start(bf16[256,128]{1,0:T(8,128)(2,1)S(1)} %get-tuple-element.48), channel_id=1, source_target_pairs={{24,0},{25,1},{26,2},{27,3},{28,4},{29,5},{30,6},{31,7}} | collective-permute-start | bytes 196616 | tf_op jit(solution)/shard_map/ppermute | solution.py:66
  77.8 4.0 %collective-permute-start.16 = (bf16[256,128]{1,0:T(8,128)(2,1)S(1)}, bf16[256,128]{1,0:T(8,128)(2,1)S(1)}, u32[]{:S(2)}, u32[]{:S(2)}) collective-permute-start(bf16[256,128]{1,0:T(8,128)(2,1)S(1)} %get-tuple-element.49), channel_id=1, source_target_pairs={{24,9},{25,8},{26,11},{27,10},{28,13},{29,12},{30,15},{31,14}} | collective-permute-start | bytes 196616 | tf_op jit(solution)/shard_map/ppermute | solution.py:66
  78.5 3.3 %collective-permute-start.17 = (bf16[256,128]{1,0:T(8,128)(2,1)S(1)}, bf16[256,128]{1,0:T(8,128)(2,1)S(1)}, u32[]{:S(2)}, u32[]{:S(2)}) collective-permute-start(bf16[256,128]{1,0:T(8,128)(2,1)S(1)} %get-tuple-element.50), channel_id=1, source_target_pairs={{24,8},{25,9},{26,10},{27,11},{28,12},{29,13},{30,14},{31,15}} | collective-permute-start | bytes 196616 | tf_op jit(solution)/shard_map/ppermute | solution.py:66
  79.2 11.5 %collective-permute-start.18 = (bf16[256,128]{1,0:T(8,128)(2,1)S(1)}, bf16[256,128]{1,0:T(8,128)(2,1)S(1)}, u32[]{:S(2)}, u32[]{:S(2)}) collective-permute-start(bf16[256,128]{1,0:T(8,128)(2,1)S(1)} %get-tuple-element.51), channel_id=1, source_target_pairs={{24,17},{25,16},{26,19},{27,18},{28,21},{29,20},{30,23},{31,22}} | collective-permute-start | bytes 196616 | tf_op jit(solution)/shard_map/ppermute | solution.py:66
  80.5 10.2 %collective-permute-start.19 = (bf16[256,128]{1,0:T(8,128)(2,1)S(1)}, bf16[256,128]{1,0:T(8,128)(2,1)S(1)}, u32[]{:S(2)}, u32[]{:S(2)}) collective-permute-start(bf16[256,128]{1,0:T(8,128)(2,1)S(1)} %get-tuple-element.52), channel_id=1, source_target_pairs={{24,16},{25,17},{26,18},{27,19},{28,20},{29,21},{30,22},{31,23}} | collective-permute-start | bytes 196616 | tf_op jit(solution)/shard_map/ppermute | solution.py:66
